TPU v7x, 512 devices: a whole 4x4x16 slice. The times are simulated.
512 devices in a mesh: gx: 32 (over x, y, core), gy: 16 (over z).
Axes of the slice: x: 4, y: 4, z: 16, core: 2. Of those that a mesh axis runs over, the one named last changes fastest.
Arguments:
- queries: bfloat16 [16384, 256], P(('gx', 'gy')), may hold values from -32 to 32
- positions: int32 [16384], P(('gx', 'gy')), may hold values from 0 to 65535
- queue: bfloat16 [65536, 256], P('gx'), may hold values from -4 to 4
- new_keys: bfloat16 [2048, 256], P(('gx', 'gy')), may hold values from -4 to 4
- step: int32 [1], replicated, may hold values from 0 to 1023
Outputs:
- losses: float32 [16384], P(('gx', 'gy'))
- query_grad: bfloat16 [16384, 256], P(('gx', 'gy'))
- updated_queue: bfloat16 [65536, 256], P('gx')
All inputs are finite; a program needn't handle non-finite values.
Results may differ from a plain program's by a relative error of at most 0.0029.
Values may be sent and summed in bfloat16 or wider, within the bound.
No kernel may reach another device: no remote copies, remote signals or barrier semaphores. Data moves between devices by JAX's collectives and lax.ppermute only.
A program may use at most 64 MiB of HBM per device.

v0:
```python
import math

import jax
import jax.numpy as jnp
from jax import lax
from jax.sharding import PartitionSpec as P


def local(queries, positions, queue, new_keys, step):
    q_dev = queries.shape[0]
    key_dev = queue.shape[0]
    width = queue.shape[1]
    scale = 2.0 / math.sqrt(width)
    slab_count = lax.axis_size("gx")
    slab_index = lax.axis_index("gx")
    all_rows, all_targets = (
        lax.all_gather(queries, "gx", axis=0, tiled=True),
        lax.all_gather(positions, "gx", axis=0, tiled=True),
    )
    arrived = lax.all_gather(new_keys, ("gx", "gy"), axis=0, tiled=True)
    scores = jnp.einsum("re,ke->rk", all_rows, queue, preferred_element_type=jnp.float32) * scale
    local_target = all_targets - slab_index * key_dev
    hits = lax.broadcasted_iota(jnp.int32, scores.shape, 1) == local_target[:, None]
    positive = jnp.sum(jnp.where(hits, scores, 0.0), axis=1)
    top = jnp.max(scores, axis=1)
    total = jnp.sum(jnp.exp(scores - top[:, None]), axis=1)
    top_all = lax.pmax(top, "gx")
    total_all, positive_all = lax.psum((total * jnp.exp(top - top_all), positive), "gx")
    lse = top_all + jnp.log(total_all)
    loss_rows = lse - positive_all
    losses = lax.dynamic_slice_in_dim(loss_rows, slab_index * q_dev, q_dev, 0)
    weights = (jnp.exp(scores - lse[:, None]) - hits.astype(jnp.float32)).astype(jnp.bfloat16)
    partial_grad = jnp.dot(weights, queue, preferred_element_type=jnp.float32)
    full_grad = lax.psum(partial_grad, "gx")
    summed = lax.dynamic_slice_in_dim(full_grad, slab_index * q_dev, q_dev, 0)
    query_grad = (summed * scale).astype(jnp.bfloat16)
    owner = step[0] % slab_count
    updated_queue = jnp.where(owner == slab_index, arrived, queue)
    return (losses, query_grad, updated_queue)


def solution(mesh):
    return jax.shard_map(
        local,
        mesh=mesh,
        in_specs=(
            P(("gx", "gy"), None),
            P(("gx", "gy")),
            P("gx", None),
            P(("gx", "gy"), None),
            P(),
        ),
        out_specs=(P(("gx", "gy")), P(("gx", "gy"), None), P("gx", None)),
        check_vma=False,
    )
```

profile of v0, /device:TPU:1, one launch (start us, length us, event | category | flops | bytes accessed | tf_op | source)
XLA Modules:
  0.0 379.8 jit_solution(3017900710933908963)
XLA Ops:
  8.0 0.0 all-reduce.4.cloned.1.call-start
  8.0 29.2 %all_gather.9 = bf16[1024,256]{1,0:T(8,128)(2,1)S(1)} all-gather(bf16[32,256]{1,0:T(8,128)(2,1)} %param.5), channel_id=1, replica_groups=mesh['gx'=32,'gy'=16] {'gx'}, dimensions={0}, use_global_device_ids=true | all-gather | bytes 540672 | tf_op jit(solution)/shard_map/all_gather | solution.py:17
  37.2 1.3 dynamic-slice
  39.2 0.9 dynamic-update-slice
  40.0 11.0 %all-reduce = s32[1024]{0:T(1024)S(1)} all-reduce(s32[1024]{0:T(1024)S(1)} %dynamic-update-slice), channel_id=1, replica_groups=mesh['gx'=32,'gy'=16] {'gx'}, use_global_device_ids=true, to_apply=%add | all-reduce | flops 1024 | bytes 8192
  51.0 0.0 copy-start
  51.0 5.8 %multiply_reduce_fusion = (f32[1024]{0:T(1024)S(1)}, f32[1024,2048]{1,0:T(8,128)}) fusion(bf16[1024,256]{1,0:T(8,128)(2,1)S(1)} %all_gather.9, bf16[2048,256]{1,0:T(8,128)(2,1)} %param.7), kind=kOutput, calls=%fused_computation.4 | convolution fusion | flops 1077935104 | bytes 9965568 | tf_op jit(solution)/shard_map/re,ke->rk/dot_general | solution.py:21
  56.8 65.7 %pmax.7 = f32[1024]{0:T(1024)S(1)} all-reduce(f32[1024]{0:T(1024)S(1)} %get-tuple-element.9), channel_id=1, replica_groups=mesh['gx'=32,'gy'=16] {'gx'}, use_global_device_ids=true, to_apply=%region_1.2 | all-reduce | flops 1024 | bytes 8192 | tf_op jit(solution)/shard_map/pmax | solution.py:27
  122.5 5.2 %select_reduce_fusion = (f32[1024]{0:T(1024)S(1)}, f32[1024]{0:T(1024)S(1)}) fusion(f32[1024,2048]{1,0:T(8,128)} %get-tuple-element.10, s32[1024]{0:T(1024)S(1)} %broadcast_subtract_fusion, f32[1024]{0:T(1024)S(1)} %get-tuple-element.9), kind=kLoop, calls=%fused_computation.1 | loop fusion | flops 12580864 | bytes 8404992 | tf_op jit(solution)/shard_map/reduce_sum | solution.py:24
  127.7 63.7 %all-reduce.1 = (f32[1024]{0:T(1024)S(1)}, f32[1024]{0:T(1024)S(1)}) all-reduce(f32[1024]{0:T(1024)S(1)} %exponential_multiply_fusion, f32[1024]{0:T(1024)S(1)} %get-tuple-element.3), channel_id=1, replica_groups=mesh['gx'=32,'gy'=16] {'gx'}, use_global_device_ids=true, to_apply=%region_3.4 | all-reduce | flops 2048 | bytes 16384 | tf_op jit(solution)/shard_map/psum | solution.py:28
  191.4 0.0 copy-done
  191.4 6.8 %fusion = f32[1024,256]{1,0:T(8,128)} fusion(bf16[2048,256]{1,0:T(8,128)(2,1)S(1)} %copy-done, f32[1024,2048]{1,0:T(8,128)} %get-tuple-element.10, f32[1024]{0:T(1024)S(1)} %get-tuple-element.8, s32[1024]{0:T(1024)S(1)} %broadcast_subtract_fusion), kind=kOutput, calls=%fused_computation.5 | convolution fusion | flops 1086324736 | bytes 10493952 | tf_op jit(solution)/shard_map/dot_general | solution.py:33
  198.2 0.0 all-reduce.4.cloned.1.call-update
  198.3 0.0 all-gather.3.cloned.1.call-start
  198.3 0.5 all-gather.3.cloned.1.call-update
  199.5 0.6 dynamic_slice.6
  200.1 130.6 %all-reduce.4.cloned.1.call-done = f32[1024,256]{1,0:T(8,128)} async-done(((f32[1024,256]{1,0:T(8,128)}), f32[1024,256]{1,0:T(8,128)}) %all-reduce.4.cloned.1.call-update) | async-done | bytes 1048592 | tf_op jit(solution)/shard_map/psum | solution.py:34
  330.7 1.4 multiply_convert_fusion
  332.1 37.8 %all-gather.3.cloned.1.call-done = bf16[512,4,256]{2,1,0:T(4,128)(2,1)} async-done(((bf16[1,4,256]{2,1,0:T(4,128)(2,1)}), bf16[512,4,256]{2,1,0:T(4,128)(2,1)}) %all-gather.3.cloned.1.call-update) | async-done | bytes 1048592 | tf_op jit(solution)/shard_map/all_gather | solution.py:20
  369.9 1.3 reshape.13
  371.3 1.1 broadcast_select_fusion
  (4 shorter events, 0.0 us)
Async XLA Ops:
  8.0 322.7 %all-reduce.4.cloned.1.call-start = ((), (), s32[]{:S(2)}) async-start(), calls=%async_computation | async-start | bytes 2097152 | tf_op jit(solution)/shard_map/psum | solution.py:34
  51.0 140.4 %copy-start = (bf16[2048,256]{1,0:T(8,128)(2,1)S(1)}, bf16[2048,256]{1,0:T(8,128)(2,1)}, u32[]{:S(2)}) copy-start(bf16[2048,256]{1,0:T(8,128)(2,1)} %param.7) | copy-start | bytes 3145732
  198.3 171.7 %all-gather.3.cloned.1.call-start = ((), (), s32[]{:S(2)}) async-start(), calls=%async_computation.1 | async-start | bytes 1050624 | tf_op jit(solution)/shard_map/all_gather | solution.py:20
Sparse Core Ops, SparseCore 0:
  198.4 132.3 all-reduce.3
Sparse Core Ops, SparseCore 1:
  204.2 165.7 all-gather.2
where the time goes:
time: 380 us
  blocking collectives  169 us (44%)
  waiting for transfers between devices  169 us (44%)
  between operations  16.9 us (4%)
  matrix products  12.7 us (3%)
  other arithmetic  7.65 us (2%)
  local copies, waits for them, and re-layouts  4.06 us (1%)
    psum x1, waiting for transfers between devices, local(): full_grad = lax.psum(partial_grad, 'gx')  131 us
    pmax x1, blocking collectives, local(): top_all = lax.pmax(top, 'gx')  65.7 us
    psum x1, blocking collectives, local(): lax.psum((total * jnp.exp(top - top_all), positive), 'gx')  63.7 us
    all_gather x1, waiting for transfers between devices, local(): arrived = lax.all_gather(new_keys, ('gx', 'gy'), axis=0, tiled=True)  37.8 us
    all_gather x1, blocking collectives, local(): lax.all_gather(queries, 'gx', axis=0, tiled=True)  29.2 us
    unnamed x1, blocking collectives  11 us
  transfers between devices with their start and end apart: 2, of which 2 were waited for; matrix products, arithmetic and copies ran while one was open for 1% of the time, Pallas kernels for 0%

commit v1 on v0

v1 whole, which is shorter than its diff:
```python
import math

import jax
import jax.numpy as jnp
import numpy as np
from jax import lax
from jax.experimental import pallas as pl
from jax.experimental.pallas import tpu as pltpu
from jax.sharding import Mesh, PartitionSpec as P

BF = jnp.bfloat16
F32 = jnp.float32
ROWS = 48
LOG2E = 1.4426950408889634
VMEM = pl.BlockSpec(memory_space=pltpu.VMEM)
SMEM = pl.BlockSpec(memory_space=pltpu.SMEM)


def rows_dot(a, b):
    return lax.dot_general(a, b, (((1,), (1,)), ((), ())), preferred_element_type=F32)


def partial_kernel(scale, srcs, nq, first_ref, msg_ref, own_ref, other_ref, out_ref, q_ref, s_ref):
    width = own_ref.shape[1]
    slab = own_ref.shape[0]
    n = srcs * nq
    block = 512
    lane = lax.broadcasted_iota(jnp.int32, (nq, width), 1)
    row = lax.broadcasted_iota(jnp.int32, (nq, width), 0)
    parts = []
    for j in range(srcs):
        q_ref[j * nq:(j + 1) * nq, :] = msg_ref[j, :nq, :]
        tail = msg_ref[j, nq:, :].astype(F32)
        line = jnp.broadcast_to(tail[4:5, :], (nq, width))
        hi = jnp.sum(jnp.where(lane == row, line, 0.0), axis=1, keepdims=True)
        lo = jnp.sum(jnp.where(lane == row + nq, line, 0.0), axis=1, keepdims=True)
        parts.append(hi * 256.0 + lo)
    target = jnp.concatenate(parts, axis=0).astype(jnp.int32)
    queries = q_ref[...]
    top = None
    blocks = []
    for half, ref in enumerate((own_ref, other_ref)):
        for b in range(slab // block):
            blocks.append((half, ref, b))
    for i, (half, ref, b) in enumerate(blocks):
        s = rows_dot(queries, ref[b * block:(b + 1) * block, :])
        s_ref[:, i * block:(i + 1) * block] = s
        for c in range(block // 128):
            piece = s[:, c * 128:(c + 1) * 128]
            top = piece if top is None else jnp.maximum(top, piece)
    point = jnp.max(top, axis=1, keepdims=True).astype(BF).astype(F32)
    total = jnp.zeros((n, 128), F32)
    grad = jnp.zeros((n, width), F32)
    positive = jnp.zeros((n, width), F32)
    column = lax.broadcasted_iota(jnp.int32, (n, block), 1)
    for i, (half, ref, b) in enumerate(blocks):
        s = s_ref[:, i * block:(i + 1) * block]
        hit = column == (target - (first_ref[half] + b * block))
        e = jnp.where(hit, 0.0, jnp.exp2((s - point) * (scale * LOG2E)))
        for c in range(block // 128):
            total += e[:, c * 128:(c + 1) * 128]
        keys = ref[b * block:(b + 1) * block, :]
        grad += jnp.dot(e.astype(BF), keys, preferred_element_type=F32)
        positive += jnp.dot(hit.astype(F32).astype(BF), keys, preferred_element_type=F32)
    total = jnp.sum(total, axis=1, keepdims=True)
    t0 = total.astype(BF).astype(F32)
    t1 = (total - t0).astype(BF).astype(F32)
    t2 = total - t0 - t1
    place = lax.broadcasted_iota(jnp.int32, (n, 128), 1)
    stats = jnp.where(place == 0, point, jnp.where(place == 1, t0, jnp.where(place == 2, t1, jnp.where(place == 3, t2, 0.0))))
    stats = stats.astype(BF)
    grad = grad.astype(BF)
    positive = positive.astype(BF)
    for j in range(srcs):
        at = slice(j * nq, (j + 1) * nq)
        out_ref[j, :, :width] = grad[at]
        out_ref[j, :, width:2 * width] = positive[at]
        out_ref[j, :, 2 * width:] = stats[at]


def combine_kernel(scale, srcs, nq, got_ref, q_ref, loss_ref, grad_ref):
    width = q_ref.shape[1]
    positive = jnp.zeros((nq, width), F32)
    points, totals = [], []
    for j in range(srcs):
        positive += got_ref[j, :, width:2 * width].astype(F32)
        st = got_ref[j, :, 2 * width:].astype(F32)
        points.append(st[:, 0:1])
        totals.append(st[:, 1:2] + st[:, 2:3] + st[:, 3:4])
    s_pos = jnp.sum(q_ref[...].astype(F32) * positive, axis=1, keepdims=True)
    top = s_pos
    for p in points:
        top = jnp.maximum(top, p)
    total = jnp.exp2((s_pos - top) * (scale * LOG2E))
    grad = jnp.zeros((nq, width), F32)
    for j in range(srcs):
        a = jnp.exp2((points[j] - top) * (scale * LOG2E))
        total += a * totals[j]
        grad += a * got_ref[j, :, :width].astype(F32)
    log_total = jnp.log(total)
    lse = top * scale + log_total
    weight = (jnp.exp(s_pos * scale - lse) - 1.0).astype(BF).astype(F32)
    grad_ref[...] = ((grad / total + weight * positive) * scale).astype(BF)
    loss = lse - s_pos * scale
    lane = lax.broadcasted_iota(jnp.int32, (nq, 128), 1)
    row = lax.broadcasted_iota(jnp.int32, (nq, 128), 0)
    loss_ref[...] = jnp.sum(jnp.where(lane == row, loss, 0.0), axis=0, keepdims=True)


def local(queries, positions, queue, new_keys, step):
    nq, width = queries.shape
    slab = queue.shape[0]
    nk = new_keys.shape[0]
    nz = lax.axis_size("z")
    srcs = lax.axis_size("x") * lax.axis_size("y")
    scale = 2.0 / math.sqrt(width)
    chip = lax.axis_index(("x", "y"))
    core = lax.axis_index("c")
    z = lax.axis_index("z")
    slab_index = chip * 2 + core

    other = lax.ppermute(queue, "c", [(0, 1), (1, 0)])

    hi = (positions // 256).astype(BF)
    lo = (positions % 256).astype(BF)
    line = jnp.concatenate([hi, lo, jnp.zeros((width - 2 * nq,), BF)])[None]
    message = jnp.concatenate([queries, new_keys, line, jnp.zeros((ROWS - nq - nk - 1, width), BF)], axis=0)
    got = lax.all_to_all(jnp.broadcast_to(message[None], (srcs, ROWS, width)), ("x", "y"), 0, 0)

    first = jnp.stack([slab_index * slab, (slab_index ^ 1) * slab]).astype(jnp.int32)
    n = srcs * nq
    flops = 2 * n * 2 * slab * width
    out = pl.pallas_call(
        lambda *refs: partial_kernel(scale, srcs, nq, *refs),
        out_shape=jax.ShapeDtypeStruct((srcs, nq, 2 * width + 128), BF),
        in_specs=[SMEM, VMEM, VMEM, VMEM],
        out_specs=VMEM,
        scratch_shapes=[pltpu.VMEM((n, width), BF), pltpu.VMEM((n, 2 * slab), F32)],
        compiler_params=pltpu.CompilerParams(vmem_limit_bytes=40 * 1024 * 1024),
        cost_estimate=pl.CostEstimate(flops=3 * flops, bytes_accessed=4 * slab * width, transcendentals=2 * n * slab),
    )(first, got, queue, other)
    back = lax.all_to_all(out, ("x", "y"), 0, 0)

    loss, grad = pl.pallas_call(
        lambda *refs: combine_kernel(scale, srcs, nq, *refs),
        out_shape=(jax.ShapeDtypeStruct((1, 128), F32), jax.ShapeDtypeStruct((nq, width), BF)),
        in_specs=[VMEM, VMEM],
        out_specs=(VMEM, VMEM),
    )(back, queries)
    losses = loss[0, :nq]

    ring = got[:, nq:nq + nk, :][None]
    gap = nz // 2
    while gap:
        pairs = [(i, (i + gap) % nz) for i in range(nz)] + [(nz + i, nz + (i - gap) % nz) for i in range(nz)]
        came = lax.ppermute(ring, ("c", "z"), pairs)
        ring = jnp.stack([ring, came], axis=1).reshape((2 * ring.shape[0],) + ring.shape[1:])
        gap //= 2
    twin = lax.ppermute(ring, "c", [(0, 1), (1, 0)])
    low = jnp.where(core == 0, ring, twin)
    high = jnp.where(core == 0, twin, ring)
    low = jnp.roll(low[::-1], z + 1, axis=0)
    high = jnp.roll(high, z, axis=0)
    arrived = jnp.stack([low, high], axis=0).transpose(2, 0, 1, 3, 4).reshape(slab, width)
    owner = step[0] % (srcs * 2)
    updated = jnp.where(owner == slab_index, arrived, queue)
    return losses, grad, updated


def solution(mesh):
    gx, gy = mesh.devices.shape
    side = math.isqrt(gx // 2)
    fine = Mesh(np.asarray(mesh.devices).reshape(side, side, 2, gy), ("x", "y", "c", "z"))
    every = ("x", "y", "c", "z")
    return jax.shard_map(
        local,
        mesh=fine,
        in_specs=(P(every, None), P(every), P(("x", "y", "c"), None), P(every, None), P()),
        out_specs=(P(every), P(every, None), P(("x", "y", "c"), None)),
        check_vma=False,
    )
```

time: 380 us -> 104 us (0.27)
  blocking collectives: 169 us -> 15.4 us
  waiting for transfers between devices: 169 us -> 22.3 us
  starting transfers between devices: 0.08 us -> 48.8 us
  between operations: 16.9 us -> 1.51 us
  matrix products: 12.7 us -> 0 us
  Pallas kernels: 0 us -> 9.51 us
  other arithmetic: 7.65 us -> 3.64 us
    psum x1 -> x0, waiting for transfers between devices: 131 us -> none  [local(): full_grad = lax.psum(partial_grad, 'gx')]
    pmax x1 -> x0, blocking collectives: 65.7 us -> none  [local(): top_all = lax.pmax(top, 'gx')]
    psum x1 -> x0, blocking collectives: 63.7 us -> none  [local(): lax.psum((total * jnp.exp(top - top_all), positive), 'gx')]
    ppermute x0 -> x6, starting transfers between devices: none -> 44.6 us  [the longest x4 30.4 us: local(): came = lax.ppermute(ring, ('c', 'z'), pairs)]
    all_gather x1 -> x0, waiting for transfers between devices: 37.8 us -> none  [local(): arrived = lax.all_gather(new_keys, ('gx', 'gy'), axis=0, tiled=True)]
    all_gather x1 -> x0, blocking collectives: 29.2 us -> none  [local(): lax.all_gather(queries, 'gx', axis=0, tiled=True)]
    all_to_all x0 -> x1, blocking collectives: none -> 15.4 us  [local(): lax.all_to_all(jnp.broadcast_to(message[None], (srcs, ROWS, width)), ('x'...]
    dot_general x2 -> x0, matrix products: 12.7 us -> none  [the longest x1 6.83 us: local(): partial_grad = jnp.dot(weights, queue, preferred_element_type=jnp.float32)]
  transfers between devices with their start and end apart: 2 -> 7, of which waited for: 2 -> 4; matrix products, arithmetic and copies ran while one was open for 1% -> 3% of each run, Pallas kernels for 0% -> 7%
where the time goes in v1:
time: 104 us; the launch traced here: 103 us
  starting transfers between devices  48.8 us (47%)
  waiting for transfers between devices  22.3 us (21%)
  blocking collectives  15.4 us (15%)
  Pallas kernels  9.51 us (9%)
  other arithmetic  3.64 us (4%)
  local copies, waits for them, and re-layouts  2.2 us (2%)
  between operations  1.51 us (1%)
    ppermute x4, starting transfers between devices, local(): came = lax.ppermute(ring, ('c', 'z'), pairs)  30.4 us
    all_to_all x1, blocking collectives, local(): lax.all_to_all(jnp.broadcast_to(message[None], (srcs, ROWS, width)), ('x'...  15.4 us
    ppermute x4, waiting for transfers between devices, local(): came = lax.ppermute(ring, ('c', 'z'), pairs)  12 us
    all_to_all x1, waiting for transfers between devices, local(): back = lax.all_to_all(out, ('x', 'y'), 0, 0)  10.3 us
    ppermute x1, starting transfers between devices, local(): twin = lax.ppermute(ring, 'c', [(0, 1), (1, 0)])  9.44 us
    pallas_call x1, Pallas kernels, local(): pl.pallas_call(lambda *refs: partial_kernel(scale, srcs, nq, *refs), out_...  7.39 us
    ppermute x1, starting transfers between devices, local(): other = lax.ppermute(queue, 'c', [(0, 1), (1, 0)])  4.7 us
    all_to_all x1, starting transfers between devices, local(): back = lax.all_to_all(out, ('x', 'y'), 0, 0)  4.27 us
  transfers between devices with their start and end apart: 7, of which 4 were waited for; matrix products, arithmetic and copies ran while one was open for 3% of the time, Pallas kernels for 7%

profile of v1, /device:TPU:1, one launch (start us, length us, event | category | flops | bytes accessed | tf_op | source)
XLA Modules:
  0.0 103.3 jit_solution(13517422403436073134)
XLA Ops:
  0.6 0.8 fusion.7
  1.6 0.8 maximum_maximum_fusion
  2.4 15.4 %all_to_all.10.refs_1_ = bf16[16,48,256]{2,1,0:T(8,128)(2,1)S(1)} all-to-all(bf16[16,48,256]{2,1,0:T(8,128)(2,1)S(1)} %broadcast_in_dim.21), channel_id=1, replica_groups=mesh['x'=4,'y'=4,'c'=2,'z'=16] {'x','y'}, dimensions={0} | all-to-all | bytes 786432 | tf_op jit(solution)/shard_map/all_to_all | solution.py:128
  17.8 15.7 %collective-permute-start.1 = (bf16[1,16,4,256]{3,2,1,0:T(4,128)(2,1)S(1)}, bf16[1,16,4,256]{3,2,1,0:T(4,128)(2,1)S(1)}, u32[]{:S(2)}, u32[]{:S(2)}) collective-permute-start(bf16[1,16,4,256]{3,2,1,0:T(4,128)(2,1)S(1)} %get-tuple-element.11), channel_id=1, source_target_pairs={{0,8},{1,9},{2,10},{3,11},{4,12},{5,13},{6,14},{7,15},{8,0},{9,1},... | collective-permute-start | bytes 98312 | tf_op jit(solution)/shard_map/ppermute | solution.py:156
  33.5 4.7 %collective-permute-start = (bf16[2048,256]{1,0:T(8,128)(2,1)S(1)}, bf16[2048,256]{1,0:T(8,128)(2,1)S(1)}, u32[]{:S(2)}, u32[]{:S(2)}) collective-permute-start(bf16[2048,256]{1,0:T(8,128)(2,1)S(1)} %copy-done), channel_id=1, source_target_pairs={{0,16},{16,0},{1,17},{17,1},{2,18},{18,2},{3,19},{19,3},{4,20},{20... | collective-permute-start | bytes 3145736 | tf_op jit(solution)/shard_map/ppermute | solution.py:122
  38.3 5.6 %collective-permute-start.2 = (bf16[2,16,4,256]{3,2,1,0:T(4,128)(2,1)S(1)}, bf16[2,16,4,256]{3,2,1,0:T(4,128)(2,1)S(1)}, u32[]{:S(2)}, u32[]{:S(2)}) collective-permute-start(bf16[2,16,4,256]{3,2,1,0:T(4,128)(2,1)S(1)} %get-tuple-element.13), channel_id=1, source_target_pairs={{0,4},{1,5},{2,6},{3,7},{4,8},{5,9},{6,10},{7,11},{8,12},{9,13},{1... | collective-permute-start | bytes 196616 | tf_op jit(solution)/shard_map/ppermute | solution.py:156
  44.0 4.9 %collective-permute-done.2 = bf16[2,16,4,256]{3,2,1,0:T(4,128)(2,1)S(1)} collective-permute-done((bf16[2,16,4,256]{3,2,1,0:T(4,128)(2,1)S(1)}, bf16[2,16,4,256]{3,2,1,0:T(4,128)(2,1)S(1)}, u32[]{:S(2)}, u32[]{:S(2)}) %collective-permute-start.2) | collective-permute-done | bytes 65568 | tf_op jit(solution)/shard_map/ppermute | solution.py:156
  49.0 4.3 %collective-permute-start.3 = (bf16[4,16,4,256]{3,1,2,0:T(8,128)(2,1)S(1)}, bf16[4,16,4,256]{3,1,2,0:T(8,128)(2,1)S(1)}, u32[]{:S(2)}, u32[]{:S(2)}) collective-permute-start(bf16[4,16,4,256]{3,1,2,0:T(8,128)(2,1)S(1)} %bitcast.38), channel_id=1, source_target_pairs={{0,2},{1,3},{2,4},{3,5},{4,6},{5,7},{6,8},{7,9},{8,10},{9,11},{10,... | collective-permute-start | bytes 393224 | tf_op jit(solution)/shard_map/ppermute | solution.py:156
  53.4 3.8 %collective-permute-done.3 = bf16[4,16,4,256]{3,1,2,0:T(8,128)(2,1)S(1)} collective-permute-done((bf16[4,16,4,256]{3,1,2,0:T(8,128)(2,1)S(1)}, bf16[4,16,4,256]{3,1,2,0:T(8,128)(2,1)S(1)}, u32[]{:S(2)}, u32[]{:S(2)}) %collective-permute-start.3) | collective-permute-done | bytes 131104 | tf_op jit(solution)/shard_map/ppermute | solution.py:156
  57.2 4.7 %collective-permute-start.4 = (bf16[8,16,4,256]{3,1,2,0:T(8,128)(2,1)S(1)}, bf16[8,16,4,256]{3,1,2,0:T(8,128)(2,1)S(1)}, u32[]{:S(2)}, u32[]{:S(2)}) collective-permute-start(bf16[8,16,4,256]{3,1,2,0:T(8,128)(2,1)S(1)} %bitcast.36), channel_id=1, source_target_pairs={{0,1},{1,2},{2,3},{3,4},{4,5},{5,6},{6,7},{7,8},{8,9},{9,10},{10,1... | collective-permute-start | bytes 786440 | tf_op jit(solution)/shard_map/ppermute | solution.py:156
  61.9 3.3 %collective-permute-done.4 = bf16[8,16,4,256]{3,1,2,0:T(8,128)(2,1)S(1)} collective-permute-done((bf16[8,16,4,256]{3,1,2,0:T(8,128)(2,1)S(1)}, bf16[8,16,4,256]{3,1,2,0:T(8,128)(2,1)S(1)}, u32[]{:S(2)}, u32[]{:S(2)}) %collective-permute-start.4) | collective-permute-done | bytes 262176 | tf_op jit(solution)/shard_map/ppermute | solution.py:156
  65.2 9.4 %collective-permute-start.5 = (bf16[16,16,4,256]{3,1,2,0:T(8,128)(2,1)S(1)}, bf16[16,16,4,256]{3,1,2,0:T(8,128)(2,1)S(1)}, u32[]{:S(2)}, u32[]{:S(2)}) collective-permute-start(bf16[16,16,4,256]{3,1,2,0:T(8,128)(2,1)S(1)} %bitcast.35), channel_id=1, source_target_pairs={{0,16},{16,0},{1,17},{17,1},{2,18},{18,2},{3,19},{19,3},{4,20},{20... | collective-permute-start | bytes 1572872 | tf_op jit(solution)/shard_map/ppermute | solution.py:159
  75.5 7.4 %shard_map.76 = bf16[16,32,640]{2,1,0:T(8,128)(2,1)} custom-call(s32[2]{0:T(128)S(1)} %pad_add_fusion.refs_0_, bf16[16,48,256]{2,1,0:T(8,128)(2,1)S(1)} %all_to_all.10.refs_1_, bf16[2048,256]{1,0:T(8,128)(2,1)S(1)} %copy-done, bf16[2048,256]{1,0:T(8,128)(2,1)S(1)} %collective-permute-done.refs_3_), custom_call_target="tpu_custom_call" | custom-call | flops 3221225472 | bytes 2097152 | tf_op jit(solution)/shard_map/pallas_call | solution.py:133
  82.9 4.3 %all-to-all-start.1 = ((bf16[16,32,640]{2,1,0:T(8,128)(2,1)}), bf16[16,32,640]{2,1,0:T(8,128)(2,1)}, u32[]{:S(2)}, u32[]{:S(2)}) async-start(bf16[16,32,640]{2,1,0:T(8,128)(2,1)} %shard_map.76), calls=%async_computation.1 | async-start | bytes 1310720 | tf_op jit(solution)/shard_map/all_to_all | solution.py:142
  87.1 0.1 broadcast_select_fusion.2
  87.3 0.4 fusion.1
  87.7 0.1 maximum_bitcast_fusion
  87.8 0.5 copy.19
  88.4 0.3 reshape.26
  88.7 1.1 %broadcast_select_fusion = bf16[2048,256]{1,0:T(8,128)(2,1)} fusion(bf16[2048,256]{1,0:T(8,128)(2,1)S(1)} %reshape.26, bf16[2048,256]{1,0:T(8,128)(2,1)S(1)} %copy-done, pred[]{:T(512)S(6)} %eq.13), kind=kLoop, calls=%fused_computation.5 | loop fusion | flops 524288 | bytes 3145729 | tf_op jit(solution)/shard_map/jit(_where)/select_n | solution.py:166
  89.8 10.3 %all-to-all-done.1.refs_0_ = bf16[16,32,640]{2,1,0:T(8,128)(2,1)} async-done(((bf16[16,32,640]{2,1,0:T(8,128)(2,1)}), bf16[16,32,640]{2,1,0:T(8,128)(2,1)}, u32[]{:S(2)}, u32[]{:S(2)}) %all-to-all-start.1) | async-done | bytes 655392 | tf_op jit(solution)/shard_map/all_to_all | solution.py:142
  100.0 2.1 %shard_map.77 = (f32[1,128]{1,0:T(1,128)}, bf16[32,256]{1,0:T(8,128)(2,1)}) custom-call(bf16[16,32,640]{2,1,0:T(8,128)(2,1)} %all-to-all-done.1.refs_0_, bf16[32,256]{1,0:T(8,128)(2,1)} %refs_1_.1), custom_call_target="tpu_custom_call" | custom-call | tf_op jit(solution)/shard_map/pallas_call | solution.py:144
  102.2 0.7 copy-done.1
  102.8 0.5 slice_bitcast_fusion.2
  (20 shorter events, 0.6 us)
Async XLA Ops:
  0.6 32.9 %copy-start = (bf16[2048,256]{1,0:T(8,128)(2,1)S(1)}, bf16[2048,256]{1,0:T(8,128)(2,1)}, u32[]{:S(2)}) copy-start(bf16[2048,256]{1,0:T(8,128)(2,1)} %refs_2_.1) | copy-start | bytes 3145732
  17.8 20.5 %collective-permute-start.1 = (bf16[1,16,4,256]{3,2,1,0:T(4,128)(2,1)S(1)}, bf16[1,16,4,256]{3,2,1,0:T(4,128)(2,1)S(1)}, u32[]{:S(2)}, u32[]{:S(2)}) collective-permute-start(bf16[1,16,4,256]{3,2,1,0:T(4,128)(2,1)S(1)} %get-tuple-element.11), channel_id=1, source_target_pairs={{0,8},{1,9},{2,10},{3,11},{4,12},{5,13},{6,14},{7,15},{8,0},{9,1},... | collective-permute-start | bytes 98312 | tf_op jit(solution)/shard_map/ppermute | solution.py:156
  33.5 41.9 %collective-permute-start = (bf16[2048,256]{1,0:T(8,128)(2,1)S(1)}, bf16[2048,256]{1,0:T(8,128)(2,1)S(1)}, u32[]{:S(2)}, u32[]{:S(2)}) collective-permute-start(bf16[2048,256]{1,0:T(8,128)(2,1)S(1)} %copy-done), channel_id=1, source_target_pairs={{0,16},{16,0},{1,17},{17,1},{2,18},{18,2},{3,19},{19,3},{4,20},{20... | collective-permute-start | bytes 3145736 | tf_op jit(solution)/shard_map/ppermute | solution.py:122
  38.3 10.6 %collective-permute-start.2 = (bf16[2,16,4,256]{3,2,1,0:T(4,128)(2,1)S(1)}, bf16[2,16,4,256]{3,2,1,0:T(4,128)(2,1)S(1)}, u32[]{:S(2)}, u32[]{:S(2)}) collective-permute-start(bf16[2,16,4,256]{3,2,1,0:T(4,128)(2,1)S(1)} %get-tuple-element.13), channel_id=1, source_target_pairs={{0,4},{1,5},{2,6},{3,7},{4,8},{5,9},{6,10},{7,11},{8,12},{9,13},{1... | collective-permute-start | bytes 196616 | tf_op jit(solution)/shard_map/ppermute | solution.py:156
  49.0 8.1 %collective-permute-start.3 = (bf16[4,16,4,256]{3,1,2,0:T(8,128)(2,1)S(1)}, bf16[4,16,4,256]{3,1,2,0:T(8,128)(2,1)S(1)}, u32[]{:S(2)}, u32[]{:S(2)}) collective-permute-start(bf16[4,16,4,256]{3,1,2,0:T(8,128)(2,1)S(1)} %bitcast.38), channel_id=1, source_target_pairs={{0,2},{1,3},{2,4},{3,5},{4,6},{5,7},{6,8},{7,9},{8,10},{9,11},{10,... | collective-permute-start | bytes 393224 | tf_op jit(solution)/shard_map/ppermute | solution.py:156
  57.2 8.0 %collective-permute-start.4 = (bf16[8,16,4,256]{3,1,2,0:T(8,128)(2,1)S(1)}, bf16[8,16,4,256]{3,1,2,0:T(8,128)(2,1)S(1)}, u32[]{:S(2)}, u32[]{:S(2)}) collective-permute-start(bf16[8,16,4,256]{3,1,2,0:T(8,128)(2,1)S(1)} %bitcast.36), channel_id=1, source_target_pairs={{0,1},{1,2},{2,3},{3,4},{4,5},{5,6},{6,7},{7,8},{8,9},{9,10},{10,1... | collective-permute-start | bytes 786440 | tf_op jit(solution)/shard_map/ppermute | solution.py:156
  65.2 21.9 %collective-permute-start.5 = (bf16[16,16,4,256]{3,1,2,0:T(8,128)(2,1)S(1)}, bf16[16,16,4,256]{3,1,2,0:T(8,128)(2,1)S(1)}, u32[]{:S(2)}, u32[]{:S(2)}) collective-permute-start(bf16[16,16,4,256]{3,1,2,0:T(8,128)(2,1)S(1)} %bitcast.35), channel_id=1, source_target_pairs={{0,16},{16,0},{1,17},{17,1},{2,18},{18,2},{3,19},{19,3},{4,20},{20... | collective-permute-start | bytes 1572872 | tf_op jit(solution)/shard_map/ppermute | solution.py:159
  82.9 17.2 %all-to-all-start.1 = ((bf16[16,32,640]{2,1,0:T(8,128)(2,1)}), bf16[16,32,640]{2,1,0:T(8,128)(2,1)}, u32[]{:S(2)}, u32[]{:S(2)}) async-start(bf16[16,32,640]{2,1,0:T(8,128)(2,1)} %shard_map.76), calls=%async_computation.1 | async-start | bytes 1310720 | tf_op jit(solution)/shard_map/all_to_all | solution.py:142
  102.2 0.7 copy-start.1

commit v2 on v1

--- a/solution.py
+++ b/solution.py
@@ -11,6 +11,7 @@
 BF = jnp.bfloat16
 F32 = jnp.float32
 ROWS = 48
+MIB = 1024 * 1024
 LOG2E = 1.4426950408889634
 VMEM = pl.BlockSpec(memory_space=pltpu.VMEM)
 SMEM = pl.BlockSpec(memory_space=pltpu.SMEM)
@@ -31,10 +32,8 @@
     for j in range(srcs):
         q_ref[j * nq:(j + 1) * nq, :] = msg_ref[j, :nq, :]
         tail = msg_ref[j, nq:, :].astype(F32)
-        line = jnp.broadcast_to(tail[4:5, :], (nq, width))
-        hi = jnp.sum(jnp.where(lane == row, line, 0.0), axis=1, keepdims=True)
-        lo = jnp.sum(jnp.where(lane == row + nq, line, 0.0), axis=1, keepdims=True)
-        parts.append(hi * 256.0 + lo)
+        line = tail[4:5, :] * 256.0 + tail[5:6, :]
+        parts.append(jnp.sum(jnp.where(lane == row, line, 0.0), axis=1, keepdims=True))
     target = jnp.concatenate(parts, axis=0).astype(jnp.int32)
     queries = q_ref[...]
     top = None
@@ -73,9 +72,11 @@
     positive = positive.astype(BF)
     for j in range(srcs):
         at = slice(j * nq, (j + 1) * nq)
-        out_ref[j, :, :width] = grad[at]
-        out_ref[j, :, width:2 * width] = positive[at]
-        out_ref[j, :, 2 * width:] = stats[at]
+        out_ref[j, :nq, :] = grad[at]
+        out_ref[j, nq:2 * nq, :] = positive[at]
+        half = nq // 2
+        out_ref[j, 2 * nq:2 * nq + half, :128] = stats[j * nq:j * nq + half]
+        out_ref[j, 2 * nq:2 * nq + half, 128:] = stats[j * nq + half:(j + 1) * nq]
 
 
 def combine_kernel(scale, srcs, nq, got_ref, q_ref, loss_ref, grad_ref):
@@ -83,8 +84,9 @@
     positive = jnp.zeros((nq, width), F32)
     points, totals = [], []
     for j in range(srcs):
-        positive += got_ref[j, :, width:2 * width].astype(F32)
-        st = got_ref[j, :, 2 * width:].astype(F32)
+        positive += got_ref[j, nq:2 * nq, :].astype(F32)
+        st = got_ref[j, 2 * nq:2 * nq + nq // 2, :].astype(F32)
+        st = jnp.concatenate([st[:, :128], st[:, 128:]], axis=0)
         points.append(st[:, 0:1])
         totals.append(st[:, 1:2] + st[:, 2:3] + st[:, 3:4])
     s_pos = jnp.sum(q_ref[...].astype(F32) * positive, axis=1, keepdims=True)
@@ -96,7 +98,7 @@
     for j in range(srcs):
         a = jnp.exp2((points[j] - top) * (scale * LOG2E))
         total += a * totals[j]
-        grad += a * got_ref[j, :, :width].astype(F32)
+        grad += a * got_ref[j, :nq, :].astype(F32)
     log_total = jnp.log(total)
     lse = top * scale + log_total
     weight = (jnp.exp(s_pos * scale - lse) - 1.0).astype(BF).astype(F32)
@@ -105,6 +107,63 @@
     lane = lax.broadcasted_iota(jnp.int32, (nq, 128), 1)
     row = lax.broadcasted_iota(jnp.int32, (nq, 128), 0)
     loss_ref[...] = jnp.sum(jnp.where(lane == row, loss, 0.0), axis=0, keepdims=True)
+
+
+def message_kernel(copies, q_ref, pos_ref, tail_ref, out_ref):
+    nq = q_ref.shape[0]
+    tail = tail_ref[...].astype(F32)
+    row = lax.broadcasted_iota(jnp.int32, tail.shape, 0)
+    high = (pos_ref[...] >> 8).astype(F32)
+    low = (pos_ref[...] & 255).astype(F32)
+    tail = jnp.where(row == 4, high, jnp.where(row == 5, low, tail)).astype(BF)
+    for j in range(copies):
+        out_ref[j, :nq, :] = q_ref[...]
+        out_ref[j, nq:, :] = tail
+
+
+def fill_kernel(copies, at, keys_ref, in_ref, out_ref):
+    del in_ref
+    keys = keys_ref[...]
+    for j in range(copies):
+        out_ref[j, at:at + keys.shape[0], :] = keys
+
+
+def place_kernel(at, place_ref, mine_ref, twin_ref, queue_ref, out_ref):
+    owner, core, z = place_ref[0], place_ref[1], place_ref[2]
+    cols, rows = twin_ref.shape[0], twin_ref.shape[1]
+    width = queue_ref.shape[1]
+
+    @pl.when(owner == 0)
+    def _():
+        out_ref[...] = queue_ref[...]
+
+    def put(ref, base, c):
+        row = lax.broadcasted_iota(jnp.int32, (8, width), 0)
+        for a in range(rows // 16):
+            for b in range(4):
+                tiles = []
+                for k in range(4):
+                    plane = 4 * b + k
+                    slot = ((z - plane) if c == 0 else (plane - z)) & (cols - 1)
+                    block = ref[slot, base + 16 * a:base + 16 * a + 16, :].astype(F32)
+                    tiles.append((block[:8], block[8:]))
+                for v in range(4):
+                    t = [tiles[k][v // 2] for k in range(4)]
+                    if v % 2 == 0:
+                        up = jnp.where(row < 4, t[0], pltpu.roll(t[1], 4, 0))
+                        down = jnp.where(row < 4, t[2], pltpu.roll(t[3], 4, 0))
+                    else:
+                        up = jnp.where(row < 4, pltpu.roll(t[0], 4, 0), t[1])
+                        down = jnp.where(row < 4, pltpu.roll(t[2], 4, 0), t[3])
+                    chip = 4 * a + v
+                    start = (chip * 2 + c) * 64 + 16 * b
+                    out_ref[start:start + 16, :] = jnp.concatenate([up, down], axis=0).astype(BF)
+
+    for mine in (0, 1):
+        @pl.when((owner == 1) & (core == mine))
+        def _():
+            put(mine_ref, at, mine)
+            put(twin_ref, 0, 1 - mine)
 
 
 def local(queries, positions, queue, new_keys, step):
@@ -118,52 +177,71 @@
     core = lax.axis_index("c")
     z = lax.axis_index("z")
     slab_index = chip * 2 + core
-
-    other = lax.ppermute(queue, "c", [(0, 1), (1, 0)])
-
-    hi = (positions // 256).astype(BF)
-    lo = (positions % 256).astype(BF)
-    line = jnp.concatenate([hi, lo, jnp.zeros((width - 2 * nq,), BF)])[None]
-    message = jnp.concatenate([queries, new_keys, line, jnp.zeros((ROWS - nq - nk - 1, width), BF)], axis=0)
-    got = lax.all_to_all(jnp.broadcast_to(message[None], (srcs, ROWS, width)), ("x", "y"), 0, 0)
+    swap = [(0, 1), (1, 0)]
+
+    other = lax.ppermute(queue, "c", swap)
+
+    message = pl.pallas_call(
+        lambda *refs: message_kernel(srcs, *refs),
+        out_shape=jax.ShapeDtypeStruct((srcs, ROWS, width), BF),
+        in_specs=[VMEM] * 3,
+        out_specs=VMEM,
+        compiler_params=pltpu.CompilerParams(vmem_limit_bytes=4 * MIB),
+    )(queries, jnp.pad(positions, (0, width - nq))[None], jnp.pad(new_keys, ((0, ROWS - nq - nk), (0, 0))))
+    got = lax.all_to_all(message, ("x", "y"), 0, 0)
+
+    pairs = []
+    for s in range(srcs):
+        for c in range(2):
+            for k in range(nz):
+                to = (k + s) % nz if c == 0 else (k - s) % nz
+                pairs.append(((s * 2 + c) * nz + k, (s * 2 + c) * nz + to))
+    plane_keys = got[:, nq:nq + nk, :].reshape(srcs * nk, width)
+    moved = lax.ppermute(plane_keys, ("x", "y", "c", "z"), pairs)
 
     first = jnp.stack([slab_index * slab, (slab_index ^ 1) * slab]).astype(jnp.int32)
     n = srcs * nq
+    at = 2 * nq + nq // 2
     flops = 2 * n * 2 * slab * width
+    out_shape = jax.ShapeDtypeStruct((srcs, at + srcs * nk, width), BF)
     out = pl.pallas_call(
         lambda *refs: partial_kernel(scale, srcs, nq, *refs),
-        out_shape=jax.ShapeDtypeStruct((srcs, nq, 2 * width + 128), BF),
+        out_shape=out_shape,
         in_specs=[SMEM, VMEM, VMEM, VMEM],
         out_specs=VMEM,
         scratch_shapes=[pltpu.VMEM((n, width), BF), pltpu.VMEM((n, 2 * slab), F32)],
-        compiler_params=pltpu.CompilerParams(vmem_limit_bytes=40 * 1024 * 1024),
+        compiler_params=pltpu.CompilerParams(vmem_limit_bytes=24 * MIB),
         cost_estimate=pl.CostEstimate(flops=3 * flops, bytes_accessed=4 * slab * width, transcendentals=2 * n * slab),
     )(first, got, queue, other)
+    out = pl.pallas_call(
+        lambda *refs: fill_kernel(srcs, at, *refs),
+        out_shape=out_shape,
+        in_specs=[VMEM, VMEM],
+        out_specs=VMEM,
+        input_output_aliases={1: 0},
+        compiler_params=pltpu.CompilerParams(vmem_limit_bytes=8 * MIB),
+    )(moved, out)
     back = lax.all_to_all(out, ("x", "y"), 0, 0)
 
+    twin = lax.ppermute(back[:, at:, :], "c", swap)
     loss, grad = pl.pallas_call(
         lambda *refs: combine_kernel(scale, srcs, nq, *refs),
         out_shape=(jax.ShapeDtypeStruct((1, 128), F32), jax.ShapeDtypeStruct((nq, width), BF)),
         in_specs=[VMEM, VMEM],
         out_specs=(VMEM, VMEM),
+        compiler_params=pltpu.CompilerParams(vmem_limit_bytes=8 * MIB),
     )(back, queries)
     losses = loss[0, :nq]
 
-    ring = got[:, nq:nq + nk, :][None]
-    gap = nz // 2
-    while gap:
-        pairs = [(i, (i + gap) % nz) for i in range(nz)] + [(nz + i, nz + (i - gap) % nz) for i in range(nz)]
-        came = lax.ppermute(ring, ("c", "z"), pairs)
-        ring = jnp.stack([ring, came], axis=1).reshape((2 * ring.shape[0],) + ring.shape[1:])
-        gap //= 2
-    twin = lax.ppermute(ring, "c", [(0, 1), (1, 0)])
-    low = jnp.where(core == 0, ring, twin)
-    high = jnp.where(core == 0, twin, ring)
-    low = jnp.roll(low[::-1], z + 1, axis=0)
-    high = jnp.roll(high, z, axis=0)
-    arrived = jnp.stack([low, high], axis=0).transpose(2, 0, 1, 3, 4).reshape(slab, width)
-    owner = step[0] % (srcs * 2)
-    updated = jnp.where(owner == slab_index, arrived, queue)
+    owner = (step[0] % (srcs * 2)) == slab_index
+    place = jnp.stack([owner.astype(jnp.int32), core, z]).astype(jnp.int32)
+    updated = pl.pallas_call(
+        lambda *refs: place_kernel(at, *refs),
+        out_shape=jax.ShapeDtypeStruct(queue.shape, BF),
+        in_specs=[SMEM, VMEM, VMEM, VMEM],
+        out_specs=VMEM,
+        compiler_params=pltpu.CompilerParams(vmem_limit_bytes=12 * MIB),
+    )(place, back, twin, queue)
     return losses, grad, updated
 
 

time: 104 us -> 73.1 us (0.70)
  starting transfers between devices: 48.8 us -> 18.3 us
  blocking collectives: 15.4 us -> 31.1 us
  waiting for transfers between devices: 22.3 us -> 9.13 us
  other arithmetic: 3.64 us -> 0.15 us
    ppermute x6 -> x3, starting transfers between devices: 44.6 us -> 14.7 us  [the longest x1 8.92 us: local(): other = lax.ppermute(queue, 'c', swap)]
    all_to_all x1, blocking collectives: 15.4 us -> 31.1 us  [local(): back = lax.all_to_all(out, ('x', 'y'), 0, 0)]
    ppermute x6 -> x3, waiting for transfers between devices: 12 us -> 0.01 us  [the longest x1 0.01 us: local(): other = lax.ppermute(queue, 'c', swap)]
    pallas_call x0 -> x3, Pallas kernels: none -> 2.4 us  [the longest x1 1.59 us: local(): pl.pallas_call(lambda *refs: place_kernel(at, *refs), out_shape=jax.Shape...]
    pad x0 -> x2, local copies, waits for them, and re-layouts: none -> 1.35 us  [the longest x1 0.69 us: local(): jnp.pad(new_keys, ((0, ROWS - nq - nk), (0, 0)))]
    select_n x2 -> x0, other arithmetic: 1.19 us -> none  [the longest x1 1.08 us: local(): updated = jnp.where(owner == slab_index, arrived, queue)]
    all_to_all x1, waiting for transfers between devices: 10.3 us -> 9.13 us  [local(): got = lax.all_to_all(message, ('x', 'y'), 0, 0)]
    pallas_call x1, Pallas kernels: 2.13 us -> 1.04 us  [local(): pl.pallas_call(lambda *refs: combine_kernel(scale, srcs, nq, *refs), out_...]
  transfers between devices with their start and end apart: 7 -> 4, of which waited for: 4 -> 1; matrix products, arithmetic and copies ran while one was open for 3% -> 3% of each run, Pallas kernels for 7% -> 11%
where the time goes in v2:
time: 73.1 us; the launch traced here: 72.7 us
  blocking collectives  31.1 us (43%)
  starting transfers between devices  18.3 us (25%)
  Pallas kernels  9.95 us (14%)
  waiting for transfers between devices  9.13 us (12%)
  local copies, waits for them, and re-layouts  2.66 us (4%)
  between operations  1.42 us (2%)
    all_to_all x1, blocking collectives, local(): back = lax.all_to_all(out, ('x', 'y'), 0, 0)  31.1 us
    all_to_all x1, waiting for transfers between devices, local(): got = lax.all_to_all(message, ('x', 'y'), 0, 0)  9.13 us
    ppermute x1, starting transfers between devices, local(): other = lax.ppermute(queue, 'c', swap)  8.92 us
    pallas_call x1, Pallas kernels, local(): pl.pallas_call(lambda *refs: partial_kernel(scale, srcs, nq, *refs), out_...  6.5 us
    ppermute x1, starting transfers between devices, local(): twin = lax.ppermute(back[:, at:, :], 'c', swap)  5.15 us
    all_to_all x1, starting transfers between devices, local(): got = lax.all_to_all(message, ('x', 'y'), 0, 0)  3.55 us
    pallas_call x1, Pallas kernels, local(): pl.pallas_call(lambda *refs: place_kernel(at, *refs), out_shape=jax.Shape...  1.59 us
  transfers between devices with their start and end apart: 4, of which 1 were waited for; matrix products, arithmetic and copies ran while one was open for 3% of the time, Pallas kernels for 11%

profile of v2, /device:TPU:1, one launch (start us, length us, event | category | flops | bytes accessed | tf_op | source)
XLA Modules:
  0.0 72.7 jit_solution(8578272128874966856)
XLA Ops:
  0.6 0.0 copy-start
  0.6 8.9 %collective-permute-start.1 = (bf16[2048,256]{1,0:T(8,128)(2,1)}, bf16[2048,256]{1,0:T(8,128)(2,1)S(1)}, u32[]{:S(2)}, u32[]{:S(2)}) collective-permute-start(bf16[2048,256]{1,0:T(8,128)(2,1)} %refs_3_.1), channel_id=1, source_target_pairs={{0,16},{16,0},{1,17},{17,1},{2,18},{18,2},{3,19},{19,3},{4,20},{20... | collective-permute-start | bytes 3145736 | tf_op jit(solution)/shard_map/ppermute | solution.py:182
  9.6 0.7 pad.9.refs_2_
  10.3 0.7 pad.8
  10.9 0.0 copy-start.1
  10.9 0.7 copy-done.1
  11.6 0.8 %shard_map.76 = bf16[16,48,256]{2,1,0:T(8,128)(2,1)} custom-call(bf16[32,256]{1,0:T(8,128)(2,1)S(1)} %copy-done.1, s32[1,256]{1,0:T(1,128)S(1)} %bitcast.12, bf16[16,256]{1,0:T(8,128)(2,1)S(1)} %pad.9.refs_2_), custom_call_target="tpu_custom_call" | custom-call | tf_op jit(solution)/shard_map/pallas_call | solution.py:184
  12.4 3.6 %all-to-all-start = ((bf16[16,48,256]{2,1,0:T(8,128)(2,1)}), bf16[16,48,256]{2,1,0:T(8,128)(2,1)S(1)}, u32[]{:S(2)}, u32[]{:S(2)}) async-start(bf16[16,48,256]{2,1,0:T(8,128)(2,1)} %shard_map.76), calls=%async_computation | async-start | bytes 786432 | tf_op jit(solution)/shard_map/all_to_all | solution.py:191
  16.0 0.1 pad_add_fusion.refs_0_
  16.1 9.1 %all-to-all-done.refs_1_ = bf16[16,48,256]{2,1,0:T(8,128)(2,1)S(1)} async-done(((bf16[16,48,256]{2,1,0:T(8,128)(2,1)}), bf16[16,48,256]{2,1,0:T(8,128)(2,1)S(1)}, u32[]{:S(2)}, u32[]{:S(2)}) %all-to-all-start) | async-done | bytes 393248 | tf_op jit(solution)/shard_map/all_to_all | solution.py:191
  25.2 0.7 collective-permute-start
  25.9 0.0 collective-permute-done.1.refs_3_
  25.9 0.0 copy-done
  25.9 6.5 %shard_map.77.refs_1_ = bf16[16,144,256]{2,1,0:T(8,128)(2,1)S(1)} custom-call(s32[2]{0:T(128)S(1)} %pad_add_fusion.refs_0_, bf16[16,48,256]{2,1,0:T(8,128)(2,1)S(1)} %all-to-all-done.refs_1_, bf16[2048,256]{1,0:T(8,128)(2,1)S(1)} %copy-done, bf16[2048,256]{1,0:T(8,128)(2,1)S(1)} %collective-permute-done.1.refs_3_), custom_call_target="tpu_custom_call" | custom-call | flops 3221225472 | bytes 2097152 | tf_op jit(solution)/shard_map/pallas_call | solution.py:207
  32.4 0.0 collective-permute-done.refs_0_
  32.5 0.0 copy-start.2
  32.5 31.1 %all_to_all.10.refs_0_.refs_1_ = bf16[16,144,256]{2,1,0:T(8,128)(2,1)S(1)} all-to-all(bf16[16,144,256]{2,1,0:T(8,128)(2,1)S(1)} %shard_map.78), channel_id=1, replica_groups=mesh['x'=4,'y'=4,'c'=2,'z'=16] {'x','y'}, dimensions={0} | all-to-all | bytes 2359296 | tf_op jit(solution)/shard_map/all_to_all | solution.py:224
  63.6 5.2 %collective-permute-start.2 = (bf16[16,64,256]{2,1,0:T(8,128)(2,1)S(1)}, bf16[16,64,256]{2,1,0:T(8,128)(2,1)S(1)}, u32[]{:S(2)}, u32[]{:S(2)}) collective-permute-start(bf16[16,64,256]{2,1,0:T(8,128)(2,1)S(1)} %slice.13), channel_id=1, source_target_pairs={{0,16},{16,0},{1,17},{17,1},{2,18},{18,2},{3,19},{19,3},{4,20},{20... | collective-permute-start | bytes 1572872 | tf_op jit(solution)/shard_map/ppermute | solution.py:226
  69.4 0.1 pad_add_fusion.1.refs_0_
  69.5 0.0 copy-done.2
  69.5 1.0 %shard_map.79 = (f32[1,128]{1,0:T(1,128)S(1)}, bf16[32,256]{1,0:T(8,128)(2,1)}) custom-call(bf16[16,144,256]{2,1,0:T(8,128)(2,1)S(1)} %all_to_all.10.refs_0_.refs_1_, bf16[32,256]{1,0:T(8,128)(2,1)S(1)} %copy-done.2), custom_call_target="tpu_custom_call" | custom-call | tf_op jit(solution)/shard_map/pallas_call | solution.py:227
  70.6 0.5 slice_bitcast_fusion
  71.1 0.0 collective-permute-done.2.refs_2_
  71.1 1.6 %shard_map.80 = bf16[2048,256]{1,0:T(8,128)(2,1)} custom-call(s32[3]{0:T(128)S(1)} %pad_add_fusion.1.refs_0_, bf16[16,144,256]{2,1,0:T(8,128)(2,1)S(1)} %all_to_all.10.refs_0_.refs_1_, bf16[16,64,256]{2,1,0:T(8,128)(2,1)S(1)} %collective-permute-done.2.refs_2_, bf16[2048,256]{1,0:T(8,128)(2,1)S(1)} %copy-done), custom_call_target="tpu_custom_call" | custom-call | tf_op jit(solution)/shard_map/pallas_call | solution.py:238
  (4 shorter events, 0.1 us)
Async XLA Ops:
  0.6 25.3 %copy-start = (bf16[2048,256]{1,0:T(8,128)(2,1)S(1)}, bf16[2048,256]{1,0:T(8,128)(2,1)}, u32[]{:S(2)}) copy-start(bf16[2048,256]{1,0:T(8,128)(2,1)} %refs_3_.1) | copy-start | bytes 3145732
  0.6 25.3 %collective-permute-start.1 = (bf16[2048,256]{1,0:T(8,128)(2,1)}, bf16[2048,256]{1,0:T(8,128)(2,1)S(1)}, u32[]{:S(2)}, u32[]{:S(2)}) collective-permute-start(bf16[2048,256]{1,0:T(8,128)(2,1)} %refs_3_.1), channel_id=1, source_target_pairs={{0,16},{16,0},{1,17},{17,1},{2,18},{18,2},{3,19},{19,3},{4,20},{20... | collective-permute-start | bytes 3145736 | tf_op jit(solution)/shard_map/ppermute | solution.py:182
  10.9 0.7 copy-start.1
  12.4 12.8 %all-to-all-start = ((bf16[16,48,256]{2,1,0:T(8,128)(2,1)}), bf16[16,48,256]{2,1,0:T(8,128)(2,1)S(1)}, u32[]{:S(2)}, u32[]{:S(2)}) async-start(bf16[16,48,256]{2,1,0:T(8,128)(2,1)} %shard_map.76), calls=%async_computation | async-start | bytes 786432 | tf_op jit(solution)/shard_map/all_to_all | solution.py:191
  25.2 7.2 %collective-permute-start = (bf16[64,256]{1,0:T(8,128)(2,1)S(1)}, bf16[64,256]{1,0:T(8,128)(2,1)S(1)}, u32[]{:S(2)}, u32[]{:S(2)}) collective-permute-start(bf16[64,256]{1,0:T(8,128)(2,1)S(1)} %reshape.9), channel_id=1, source_target_pairs={{0,0},{1,1},{2,2},{3,3},{4,4},{5,5},{6,6},{7,7},{8,8},{9,9},{10,10... | collective-permute-start | bytes 98312 | tf_op jit(solution)/shard_map/ppermute | solution.py:200
  32.5 37.1 %copy-start.2 = (bf16[32,256]{1,0:T(8,128)(2,1)S(1)}, bf16[32,256]{1,0:T(8,128)(2,1)}, u32[]{:S(2)}) copy-start(bf16[32,256]{1,0:T(8,128)(2,1)} %refs_1_.1) | copy-start | bytes 49156
  63.6 7.5 %collective-permute-start.2 = (bf16[16,64,256]{2,1,0:T(8,128)(2,1)S(1)}, bf16[16,64,256]{2,1,0:T(8,128)(2,1)S(1)}, u32[]{:S(2)}, u32[]{:S(2)}) collective-permute-start(bf16[16,64,256]{2,1,0:T(8,128)(2,1)S(1)} %slice.13), channel_id=1, source_target_pairs={{0,16},{16,0},{1,17},{17,1},{2,18},{18,2},{3,19},{19,3},{4,20},{20... | collective-permute-start | bytes 1572872 | tf_op jit(solution)/shard_map/ppermute | solution.py:226

commit v3 on v2

--- a/solution.py
+++ b/solution.py
@@ -11,9 +11,12 @@
 BF = jnp.bfloat16
 F32 = jnp.float32
 ROWS = 48
+PIECES = 4
 MIB = 1024 * 1024
 LOG2E = 1.4426950408889634
 VMEM = pl.BlockSpec(memory_space=pltpu.VMEM)
+ANY = pl.BlockSpec(memory_space=pl.ANY)
+LATE = pl.CostEstimate(flops=6 * 10**9, bytes_accessed=0, transcendentals=0)
 SMEM = pl.BlockSpec(memory_space=pltpu.SMEM)
 
 
@@ -21,7 +24,8 @@
     return lax.dot_general(a, b, (((1,), (1,)), ((), ())), preferred_element_type=F32)
 
 
-def partial_kernel(scale, srcs, nq, first_ref, msg_ref, own_ref, other_ref, out_ref, q_ref, s_ref):
+def partial_kernel(scale, srcs, nq, first_ref, msg_ref, own_ref, *refs):
+    *other_refs, _, out_ref, q_ref, s_ref = refs
     width = own_ref.shape[1]
     slab = own_ref.shape[0]
     n = srcs * nq
@@ -38,10 +42,13 @@
     queries = q_ref[...]
     top = None
     blocks = []
-    for half, ref in enumerate((own_ref, other_ref)):
-        for b in range(slab // block):
-            blocks.append((half, ref, b))
-    for i, (half, ref, b) in enumerate(blocks):
+    for b in range(slab // block):
+        blocks.append((first_ref[0] + b * block, own_ref, b))
+    cut = slab // len(other_refs)
+    for i, ref in enumerate(other_refs):
+        for b in range(cut // block):
+            blocks.append((first_ref[1] + i * cut + b * block, ref, b))
+    for i, (start, ref, b) in enumerate(blocks):
         s = rows_dot(queries, ref[b * block:(b + 1) * block, :])
         s_ref[:, i * block:(i + 1) * block] = s
         for c in range(block // 128):
@@ -52,9 +59,9 @@
     grad = jnp.zeros((n, width), F32)
     positive = jnp.zeros((n, width), F32)
     column = lax.broadcasted_iota(jnp.int32, (n, block), 1)
-    for i, (half, ref, b) in enumerate(blocks):
+    for i, (start, ref, b) in enumerate(blocks):
         s = s_ref[:, i * block:(i + 1) * block]
-        hit = column == (target - (first_ref[half] + b * block))
+        hit = column == (target - start)
         e = jnp.where(hit, 0.0, jnp.exp2((s - point) * (scale * LOG2E)))
         for c in range(block // 128):
             total += e[:, c * 128:(c + 1) * 128]
@@ -109,26 +116,41 @@
     loss_ref[...] = jnp.sum(jnp.where(lane == row, loss, 0.0), axis=0, keepdims=True)
 
 
-def message_kernel(copies, q_ref, pos_ref, tail_ref, out_ref):
-    nq = q_ref.shape[0]
-    tail = tail_ref[...].astype(F32)
-    row = lax.broadcasted_iota(jnp.int32, tail.shape, 0)
-    high = (pos_ref[...] >> 8).astype(F32)
-    low = (pos_ref[...] & 255).astype(F32)
-    tail = jnp.where(row == 4, high, jnp.where(row == 5, low, tail)).astype(BF)
+def message_kernel(copies, q_ref, pos_ref, keys_ref, out_ref, tail_ref):
+    nq, nk = q_ref.shape[0], keys_ref.shape[0]
+    tail_ref[...] = jnp.zeros_like(tail_ref)
+    tail_ref[:nk, :] = keys_ref[...].astype(F32)
+    tail_ref[nk:nk + 1, :nq] = (pos_ref[...] >> 8).astype(F32)
+    tail_ref[nk + 1:nk + 2, :nq] = (pos_ref[...] & 255).astype(F32)
+    tail = tail_ref[...].astype(BF)
     for j in range(copies):
         out_ref[j, :nq, :] = q_ref[...]
         out_ref[j, nq:, :] = tail
 
 
-def fill_kernel(copies, at, keys_ref, in_ref, out_ref):
-    del in_ref
-    keys = keys_ref[...]
+def copies_kernel(copies, keys_ref, after_ref, out_ref):
+    del after_ref
     for j in range(copies):
-        out_ref[j, at:at + keys.shape[0], :] = keys
-
-
-def place_kernel(at, place_ref, mine_ref, twin_ref, queue_ref, out_ref):
+        out_ref[j] = keys_ref[...]
+
+
+def gate_kernel(after_ref, out_ref):
+    del after_ref
+    out_ref[...] = jnp.zeros_like(out_ref)
+
+
+def plane_keys_kernel(nq, got_ref, after_ref, out_ref):
+    del after_ref
+    width = out_ref.shape[1]
+    row = lax.broadcasted_iota(jnp.int32, (8, width), 0)
+    for a in range(got_ref.shape[0] // 4):
+        t = [got_ref[4 * a + k, nq:, :].astype(F32)[:8] for k in range(4)]
+        up = jnp.where(row < 4, t[0], pltpu.roll(t[1], 4, 0))
+        down = jnp.where(row < 4, t[2], pltpu.roll(t[3], 4, 0))
+        out_ref[16 * a:16 * a + 16, :] = jnp.concatenate([up, down], axis=0).astype(BF)
+
+
+def place_kernel(place_ref, mine_ref, twin_ref, queue_ref, out_ref):
     owner, core, z = place_ref[0], place_ref[1], place_ref[2]
     cols, rows = twin_ref.shape[0], twin_ref.shape[1]
     width = queue_ref.shape[1]
@@ -137,7 +159,7 @@
     def _():
         out_ref[...] = queue_ref[...]
 
-    def put(ref, base, c):
+    def put(ref, c):
         row = lax.broadcasted_iota(jnp.int32, (8, width), 0)
         for a in range(rows // 16):
             for b in range(4):
@@ -145,7 +167,7 @@
                 for k in range(4):
                     plane = 4 * b + k
                     slot = ((z - plane) if c == 0 else (plane - z)) & (cols - 1)
-                    block = ref[slot, base + 16 * a:base + 16 * a + 16, :].astype(F32)
+                    block = ref[slot, 16 * a:16 * a + 16, :].astype(F32)
                     tiles.append((block[:8], block[8:]))
                 for v in range(4):
                     t = [tiles[k][v // 2] for k in range(4)]
@@ -162,8 +184,8 @@
     for mine in (0, 1):
         @pl.when((owner == 1) & (core == mine))
         def _():
-            put(mine_ref, at, mine)
-            put(twin_ref, 0, 1 - mine)
+            put(mine_ref, mine)
+            put(twin_ref, 1 - mine)
 
 
 def local(queries, positions, queue, new_keys, step):
@@ -179,16 +201,48 @@
     slab_index = chip * 2 + core
     swap = [(0, 1), (1, 0)]
 
-    other = lax.ppermute(queue, "c", swap)
-
     message = pl.pallas_call(
         lambda *refs: message_kernel(srcs, *refs),
         out_shape=jax.ShapeDtypeStruct((srcs, ROWS, width), BF),
         in_specs=[VMEM] * 3,
         out_specs=VMEM,
+        scratch_shapes=[pltpu.VMEM((ROWS - nq, width), F32)],
+        compiler_params=pltpu.CompilerParams(vmem_limit_bytes=56 * MIB),
+    )(queries, positions[None], new_keys)
+    got = lax.all_to_all(message, ("x", "y"), 0, 0)
+    gate = pl.pallas_call(
+        gate_kernel,
+        out_shape=jax.ShapeDtypeStruct((8, 128), F32),
+        in_specs=[ANY],
+        out_specs=VMEM,
+        compiler_params=pltpu.CompilerParams(vmem_limit_bytes=MIB),
+        cost_estimate=LATE,
+    )(message)
+    slab_keys, gate = lax.optimization_barrier((queue, gate))
+    cut = slab // PIECES
+    other = [lax.ppermute(slab_keys[i * cut:(i + 1) * cut], "c", swap) for i in range(PIECES)]
+
+    first = jnp.stack([slab_index * slab, (slab_index ^ 1) * slab]).astype(jnp.int32)
+    n = srcs * nq
+    flops = 2 * n * 2 * slab * width
+    out = pl.pallas_call(
+        lambda *refs: partial_kernel(scale, srcs, nq, *refs),
+        out_shape=jax.ShapeDtypeStruct((srcs, 2 * nq + nq // 2, width), BF),
+        in_specs=[SMEM, VMEM, VMEM] + [VMEM] * PIECES + [ANY],
+        out_specs=VMEM,
+        scratch_shapes=[pltpu.VMEM((n, width), BF), pltpu.VMEM((n, 2 * slab), F32)],
+        compiler_params=pltpu.CompilerParams(vmem_limit_bytes=24 * MIB),
+        cost_estimate=pl.CostEstimate(flops=3 * flops, bytes_accessed=4 * slab * width, transcendentals=2 * n * slab),
+    )(first, got, queue, *other, gate)
+    back = lax.all_to_all(out, ("x", "y"), 0, 0)
+    plane_keys = pl.pallas_call(
+        lambda *refs: plane_keys_kernel(nq, *refs),
+        out_shape=jax.ShapeDtypeStruct((srcs * nk, width), BF),
+        in_specs=[VMEM, ANY],
+        out_specs=VMEM,
         compiler_params=pltpu.CompilerParams(vmem_limit_bytes=4 * MIB),
-    )(queries, jnp.pad(positions, (0, width - nq))[None], jnp.pad(new_keys, ((0, ROWS - nq - nk), (0, 0))))
-    got = lax.all_to_all(message, ("x", "y"), 0, 0)
+        cost_estimate=LATE,
+    )(got, out)
 
     pairs = []
     for s in range(srcs):
@@ -196,34 +250,19 @@
             for k in range(nz):
                 to = (k + s) % nz if c == 0 else (k - s) % nz
                 pairs.append(((s * 2 + c) * nz + k, (s * 2 + c) * nz + to))
-    plane_keys = got[:, nq:nq + nk, :].reshape(srcs * nk, width)
     moved = lax.ppermute(plane_keys, ("x", "y", "c", "z"), pairs)
-
-    first = jnp.stack([slab_index * slab, (slab_index ^ 1) * slab]).astype(jnp.int32)
-    n = srcs * nq
-    at = 2 * nq + nq // 2
-    flops = 2 * n * 2 * slab * width
-    out_shape = jax.ShapeDtypeStruct((srcs, at + srcs * nk, width), BF)
-    out = pl.pallas_call(
-        lambda *refs: partial_kernel(scale, srcs, nq, *refs),
-        out_shape=out_shape,
-        in_specs=[SMEM, VMEM, VMEM, VMEM],
-        out_specs=VMEM,
-        scratch_shapes=[pltpu.VMEM((n, width), BF), pltpu.VMEM((n, 2 * slab), F32)],
-        compiler_params=pltpu.CompilerParams(vmem_limit_bytes=24 * MIB),
-        cost_estimate=pl.CostEstimate(flops=3 * flops, bytes_accessed=4 * slab * width, transcendentals=2 * n * slab),
-    )(first, got, queue, other)
-    out = pl.pallas_call(
-        lambda *refs: fill_kernel(srcs, at, *refs),
-        out_shape=out_shape,
-        in_specs=[VMEM, VMEM],
-        out_specs=VMEM,
-        input_output_aliases={1: 0},
-        compiler_params=pltpu.CompilerParams(vmem_limit_bytes=8 * MIB),
-    )(moved, out)
-    back = lax.all_to_all(out, ("x", "y"), 0, 0)
-
-    twin = lax.ppermute(back[:, at:, :], "c", swap)
+    mine = lax.all_to_all(
+        pl.pallas_call(
+            lambda *refs: copies_kernel(srcs, *refs),
+            out_shape=jax.ShapeDtypeStruct((srcs, srcs * nk, width), BF),
+            in_specs=[VMEM, ANY],
+            out_specs=VMEM,
+            compiler_params=pltpu.CompilerParams(vmem_limit_bytes=4 * MIB),
+        )(moved, back),
+        ("x", "y"), 0, 0,
+    )
+    twin = lax.ppermute(mine, "c", swap)
+
     loss, grad = pl.pallas_call(
         lambda *refs: combine_kernel(scale, srcs, nq, *refs),
         out_shape=(jax.ShapeDtypeStruct((1, 128), F32), jax.ShapeDtypeStruct((nq, width), BF)),
@@ -236,12 +275,12 @@
     owner = (step[0] % (srcs * 2)) == slab_index
     place = jnp.stack([owner.astype(jnp.int32), core, z]).astype(jnp.int32)
     updated = pl.pallas_call(
-        lambda *refs: place_kernel(at, *refs),
+        place_kernel,
         out_shape=jax.ShapeDtypeStruct(queue.shape, BF),
         in_specs=[SMEM, VMEM, VMEM, VMEM],
         out_specs=VMEM,
         compiler_params=pltpu.CompilerParams(vmem_limit_bytes=12 * MIB),
-    )(place, back, twin, queue)
+    )(place, mine, twin, queue)
     return losses, grad, updated
 
 

time: 73.1 us -> 78.7 us (1.077)
  starting transfers between devices: 18.3 us -> 31.4 us
  blocking collectives: 31.1 us -> 18.4 us
  waiting for transfers between devices: 9.13 us -> 12 us
  Pallas kernels: 9.95 us -> 11.5 us
    all_to_all x1, blocking collectives: 31.1 us -> 18.4 us  [local(): lax.all_to_all(pl.pallas_call(lambda *refs: copies_kernel(srcs, *refs), o...]
    all_to_all x0 -> x1, waiting for transfers between devices: none -> 10.6 us  [local(): back = lax.all_to_all(out, ('x', 'y'), 0, 0)]
    all_to_all x1, waiting for transfers between devices: 9.13 us -> 0.01 us  [local(): got = lax.all_to_all(message, ('x', 'y'), 0, 0)]
    all_to_all x0 -> x1, starting transfers between devices: none -> 6.87 us  [local(): back = lax.all_to_all(out, ('x', 'y'), 0, 0)]
    all_to_all x1, starting transfers between devices: 3.55 us -> 7.72 us  [local(): got = lax.all_to_all(message, ('x', 'y'), 0, 0)]
    ppermute x2 -> x5, starting transfers between devices: 14.1 us -> 16.1 us  [the longest x4 11 us: local(): lax.ppermute(slab_keys[i * cut:(i + 1) * cut], 'c', swap)]
    ppermute x2 -> x5, waiting for transfers between devices: 0.01 us -> 1.41 us  [the longest x4 1.41 us: local(): lax.ppermute(slab_keys[i * cut:(i + 1) * cut], 'c', swap)]
    pad x2 -> x0, local copies, waits for them, and re-layouts: 1.35 us -> none  [the longest x1 0.69 us: local(): jnp.pad(new_keys, ((0, ROWS - nq - nk), (0, 0)))]
  transfers between devices with their start and end apart: 4 -> 8, of which waited for: 1 -> 2; matrix products, arithmetic and copies ran while one was open for 3% -> 2% of each run, Pallas kernels for 11% -> 1%
where the time goes in v3:
time: 78.7 us; the launch traced here: 78 us
  starting transfers between devices  31.4 us (40%)
  blocking collectives  18.4 us (23%)
  waiting for transfers between devices  12 us (15%)
  Pallas kernels  11.5 us (15%)
  local copies, waits for them, and re-layouts  3.11 us (4%)
  between operations  1.44 us (2%)
    all_to_all x1, blocking collectives, local(): lax.all_to_all(pl.pallas_call(lambda *refs: copies_kernel(srcs, *refs), o...  18.4 us
    ppermute x4, starting transfers between devices, local(): lax.ppermute(slab_keys[i * cut:(i + 1) * cut], 'c', swap)  11 us
    all_to_all x1, waiting for transfers between devices, local(): back = lax.all_to_all(out, ('x', 'y'), 0, 0)  10.6 us
    all_to_all x1, starting transfers between devices, local(): got = lax.all_to_all(message, ('x', 'y'), 0, 0)  7.72 us
    pallas_call x1, Pallas kernels, local(): pl.pallas_call(lambda *refs: partial_kernel(scale, srcs, nq, *refs), out_...  7.34 us
    all_to_all x1, starting transfers between devices, local(): back = lax.all_to_all(out, ('x', 'y'), 0, 0)  6.87 us
    ppermute x1, starting transfers between devices, local(): twin = lax.ppermute(mine, 'c', swap)  5.13 us
    unnamed x6, local copies, waits for them, and re-layouts  1.83 us
  transfers between devices with their start and end apart: 8, of which 2 were waited for; matrix products, arithmetic and copies ran while one was open for 2% of the time, Pallas kernels for 1%

profile of v3, /device:TPU:1, one launch (start us, length us, event | category | flops | bytes accessed | tf_op | source)
XLA Modules:
  0.0 78.0 jit_solution(11396189899504164224)
XLA Ops:
  0.6 1.5 %shard_map.76.after_ref = bf16[16,48,256]{2,1,0:T(8,128)(2,1)} custom-call(bf16[32,256]{1,0:T(8,128)(2,1)} %refs_1_.1, s32[1,32]{1,0:T(1,128)} %bitcast.12, bf16[4,256]{1,0:T(4,128)(2,1)} %refs_2_.2), custom_call_target="tpu_custom_call" | custom-call | tf_op jit(solution)/shard_map/pallas_call | solution.py:204
  2.1 7.7 %all-to-all-start = ((bf16[16,48,256]{2,1,0:T(8,128)(2,1)}), bf16[16,48,256]{2,1,0:T(8,128)(2,1)S(1)}, u32[]{:S(2)}, u32[]{:S(2)}) async-start(bf16[16,48,256]{2,1,0:T(8,128)(2,1)} %shard_map.76.after_ref), calls=%async_computation | async-start | bytes 786432 | tf_op jit(solution)/shard_map/all_to_all | solution.py:212
  9.9 0.0 copy-start
  9.9 1.2 %copy-done = bf16[2048,256]{1,0:T(8,128)(2,1)S(1)} copy-done((bf16[2048,256]{1,0:T(8,128)(2,1)S(1)}, bf16[2048,256]{1,0:T(8,128)(2,1)}, u32[]{:S(2)}) %copy-start) | copy-done | bytes 1048600
  11.1 0.8 fusion
  11.9 4.7 %collective-permute-start.3 = (bf16[512,256]{1,0:T(8,128)(2,1)}, bf16[512,256]{1,0:T(8,128)(2,1)S(1)}, u32[]{:S(2)}, u32[]{:S(2)}) collective-permute-start(bf16[512,256]{1,0:T(8,128)(2,1)} %get-tuple-element.11), channel_id=1, source_target_pairs={{0,16},{16,0},{1,17},{17,1},{2,18},{18,2},{3,19},{19,3},{4,20},{20... | collective-permute-start | bytes 786440 | tf_op jit(solution)/shard_map/ppermute | solution.py:223
  16.6 1.9 %collective-permute-start.2 = (bf16[512,256]{1,0:T(8,128)(2,1)S(1)}, bf16[512,256]{1,0:T(8,128)(2,1)S(1)}, u32[]{:S(2)}, u32[]{:S(2)}) collective-permute-start(bf16[512,256]{1,0:T(8,128)(2,1)S(1)} %get-tuple-element.12), channel_id=1, source_target_pairs={{0,16},{16,0},{1,17},{17,1},{2,18},{18,2},{3,19},{19,3},{4,20},{20... | collective-permute-start | bytes 786440 | tf_op jit(solution)/shard_map/ppermute | solution.py:223
  18.6 2.4 %collective-permute-start.1 = (bf16[512,256]{1,0:T(8,128)(2,1)S(1)}, bf16[512,256]{1,0:T(8,128)(2,1)S(1)}, u32[]{:S(2)}, u32[]{:S(2)}) collective-permute-start(bf16[512,256]{1,0:T(8,128)(2,1)S(1)} %get-tuple-element.13), channel_id=1, source_target_pairs={{0,16},{16,0},{1,17},{17,1},{2,18},{18,2},{3,19},{19,3},{4,20},{20... | collective-permute-start | bytes 786440 | tf_op jit(solution)/shard_map/ppermute | solution.py:223
  21.0 1.9 %collective-permute-start = (bf16[512,256]{1,0:T(8,128)(2,1)S(1)}, bf16[512,256]{1,0:T(8,128)(2,1)S(1)}, u32[]{:S(2)}, u32[]{:S(2)}) collective-permute-start(bf16[512,256]{1,0:T(8,128)(2,1)S(1)} %get-tuple-element.14), channel_id=1, source_target_pairs={{0,16},{16,0},{1,17},{17,1},{2,18},{18,2},{3,19},{19,3},{4,20},{20... | collective-permute-start | bytes 786440 | tf_op jit(solution)/shard_map/ppermute | solution.py:223
  22.9 0.1 pad_add_fusion.refs_0_
  23.0 0.0 collective-permute-done.3.refs_6_
  23.0 1.4 %collective-permute-done.refs_3_ = bf16[512,256]{1,0:T(8,128)(2,1)S(1)} collective-permute-done((bf16[512,256]{1,0:T(8,128)(2,1)S(1)}, bf16[512,256]{1,0:T(8,128)(2,1)S(1)}, u32[]{:S(2)}, u32[]{:S(2)}) %collective-permute-start) | collective-permute-done | bytes 262176 | tf_op jit(solution)/shard_map/ppermute | solution.py:223
  24.4 7.3 %shard_map.78.refs_1_ = bf16[16,80,256]{2,1,0:T(8,128)(2,1)} custom-call(s32[2]{0:T(128)S(1)} %pad_add_fusion.refs_0_, bf16[16,48,256]{2,1,0:T(8,128)(2,1)S(1)} %all-to-all-done.refs_1_.refs_0_, bf16[2048,256]{1,0:T(8,128)(2,1)S(1)} %copy-done, bf16[512,256]{1,0:T(8,128)(2,1)S(1)} %collective-permute-done.refs_3_, ...), custom_call_target="tpu_custom_call" | custom-call | flops 3221225472 | bytes 2097152 | tf_op jit(solution)/shard_map/pallas_call | solution.py:228
  31.8 6.9 %all-to-all-start.1 = ((bf16[16,80,256]{2,1,0:T(8,128)(2,1)}), bf16[16,80,256]{2,1,0:T(8,128)(2,1)S(1)}, u32[]{:S(2)}, u32[]{:S(2)}) async-start(bf16[16,80,256]{2,1,0:T(8,128)(2,1)} %shard_map.78.refs_1_), calls=%async_computation.1 | async-start | bytes 1310720 | tf_op jit(solution)/shard_map/all_to_all | solution.py:237
  38.7 0.7 collective-permute-start.4
  39.3 10.6 %all-to-all-done.1.refs_0_.refs_1_ = bf16[16,80,256]{2,1,0:T(8,128)(2,1)S(1)} async-done(((bf16[16,80,256]{2,1,0:T(8,128)(2,1)}), bf16[16,80,256]{2,1,0:T(8,128)(2,1)S(1)}, u32[]{:S(2)}, u32[]{:S(2)}) %all-to-all-start.1) | async-done | bytes 655392 | tf_op jit(solution)/shard_map/all_to_all | solution.py:237
  50.0 18.4 %all_to_all.15.mine_ref = bf16[16,64,256]{2,1,0:T(8,128)(2,1)S(1)} all-to-all(bf16[16,64,256]{2,1,0:T(8,128)(2,1)S(1)} %shard_map.81), channel_id=1, replica_groups=mesh['x'=4,'y'=4,'c'=2,'z'=16] {'x','y'}, dimensions={0} | all-to-all | bytes 1048576 | tf_op jit(solution)/shard_map/all_to_all | solution.py:254
  68.4 5.1 %collective-permute-start.5 = (bf16[16,64,256]{2,1,0:T(8,128)(2,1)S(1)}, bf16[16,64,256]{2,1,0:T(8,128)(2,1)S(1)}, u32[]{:S(2)}, u32[]{:S(2)}) collective-permute-start(bf16[16,64,256]{2,1,0:T(8,128)(2,1)S(1)} %all_to_all.15.mine_ref), channel_id=1, source_target_pairs={{0,16},{16,0},{1,17},{17,1},{2,18},{18,2},{3,19},{19,3},{4,20},{20... | collective-permute-start | bytes 1572872 | tf_op jit(solution)/shard_map/ppermute | solution.py:264
  74.2 0.0 copy-start.2
  74.2 0.1 pad_add_fusion.1.place_ref
  74.3 0.6 copy-done.2
  74.9 1.0 %shard_map.79 = (f32[1,128]{1,0:T(1,128)S(1)}, bf16[32,256]{1,0:T(8,128)(2,1)}) custom-call(bf16[16,80,256]{2,1,0:T(8,128)(2,1)S(1)} %all-to-all-done.1.refs_0_.refs_1_, bf16[32,256]{1,0:T(8,128)(2,1)S(1)} %copy-done.2), custom_call_target="tpu_custom_call" | custom-call | tf_op jit(solution)/shard_map/pallas_call | solution.py:266
  75.9 0.5 slice_bitcast_fusion
  76.4 1.6 %shard_map.82 = bf16[2048,256]{1,0:T(8,128)(2,1)} custom-call(s32[3]{0:T(128)S(1)} %pad_add_fusion.1.place_ref, bf16[16,64,256]{2,1,0:T(8,128)(2,1)S(1)} %all_to_all.15.mine_ref, bf16[16,64,256]{2,1,0:T(8,128)(2,1)S(1)} %collective-permute-done.5.twin_ref, bf16[2048,256]{1,0:T(8,128)(2,1)S(1)} %copy-done), custom_call_target="tpu_custom_call" | custom-call | tf_op jit(solution)/shard_map/pallas_call | solution.py:277
  (10 shorter events, 0.1 us)
Async XLA Ops:
  2.1 7.7 %copy-start.1 = (bf16[16,48,256]{2,1,0:T(8,128)(2,1)S(1)}, bf16[16,48,256]{2,1,0:T(8,128)(2,1)}, u32[]{:S(2)}) copy-start(bf16[16,48,256]{2,1,0:T(8,128)(2,1)} %shard_map.76.after_ref) | copy-start | bytes 1179652
  2.1 22.3 %all-to-all-start = ((bf16[16,48,256]{2,1,0:T(8,128)(2,1)}), bf16[16,48,256]{2,1,0:T(8,128)(2,1)S(1)}, u32[]{:S(2)}, u32[]{:S(2)}) async-start(bf16[16,48,256]{2,1,0:T(8,128)(2,1)} %shard_map.76.after_ref), calls=%async_computation | async-start | bytes 786432 | tf_op jit(solution)/shard_map/all_to_all | solution.py:212
  9.9 1.2 %copy-start = (bf16[2048,256]{1,0:T(8,128)(2,1)S(1)}, bf16[2048,256]{1,0:T(8,128)(2,1)}, u32[]{:S(2)}) copy-start(bf16[2048,256]{1,0:T(8,128)(2,1)} %queue_ref.1) | copy-start | bytes 3145732
  11.9 11.1 %collective-permute-start.3 = (bf16[512,256]{1,0:T(8,128)(2,1)}, bf16[512,256]{1,0:T(8,128)(2,1)S(1)}, u32[]{:S(2)}, u32[]{:S(2)}) collective-permute-start(bf16[512,256]{1,0:T(8,128)(2,1)} %get-tuple-element.11), channel_id=1, source_target_pairs={{0,16},{16,0},{1,17},{17,1},{2,18},{18,2},{3,19},{19,3},{4,20},{20... | collective-permute-start | bytes 786440 | tf_op jit(solution)/shard_map/ppermute | solution.py:223
  16.6 6.4 %collective-permute-start.2 = (bf16[512,256]{1,0:T(8,128)(2,1)S(1)}, bf16[512,256]{1,0:T(8,128)(2,1)S(1)}, u32[]{:S(2)}, u32[]{:S(2)}) collective-permute-start(bf16[512,256]{1,0:T(8,128)(2,1)S(1)} %get-tuple-element.12), channel_id=1, source_target_pairs={{0,16},{16,0},{1,17},{17,1},{2,18},{18,2},{3,19},{19,3},{4,20},{20... | collective-permute-start | bytes 786440 | tf_op jit(solution)/shard_map/ppermute | solution.py:223
  18.6 4.4 %collective-permute-start.1 = (bf16[512,256]{1,0:T(8,128)(2,1)S(1)}, bf16[512,256]{1,0:T(8,128)(2,1)S(1)}, u32[]{:S(2)}, u32[]{:S(2)}) collective-permute-start(bf16[512,256]{1,0:T(8,128)(2,1)S(1)} %get-tuple-element.13), channel_id=1, source_target_pairs={{0,16},{16,0},{1,17},{17,1},{2,18},{18,2},{3,19},{19,3},{4,20},{20... | collective-permute-start | bytes 786440 | tf_op jit(solution)/shard_map/ppermute | solution.py:223
  21.0 3.4 %collective-permute-start = (bf16[512,256]{1,0:T(8,128)(2,1)S(1)}, bf16[512,256]{1,0:T(8,128)(2,1)S(1)}, u32[]{:S(2)}, u32[]{:S(2)}) collective-permute-start(bf16[512,256]{1,0:T(8,128)(2,1)S(1)} %get-tuple-element.14), channel_id=1, source_target_pairs={{0,16},{16,0},{1,17},{17,1},{2,18},{18,2},{3,19},{19,3},{4,20},{20... | collective-permute-start | bytes 786440 | tf_op jit(solution)/shard_map/ppermute | solution.py:223
  31.8 18.2 %all-to-all-start.1 = ((bf16[16,80,256]{2,1,0:T(8,128)(2,1)}), bf16[16,80,256]{2,1,0:T(8,128)(2,1)S(1)}, u32[]{:S(2)}, u32[]{:S(2)}) async-start(bf16[16,80,256]{2,1,0:T(8,128)(2,1)} %shard_map.78.refs_1_), calls=%async_computation.1 | async-start | bytes 1310720 | tf_op jit(solution)/shard_map/all_to_all | solution.py:237
  38.7 0.7 collective-permute-start.4
  68.4 8.1 %collective-permute-start.5 = (bf16[16,64,256]{2,1,0:T(8,128)(2,1)S(1)}, bf16[16,64,256]{2,1,0:T(8,128)(2,1)S(1)}, u32[]{:S(2)}, u32[]{:S(2)}) collective-permute-start(bf16[16,64,256]{2,1,0:T(8,128)(2,1)S(1)} %all_to_all.15.mine_ref), channel_id=1, source_target_pairs={{0,16},{16,0},{1,17},{17,1},{2,18},{18,2},{3,19},{19,3},{4,20},{20... | collective-permute-start | bytes 1572872 | tf_op jit(solution)/shard_map/ppermute | solution.py:264
  74.2 0.7 copy-start.2

commit v4 on v2

--- a/solution.py
+++ b/solution.py
@@ -14,6 +14,9 @@
 MIB = 1024 * 1024
 LOG2E = 1.4426950408889634
 VMEM = pl.BlockSpec(memory_space=pltpu.VMEM)
+ANY = pl.BlockSpec(memory_space=pl.ANY)
+LATE = pl.CostEstimate(flops=6 * 10**9, bytes_accessed=0, transcendentals=0)
+EARLY = pl.CostEstimate(flops=92 * 10**8, bytes_accessed=0, transcendentals=0)
 SMEM = pl.BlockSpec(memory_space=pltpu.SMEM)
 
 
@@ -21,11 +24,12 @@
     return lax.dot_general(a, b, (((1,), (1,)), ((), ())), preferred_element_type=F32)
 
 
-def partial_kernel(scale, srcs, nq, first_ref, msg_ref, own_ref, other_ref, out_ref, q_ref, s_ref):
+def partial_kernel(scale, srcs, nq, first_ref, msg_ref, own_ref, *refs):
+    other_ref, _, _, out_ref, q_ref, s_ref = refs
     width = own_ref.shape[1]
     slab = own_ref.shape[0]
     n = srcs * nq
-    block = 512
+    block = 256
     lane = lax.broadcasted_iota(jnp.int32, (nq, width), 1)
     row = lax.broadcasted_iota(jnp.int32, (nq, width), 0)
     parts = []
@@ -38,10 +42,11 @@
     queries = q_ref[...]
     top = None
     blocks = []
-    for half, ref in enumerate((own_ref, other_ref)):
-        for b in range(slab // block):
-            blocks.append((half, ref, b))
-    for i, (half, ref, b) in enumerate(blocks):
+    for b in range(slab // block):
+        blocks.append((first_ref[0] + b * block, own_ref, b))
+    for b in range(slab // block):
+        blocks.append((first_ref[1] + b * block, other_ref, b))
+    for i, (start, ref, b) in enumerate(blocks):
         s = rows_dot(queries, ref[b * block:(b + 1) * block, :])
         s_ref[:, i * block:(i + 1) * block] = s
         for c in range(block // 128):
@@ -52,9 +57,9 @@
     grad = jnp.zeros((n, width), F32)
     positive = jnp.zeros((n, width), F32)
     column = lax.broadcasted_iota(jnp.int32, (n, block), 1)
-    for i, (half, ref, b) in enumerate(blocks):
+    for i, (start, ref, b) in enumerate(blocks):
         s = s_ref[:, i * block:(i + 1) * block]
-        hit = column == (target - (first_ref[half] + b * block))
+        hit = column == (target - start)
         e = jnp.where(hit, 0.0, jnp.exp2((s - point) * (scale * LOG2E)))
         for c in range(block // 128):
             total += e[:, c * 128:(c + 1) * 128]
@@ -109,13 +114,13 @@
     loss_ref[...] = jnp.sum(jnp.where(lane == row, loss, 0.0), axis=0, keepdims=True)
 
 
-def message_kernel(copies, q_ref, pos_ref, tail_ref, out_ref):
-    nq = q_ref.shape[0]
-    tail = tail_ref[...].astype(F32)
-    row = lax.broadcasted_iota(jnp.int32, tail.shape, 0)
-    high = (pos_ref[...] >> 8).astype(F32)
-    low = (pos_ref[...] & 255).astype(F32)
-    tail = jnp.where(row == 4, high, jnp.where(row == 5, low, tail)).astype(BF)
+def message_kernel(copies, q_ref, pos_ref, keys_ref, out_ref, tail_ref):
+    nq, nk = q_ref.shape[0], keys_ref.shape[0]
+    tail_ref[...] = jnp.zeros_like(tail_ref)
+    tail_ref[:nk, :] = keys_ref[...].astype(F32)
+    tail_ref[nk:nk + 1, :nq] = (pos_ref[...] >> 8).astype(F32)
+    tail_ref[nk + 1:nk + 2, :nq] = (pos_ref[...] & 255).astype(F32)
+    tail = tail_ref[...].astype(BF)
     for j in range(copies):
         out_ref[j, :nq, :] = q_ref[...]
         out_ref[j, nq:, :] = tail
@@ -126,6 +131,21 @@
     keys = keys_ref[...]
     for j in range(copies):
         out_ref[j, at:at + keys.shape[0], :] = keys
+
+
+def gate_kernel(after_ref, out_ref):
+    del after_ref
+    out_ref[...] = jnp.zeros_like(out_ref)
+
+
+def plane_keys_kernel(nq, got_ref, out_ref):
+    width = out_ref.shape[1]
+    row = lax.broadcasted_iota(jnp.int32, (8, width), 0)
+    for a in range(got_ref.shape[0] // 4):
+        t = [got_ref[4 * a + k, nq:, :].astype(F32)[:8] for k in range(4)]
+        up = jnp.where(row < 4, t[0], pltpu.roll(t[1], 4, 0))
+        down = jnp.where(row < 4, t[2], pltpu.roll(t[3], 4, 0))
+        out_ref[16 * a:16 * a + 16, :] = jnp.concatenate([up, down], axis=0).astype(BF)
 
 
 def place_kernel(at, place_ref, mine_ref, twin_ref, queue_ref, out_ref):
@@ -179,24 +199,40 @@
     slab_index = chip * 2 + core
     swap = [(0, 1), (1, 0)]
 
-    other = lax.ppermute(queue, "c", swap)
-
     message = pl.pallas_call(
         lambda *refs: message_kernel(srcs, *refs),
         out_shape=jax.ShapeDtypeStruct((srcs, ROWS, width), BF),
         in_specs=[VMEM] * 3,
         out_specs=VMEM,
+        scratch_shapes=[pltpu.VMEM((ROWS - nq, width), F32)],
+        compiler_params=pltpu.CompilerParams(vmem_limit_bytes=56 * MIB),
+    )(queries, positions[None], new_keys)
+    got = lax.all_to_all(message, ("x", "y"), 0, 0)
+    gate = pl.pallas_call(
+        gate_kernel,
+        out_shape=jax.ShapeDtypeStruct((8, 128), F32),
+        in_specs=[ANY],
+        out_specs=VMEM,
+        compiler_params=pltpu.CompilerParams(vmem_limit_bytes=MIB),
+        cost_estimate=LATE,
+    )(message)
+    slab_keys, gate = lax.optimization_barrier((queue, gate))
+    other = lax.ppermute(slab_keys, "c", swap)
+
+    plane_keys = pl.pallas_call(
+        lambda *refs: plane_keys_kernel(nq, *refs),
+        out_shape=jax.ShapeDtypeStruct((srcs * nk, width), BF),
+        in_specs=[VMEM],
+        out_specs=VMEM,
         compiler_params=pltpu.CompilerParams(vmem_limit_bytes=4 * MIB),
-    )(queries, jnp.pad(positions, (0, width - nq))[None], jnp.pad(new_keys, ((0, ROWS - nq - nk), (0, 0))))
-    got = lax.all_to_all(message, ("x", "y"), 0, 0)
-
+        cost_estimate=EARLY,
+    )(got)
     pairs = []
     for s in range(srcs):
         for c in range(2):
             for k in range(nz):
                 to = (k + s) % nz if c == 0 else (k - s) % nz
                 pairs.append(((s * 2 + c) * nz + k, (s * 2 + c) * nz + to))
-    plane_keys = got[:, nq:nq + nk, :].reshape(srcs * nk, width)
     moved = lax.ppermute(plane_keys, ("x", "y", "c", "z"), pairs)
 
     first = jnp.stack([slab_index * slab, (slab_index ^ 1) * slab]).astype(jnp.int32)
@@ -207,12 +243,12 @@
     out = pl.pallas_call(
         lambda *refs: partial_kernel(scale, srcs, nq, *refs),
         out_shape=out_shape,
-        in_specs=[SMEM, VMEM, VMEM, VMEM],
+        in_specs=[SMEM, VMEM, VMEM, VMEM, ANY, ANY],
         out_specs=VMEM,
         scratch_shapes=[pltpu.VMEM((n, width), BF), pltpu.VMEM((n, 2 * slab), F32)],
         compiler_params=pltpu.CompilerParams(vmem_limit_bytes=24 * MIB),
         cost_estimate=pl.CostEstimate(flops=3 * flops, bytes_accessed=4 * slab * width, transcendentals=2 * n * slab),
-    )(first, got, queue, other)
+    )(first, got, queue, other, gate, plane_keys)
     out = pl.pallas_call(
         lambda *refs: fill_kernel(srcs, at, *refs),
         out_shape=out_shape,
@@ -222,8 +258,8 @@
         compiler_params=pltpu.CompilerParams(vmem_limit_bytes=8 * MIB),
     )(moved, out)
     back = lax.all_to_all(out, ("x", "y"), 0, 0)
-
     twin = lax.ppermute(back[:, at:, :], "c", swap)
+
     loss, grad = pl.pallas_call(
         lambda *refs: combine_kernel(scale, srcs, nq, *refs),
         out_shape=(jax.ShapeDtypeStruct((1, 128), F32), jax.ShapeDtypeStruct((nq, width), BF)),

time: 73.1 us -> 67.9 us (0.929)
  waiting for transfers between devices: 9.13 us -> 1.49 us
  blocking collectives: 31.1 us -> 32.2 us
    all_to_all x1, waiting for transfers between devices: 9.13 us -> 0.91 us  [local(): got = lax.all_to_all(message, ('x', 'y'), 0, 0)]
    ppermute x1, starting transfers between devices: 8.92 us -> 4.74 us  [local(): other = lax.ppermute(slab_keys, 'c', swap)]
    all_to_all x1, starting transfers between devices: 3.55 us -> 7.58 us  [local(): got = lax.all_to_all(message, ('x', 'y'), 0, 0)]
    unnamed x6, local copies, waits for them, and re-layouts: 0.73 us -> 2.25 us
    pad x2 -> x0, local copies, waits for them, and re-layouts: 1.35 us -> none  [the longest x1 0.69 us: local(): jnp.pad(new_keys, ((0, ROWS - nq - nk), (0, 0)))]
    all_to_all x1, blocking collectives: 31.1 us -> 32.2 us  [local(): back = lax.all_to_all(out, ('x', 'y'), 0, 0)]
    ppermute x1, starting transfers between devices: 5.15 us -> 6 us  [local(): twin = lax.ppermute(back[:, at:, :], 'c', swap)]
    pallas_call x1, Pallas kernels: 0.77 us -> 1.52 us  [local(): pl.pallas_call(lambda *refs: message_kernel(srcs, *refs), out_shape=jax.S...]
  transfers between devices with their start and end apart: 4 -> 4, of which waited for: 1 -> 2; matrix products, arithmetic and copies ran while one was open for 3% -> 1% of each run, Pallas kernels for 11% -> 11%
where the time goes in v4:
time: 67.9 us; the launch traced here: 67.4 us
  blocking collectives  32.2 us (47%)
  starting transfers between devices  19 us (28%)
  Pallas kernels  10.4 us (15%)
  local copies, waits for them, and re-layouts  2.81 us (4%)
  waiting for transfers between devices  1.49 us (2%)
  between operations  1.4 us (2%)
    all_to_all x1, blocking collectives, local(): back = lax.all_to_all(out, ('x', 'y'), 0, 0)  32.2 us
    all_to_all x1, starting transfers between devices, local(): got = lax.all_to_all(message, ('x', 'y'), 0, 0)  7.58 us
    pallas_call x1, Pallas kernels, local(): pl.pallas_call(lambda *refs: partial_kernel(scale, srcs, nq, *refs), out_...  6.17 us
    ppermute x1, starting transfers between devices, local(): twin = lax.ppermute(back[:, at:, :], 'c', swap)  6 us
    ppermute x1, starting transfers between devices, local(): other = lax.ppermute(slab_keys, 'c', swap)  4.74 us
    unnamed x6, local copies, waits for them, and re-layouts  2.25 us
    pallas_call x1, Pallas kernels, local(): pl.pallas_call(lambda *refs: place_kernel(at, *refs), out_shape=jax.Shape...  1.59 us
    pallas_call x1, Pallas kernels, local(): pl.pallas_call(lambda *refs: message_kernel(srcs, *refs), out_shape=jax.S...  1.52 us
  transfers between devices with their start and end apart: 4, of which 2 were waited for; matrix products, arithmetic and copies ran while one was open for 1% of the time, Pallas kernels for 11%

profile of v4, /device:TPU:1, one launch (start us, length us, event | category | flops | bytes accessed | tf_op | source)
XLA Modules:
  0.0 67.4 jit_solution(8864138433749986048)
XLA Ops:
  0.6 1.5 %shard_map.76.after_ref = bf16[16,48,256]{2,1,0:T(8,128)(2,1)} custom-call(bf16[32,256]{1,0:T(8,128)(2,1)} %refs_1_.1, s32[1,32]{1,0:T(1,128)} %bitcast.12, bf16[4,256]{1,0:T(4,128)(2,1)} %refs_2_.2), custom_call_target="tpu_custom_call" | custom-call | tf_op jit(solution)/shard_map/pallas_call | solution.py:202
  2.1 7.6 %all-to-all-start = ((bf16[16,48,256]{2,1,0:T(8,128)(2,1)}), bf16[16,48,256]{2,1,0:T(8,128)(2,1)S(1)}, u32[]{:S(2)}, u32[]{:S(2)}) async-start(bf16[16,48,256]{2,1,0:T(8,128)(2,1)} %shard_map.76.after_ref), calls=%async_computation | async-start | bytes 786432 | tf_op jit(solution)/shard_map/all_to_all | solution.py:210
  9.7 0.0 copy-start
  9.8 1.0 %copy-done = bf16[16,48,256]{2,1,0:T(8,128)(2,1)S(1)} copy-done((bf16[16,48,256]{2,1,0:T(8,128)(2,1)S(1)}, bf16[16,48,256]{2,1,0:T(8,128)(2,1)}, u32[]{:S(2)}) %copy-start) | copy-done | bytes 393240
  10.8 0.0 copy-start.1
  10.8 1.2 %copy-done.1 = bf16[2048,256]{1,0:T(8,128)(2,1)S(1)} copy-done((bf16[2048,256]{1,0:T(8,128)(2,1)S(1)}, bf16[2048,256]{1,0:T(8,128)(2,1)}, u32[]{:S(2)}) %copy-start.1) | copy-done | bytes 1048600
  12.0 4.7 %collective-permute-start.1 = (bf16[2048,256]{1,0:T(8,128)(2,1)S(1)}, bf16[2048,256]{1,0:T(8,128)(2,1)S(1)}, u32[]{:S(2)}, u32[]{:S(2)}) collective-permute-start(bf16[2048,256]{1,0:T(8,128)(2,1)S(1)} %copy-done.1), channel_id=1, source_target_pairs={{0,16},{16,0},{1,17},{17,1},{2,18},{18,2},{3,19},{19,3},{4,20},{20... | collective-permute-start | bytes 3145736 | tf_op jit(solution)/shard_map/ppermute | solution.py:220
  16.8 0.1 pad_add_fusion.refs_0_
  16.8 0.9 %all-to-all-done.refs_0_.refs_1_ = bf16[16,48,256]{2,1,0:T(8,128)(2,1)S(1)} async-done(((bf16[16,48,256]{2,1,0:T(8,128)(2,1)}), bf16[16,48,256]{2,1,0:T(8,128)(2,1)S(1)}, u32[]{:S(2)}, u32[]{:S(2)}) %all-to-all-start) | async-done | bytes 393248 | tf_op jit(solution)/shard_map/all_to_all | solution.py:210
  17.8 0.7 collective-permute-start
  18.4 0.6 collective-permute-done.1.refs_3_
  19.0 6.2 %shard_map.79.refs_1_ = bf16[16,144,256]{2,1,0:T(8,128)(2,1)S(1)} custom-call(s32[2]{0:T(128)S(1)} %pad_add_fusion.refs_0_, bf16[16,48,256]{2,1,0:T(8,128)(2,1)S(1)} %all-to-all-done.refs_0_.refs_1_, bf16[2048,256]{1,0:T(8,128)(2,1)S(1)} %copy-done.1, bf16[2048,256]{1,0:T(8,128)(2,1)S(1)} %collective-permute-done.1.refs_3_, f32[8,128]{1,0:T(8,128)S(1)} %shard_map.78.refs_4_, ...), custom_call_target="tpu_custom_call" | custom-call | flops 3221225472 | bytes 2097152 | tf_op jit(solution)/shard_map/pallas_call | solution.py:243
  25.2 0.0 collective-permute-done.refs_0_
  25.2 0.0 copy-start.2
  25.3 32.2 %all_to_all.10.refs_0_.refs_1_ = bf16[16,144,256]{2,1,0:T(8,128)(2,1)S(1)} all-to-all(bf16[16,144,256]{2,1,0:T(8,128)(2,1)S(1)} %shard_map.80), channel_id=1, replica_groups=mesh['x'=4,'y'=4,'c'=2,'z'=16] {'x','y'}, dimensions={0} | all-to-all | bytes 2359296 | tf_op jit(solution)/shard_map/all_to_all | solution.py:260
  57.5 6.0 %collective-permute-start.2 = (bf16[16,64,256]{2,1,0:T(8,128)(2,1)S(1)}, bf16[16,64,256]{2,1,0:T(8,128)(2,1)S(1)}, u32[]{:S(2)}, u32[]{:S(2)}) collective-permute-start(bf16[16,64,256]{2,1,0:T(8,128)(2,1)S(1)} %slice.8), channel_id=1, source_target_pairs={{0,16},{16,0},{1,17},{17,1},{2,18},{18,2},{3,19},{19,3},{4,20},{20... | collective-permute-start | bytes 1572872 | tf_op jit(solution)/shard_map/ppermute | solution.py:261
  64.1 0.1 pad_add_fusion.1.refs_0_
  64.2 0.0 copy-done.2
  64.2 1.0 %shard_map.81 = (f32[1,128]{1,0:T(1,128)S(1)}, bf16[32,256]{1,0:T(8,128)(2,1)}) custom-call(bf16[16,144,256]{2,1,0:T(8,128)(2,1)S(1)} %all_to_all.10.refs_0_.refs_1_, bf16[32,256]{1,0:T(8,128)(2,1)S(1)} %copy-done.2), custom_call_target="tpu_custom_call" | custom-call | tf_op jit(solution)/shard_map/pallas_call | solution.py:263
  65.3 0.5 slice_bitcast_fusion
  65.8 0.0 collective-permute-done.2.refs_2_
  65.8 1.6 %shard_map.82 = bf16[2048,256]{1,0:T(8,128)(2,1)} custom-call(s32[3]{0:T(128)S(1)} %pad_add_fusion.1.refs_0_, bf16[16,144,256]{2,1,0:T(8,128)(2,1)S(1)} %all_to_all.10.refs_0_.refs_1_, bf16[16,64,256]{2,1,0:T(8,128)(2,1)S(1)} %collective-permute-done.2.refs_2_, bf16[2048,256]{1,0:T(8,128)(2,1)S(1)} %copy-done.1), custom_call_target="tpu_custom_call" | custom-call | tf_op jit(solution)/shard_map/pallas_call | solution.py:274
  (4 shorter events, 0.1 us)
Async XLA Ops:
  2.1 15.6 %all-to-all-start = ((bf16[16,48,256]{2,1,0:T(8,128)(2,1)}), bf16[16,48,256]{2,1,0:T(8,128)(2,1)S(1)}, u32[]{:S(2)}, u32[]{:S(2)}) async-start(bf16[16,48,256]{2,1,0:T(8,128)(2,1)} %shard_map.76.after_ref), calls=%async_computation | async-start | bytes 786432 | tf_op jit(solution)/shard_map/all_to_all | solution.py:210
  9.7 1.0 %copy-start = (bf16[16,48,256]{2,1,0:T(8,128)(2,1)S(1)}, bf16[16,48,256]{2,1,0:T(8,128)(2,1)}, u32[]{:S(2)}) copy-start(bf16[16,48,256]{2,1,0:T(8,128)(2,1)} %shard_map.76.after_ref) | copy-start | bytes 1179652
  10.8 1.2 %copy-start.1 = (bf16[2048,256]{1,0:T(8,128)(2,1)S(1)}, bf16[2048,256]{1,0:T(8,128)(2,1)}, u32[]{:S(2)}) copy-start(bf16[2048,256]{1,0:T(8,128)(2,1)} %refs_3_.1) | copy-start | bytes 3145732
  12.0 7.0 %collective-permute-start.1 = (bf16[2048,256]{1,0:T(8,128)(2,1)S(1)}, bf16[2048,256]{1,0:T(8,128)(2,1)S(1)}, u32[]{:S(2)}, u32[]{:S(2)}) collective-permute-start(bf16[2048,256]{1,0:T(8,128)(2,1)S(1)} %copy-done.1), channel_id=1, source_target_pairs={{0,16},{16,0},{1,17},{17,1},{2,18},{18,2},{3,19},{19,3},{4,20},{20... | collective-permute-start | bytes 3145736 | tf_op jit(solution)/shard_map/ppermute | solution.py:220
  17.8 7.4 %collective-permute-start = (bf16[64,256]{1,0:T(8,128)(2,1)S(1)}, bf16[64,256]{1,0:T(8,128)(2,1)S(1)}, u32[]{:S(2)}, u32[]{:S(2)}) collective-permute-start(bf16[64,256]{1,0:T(8,128)(2,1)S(1)} %shard_map.77.refs_5_), channel_id=1, source_target_pairs={{0,0},{1,1},{2,2},{3,3},{4,4},{5,5},{6,6},{7,7},{8,8},{9,9},{10,10... | collective-permute-start | bytes 98312 | tf_op jit(solution)/shard_map/ppermute | solution.py:236
  25.2 39.0 %copy-start.2 = (bf16[32,256]{1,0:T(8,128)(2,1)S(1)}, bf16[32,256]{1,0:T(8,128)(2,1)}, u32[]{:S(2)}) copy-start(bf16[32,256]{1,0:T(8,128)(2,1)} %refs_1_.1) | copy-start | bytes 49156
  57.5 8.3 %collective-permute-start.2 = (bf16[16,64,256]{2,1,0:T(8,128)(2,1)S(1)}, bf16[16,64,256]{2,1,0:T(8,128)(2,1)S(1)}, u32[]{:S(2)}, u32[]{:S(2)}) collective-permute-start(bf16[16,64,256]{2,1,0:T(8,128)(2,1)S(1)} %slice.8), channel_id=1, source_target_pairs={{0,16},{16,0},{1,17},{17,1},{2,18},{18,2},{3,19},{19,3},{4,20},{20... | collective-permute-start | bytes 1572872 | tf_op jit(solution)/shard_map/ppermute | solution.py:261

commit v5 on v4

--- a/solution.py
+++ b/solution.py
@@ -10,7 +10,7 @@
 
 BF = jnp.bfloat16
 F32 = jnp.float32
-ROWS = 48
+ROWS = 40
 MIB = 1024 * 1024
 LOG2E = 1.4426950408889634
 VMEM = pl.BlockSpec(memory_space=pltpu.VMEM)
@@ -24,8 +24,8 @@
     return lax.dot_general(a, b, (((1,), (1,)), ((), ())), preferred_element_type=F32)
 
 
-def partial_kernel(scale, srcs, nq, first_ref, msg_ref, own_ref, *refs):
-    other_ref, _, _, out_ref, q_ref, s_ref = refs
+def partial_kernel(scale, srcs, nq, info_ref, msg_ref, own_ref, *refs):
+    other_ref, _, out_ref, q_ref, s_ref = refs
     width = own_ref.shape[1]
     slab = own_ref.shape[0]
     n = srcs * nq
@@ -43,9 +43,9 @@
     top = None
     blocks = []
     for b in range(slab // block):
-        blocks.append((first_ref[0] + b * block, own_ref, b))
+        blocks.append((info_ref[0] + b * block, own_ref, b))
     for b in range(slab // block):
-        blocks.append((first_ref[1] + b * block, other_ref, b))
+        blocks.append((info_ref[1] + b * block, other_ref, b))
     for i, (start, ref, b) in enumerate(blocks):
         s = rows_dot(queries, ref[b * block:(b + 1) * block, :])
         s_ref[:, i * block:(i + 1) * block] = s
@@ -70,30 +70,36 @@
     t0 = total.astype(BF).astype(F32)
     t1 = (total - t0).astype(BF).astype(F32)
     t2 = total - t0 - t1
-    place = lax.broadcasted_iota(jnp.int32, (n, 128), 1)
-    stats = jnp.where(place == 0, point, jnp.where(place == 1, t0, jnp.where(place == 2, t1, jnp.where(place == 3, t2, 0.0))))
-    stats = stats.astype(BF)
+    stats = (point, t0, t1, t2)
     grad = grad.astype(BF)
     positive = positive.astype(BF)
     for j in range(srcs):
         at = slice(j * nq, (j + 1) * nq)
         out_ref[j, :nq, :] = grad[at]
         out_ref[j, nq:2 * nq, :] = positive[at]
-        half = nq // 2
-        out_ref[j, 2 * nq:2 * nq + half, :128] = stats[j * nq:j * nq + half]
-        out_ref[j, 2 * nq:2 * nq + half, 128:] = stats[j * nq + half:(j + 1) * nq]
+    lane = lax.broadcasted_iota(jnp.int32, (nq, width), 1)
+    row = lax.broadcasted_iota(jnp.int32, (nq, width), 0)
+    for j in range(srcs):
+        at = slice(j * nq, (j + 1) * nq)
+        line = jnp.zeros((nq, width), F32)
+        for k, value in enumerate(stats):
+            line = jnp.where(lane == row + k * nq, value[at], line)
+        line = jnp.sum(line, axis=0, keepdims=True)
+        out_ref[j, out_ref.shape[1] - 8:, :] = jnp.broadcast_to(line, (8, width)).astype(BF)
 
 
 def combine_kernel(scale, srcs, nq, got_ref, q_ref, loss_ref, grad_ref):
     width = q_ref.shape[1]
+    lane = lax.broadcasted_iota(jnp.int32, (nq, 128), 1)
+    row = lax.broadcasted_iota(jnp.int32, (nq, 128), 0)
     positive = jnp.zeros((nq, width), F32)
     points, totals = [], []
     for j in range(srcs):
         positive += got_ref[j, nq:2 * nq, :].astype(F32)
-        st = got_ref[j, 2 * nq:2 * nq + nq // 2, :].astype(F32)
-        st = jnp.concatenate([st[:, :128], st[:, 128:]], axis=0)
-        points.append(st[:, 0:1])
-        totals.append(st[:, 1:2] + st[:, 2:3] + st[:, 3:4])
+        st = jnp.broadcast_to(got_ref[j, got_ref.shape[1] - 8:, :].astype(F32)[:1, :128], (nq, 128))
+        points.append(jnp.sum(jnp.where(lane == row, st, 0.0), axis=1, keepdims=True))
+        three = (lane >= nq) & (lane % nq == row)
+        totals.append(jnp.sum(jnp.where(three, st, 0.0), axis=1, keepdims=True))
     s_pos = jnp.sum(q_ref[...].astype(F32) * positive, axis=1, keepdims=True)
     top = s_pos
     for p in points:
@@ -109,9 +115,7 @@
     weight = (jnp.exp(s_pos * scale - lse) - 1.0).astype(BF).astype(F32)
     grad_ref[...] = ((grad / total + weight * positive) * scale).astype(BF)
     loss = lse - s_pos * scale
-    lane = lax.broadcasted_iota(jnp.int32, (nq, 128), 1)
-    row = lax.broadcasted_iota(jnp.int32, (nq, 128), 0)
-    loss_ref[...] = jnp.sum(jnp.where(lane == row, loss, 0.0), axis=0, keepdims=True)
+    loss_ref[...] = jnp.sum(jnp.where(lane == row, loss, 0.0), axis=0, keepdims=True)[:, :nq]
 
 
 def message_kernel(copies, q_ref, pos_ref, keys_ref, out_ref, tail_ref):
@@ -133,9 +137,11 @@
         out_ref[j, at:at + keys.shape[0], :] = keys
 
 
-def gate_kernel(after_ref, out_ref):
+def slab_kernel(after_ref, queue_ref, out_ref, sem):
     del after_ref
-    out_ref[...] = jnp.zeros_like(out_ref)
+    copy = pltpu.make_async_copy(queue_ref, out_ref, sem)
+    copy.start()
+    copy.wait()
 
 
 def plane_keys_kernel(nq, got_ref, out_ref):
@@ -148,14 +154,11 @@
         out_ref[16 * a:16 * a + 16, :] = jnp.concatenate([up, down], axis=0).astype(BF)
 
 
-def place_kernel(at, place_ref, mine_ref, twin_ref, queue_ref, out_ref):
-    owner, core, z = place_ref[0], place_ref[1], place_ref[2]
+def place_kernel(at, info_ref, mine_ref, twin_ref, queue_ref, out_ref, new_ref, sem):
+    del queue_ref
+    owner, core, z = info_ref[2], info_ref[3], info_ref[4]
     cols, rows = twin_ref.shape[0], twin_ref.shape[1]
-    width = queue_ref.shape[1]
-
-    @pl.when(owner == 0)
-    def _():
-        out_ref[...] = queue_ref[...]
+    width = twin_ref.shape[2]
 
     def put(ref, base, c):
         row = lax.broadcasted_iota(jnp.int32, (8, width), 0)
@@ -177,13 +180,19 @@
                         down = jnp.where(row < 4, pltpu.roll(t[2], 4, 0), t[3])
                     chip = 4 * a + v
                     start = (chip * 2 + c) * 64 + 16 * b
-                    out_ref[start:start + 16, :] = jnp.concatenate([up, down], axis=0).astype(BF)
+                    new_ref[start:start + 16, :] = jnp.concatenate([up, down], axis=0).astype(BF)
 
     for mine in (0, 1):
         @pl.when((owner == 1) & (core == mine))
         def _():
             put(mine_ref, at, mine)
             put(twin_ref, 0, 1 - mine)
+
+    @pl.when(owner == 1)
+    def _():
+        copy = pltpu.make_async_copy(new_ref, out_ref, sem)
+        copy.start()
+        copy.wait()
 
 
 def local(queries, positions, queue, new_keys, step):
@@ -208,15 +217,16 @@
         compiler_params=pltpu.CompilerParams(vmem_limit_bytes=56 * MIB),
     )(queries, positions[None], new_keys)
     got = lax.all_to_all(message, ("x", "y"), 0, 0)
-    gate = pl.pallas_call(
-        gate_kernel,
-        out_shape=jax.ShapeDtypeStruct((8, 128), F32),
-        in_specs=[ANY],
-        out_specs=VMEM,
-        compiler_params=pltpu.CompilerParams(vmem_limit_bytes=MIB),
+    kept = pl.pallas_call(
+        slab_kernel,
+        out_shape=jax.ShapeDtypeStruct(queue.shape, BF),
+        in_specs=[ANY, ANY],
+        out_specs=ANY,
+        scratch_shapes=[pltpu.SemaphoreType.DMA],
+        compiler_params=pltpu.CompilerParams(vmem_limit_bytes=56 * MIB),
         cost_estimate=LATE,
-    )(message)
-    slab_keys, gate = lax.optimization_barrier((queue, gate))
+    )(message, queue)
+    slab_keys, kept = lax.optimization_barrier((queue, kept))
     other = lax.ppermute(slab_keys, "c", swap)
 
     plane_keys = pl.pallas_call(
@@ -235,20 +245,21 @@
                 pairs.append(((s * 2 + c) * nz + k, (s * 2 + c) * nz + to))
     moved = lax.ppermute(plane_keys, ("x", "y", "c", "z"), pairs)
 
-    first = jnp.stack([slab_index * slab, (slab_index ^ 1) * slab]).astype(jnp.int32)
+    owner = (step[0] % (srcs * 2)) == slab_index
+    info = jnp.stack([slab_index * slab, (slab_index ^ 1) * slab, owner.astype(jnp.int32), core, z]).astype(jnp.int32)
     n = srcs * nq
-    at = 2 * nq + nq // 2
+    at = 2 * nq
     flops = 2 * n * 2 * slab * width
-    out_shape = jax.ShapeDtypeStruct((srcs, at + srcs * nk, width), BF)
+    out_shape = jax.ShapeDtypeStruct((srcs, at + srcs * nk + 8, width), BF)
     out = pl.pallas_call(
         lambda *refs: partial_kernel(scale, srcs, nq, *refs),
         out_shape=out_shape,
-        in_specs=[SMEM, VMEM, VMEM, VMEM, ANY, ANY],
+        in_specs=[SMEM, VMEM, VMEM, VMEM, ANY],
         out_specs=VMEM,
         scratch_shapes=[pltpu.VMEM((n, width), BF), pltpu.VMEM((n, 2 * slab), F32)],
         compiler_params=pltpu.CompilerParams(vmem_limit_bytes=24 * MIB),
         cost_estimate=pl.CostEstimate(flops=3 * flops, bytes_accessed=4 * slab * width, transcendentals=2 * n * slab),
-    )(first, got, queue, other, gate, plane_keys)
+    )(info, got, queue, other, plane_keys)
     out = pl.pallas_call(
         lambda *refs: fill_kernel(srcs, at, *refs),
         out_shape=out_shape,
@@ -258,26 +269,26 @@
         compiler_params=pltpu.CompilerParams(vmem_limit_bytes=8 * MIB),
     )(moved, out)
     back = lax.all_to_all(out, ("x", "y"), 0, 0)
-    twin = lax.ppermute(back[:, at:, :], "c", swap)
+    twin = lax.ppermute(back[:, at:at + srcs * nk, :], "c", swap)
 
     loss, grad = pl.pallas_call(
         lambda *refs: combine_kernel(scale, srcs, nq, *refs),
-        out_shape=(jax.ShapeDtypeStruct((1, 128), F32), jax.ShapeDtypeStruct((nq, width), BF)),
+        out_shape=(jax.ShapeDtypeStruct((1, nq), F32), jax.ShapeDtypeStruct((nq, width), BF)),
         in_specs=[VMEM, VMEM],
         out_specs=(VMEM, VMEM),
         compiler_params=pltpu.CompilerParams(vmem_limit_bytes=8 * MIB),
     )(back, queries)
-    losses = loss[0, :nq]
-
-    owner = (step[0] % (srcs * 2)) == slab_index
-    place = jnp.stack([owner.astype(jnp.int32), core, z]).astype(jnp.int32)
+    losses = loss.reshape(nq)
+
     updated = pl.pallas_call(
         lambda *refs: place_kernel(at, *refs),
         out_shape=jax.ShapeDtypeStruct(queue.shape, BF),
-        in_specs=[SMEM, VMEM, VMEM, VMEM],
-        out_specs=VMEM,
+        in_specs=[SMEM, VMEM, VMEM, ANY],
+        out_specs=ANY,
+        scratch_shapes=[pltpu.VMEM(queue.shape, BF), pltpu.SemaphoreType.DMA],
+        input_output_aliases={3: 0},
         compiler_params=pltpu.CompilerParams(vmem_limit_bytes=12 * MIB),
-    )(place, back, twin, queue)
+    )(info, back, twin, kept)
     return losses, grad, updated
 
 

time: 67.9 us -> 95.6 us (1.41)
  Pallas kernels: 10.4 us -> 42 us
  local copies, waits for them, and re-layouts: 2.81 us -> 0.14 us
  starting transfers between devices: 19 us -> 18 us
    pallas_call x1, Pallas kernels: 0.01 us -> 32.9 us  [local(): pl.pallas_call(slab_kernel, out_shape=jax.ShapeDtypeStruct(queue.shape, B...]
    unnamed x6 -> x4, local copies, waits for them, and re-layouts: 2.25 us -> 0.01 us
    ppermute x1, starting transfers between devices: 6 us -> 4.97 us  [local(): twin = lax.ppermute(back[:, at:at + srcs * nk, :], 'c', swap)]
    pallas_call x1, Pallas kernels: 1.59 us -> 0.57 us  [local(): pl.pallas_call(lambda *refs: place_kernel(at, *refs), out_shape=jax.Shape...]
  transfers between devices with their start and end apart: 4 -> 4, of which waited for: 2 -> 2; matrix products, arithmetic and copies ran while one was open for 1% -> 0% of each run, Pallas kernels for 11% -> 42%
where the time goes in v5:
time: 95.6 us; the launch traced here: 95.3 us
  Pallas kernels  42 us (44%)
  blocking collectives  32.3 us (34%)
  starting transfers between devices  18 us (19%)
  waiting for transfers between devices  1.43 us (1%)
  between operations  1.41 us (1%)
    pallas_call x1, Pallas kernels, local(): pl.pallas_call(slab_kernel, out_shape=jax.ShapeDtypeStruct(queue.shape, B...  32.9 us
    all_to_all x1, blocking collectives, local(): back = lax.all_to_all(out, ('x', 'y'), 0, 0)  32.3 us
    all_to_all x1, starting transfers between devices, local(): got = lax.all_to_all(message, ('x', 'y'), 0, 0)  7.58 us
    pallas_call x1, Pallas kernels, local(): pl.pallas_call(lambda *refs: partial_kernel(scale, srcs, nq, *refs), out_...  6.1 us
    ppermute x1, starting transfers between devices, local(): twin = lax.ppermute(back[:, at:at + srcs * nk, :], 'c', swap)  4.97 us
    ppermute x1, starting transfers between devices, local(): other = lax.ppermute(slab_keys, 'c', swap)  4.74 us
  transfers between devices with their start and end apart: 4, of which 2 were waited for; matrix products, arithmetic and copies ran while one was open for 0% of the time, Pallas kernels for 42%

profile of v5, /device:TPU:1, one launch (start us, length us, event | category | flops | bytes accessed | tf_op | source)
XLA Modules:
  0.0 95.3 jit_solution(14640627596983220373)
XLA Ops:
  0.6 1.5 %shard_map.76.after_ref = bf16[16,40,256]{2,1,0:T(8,128)(2,1)} custom-call(bf16[32,256]{1,0:T(8,128)(2,1)} %refs_1_.1, s32[1,32]{1,0:T(1,128)} %bitcast.11, bf16[4,256]{1,0:T(4,128)(2,1)} %refs_2_.2), custom_call_target="tpu_custom_call" | custom-call | tf_op jit(solution)/shard_map/pallas_call | solution.py:211
  2.1 7.6 %all-to-all-start = ((bf16[16,40,256]{2,1,0:T(8,128)(2,1)}), bf16[16,40,256]{2,1,0:T(8,128)(2,1)S(1)}, u32[]{:S(2)}, u32[]{:S(2)}) async-start(bf16[16,40,256]{2,1,0:T(8,128)(2,1)} %shard_map.76.after_ref), calls=%async_computation | async-start | bytes 655360 | tf_op jit(solution)/shard_map/all_to_all | solution.py:219
  9.7 0.0 copy-start.1
  9.7 32.9 %shard_map.78.refs_3_ = bf16[2048,256]{1,0:T(8,128)(2,1)} custom-call(bf16[16,40,256]{2,1,0:T(8,128)(2,1)} %shard_map.76.after_ref, bf16[2048,256]{1,0:T(8,128)(2,1)} %refs_2_.3), custom_call_target="tpu_custom_call" | custom-call | flops 6000000000 | tf_op jit(solution)/shard_map/pallas_call | solution.py:220
  42.6 0.0 copy-done.1
  42.6 4.7 %collective-permute-start.1 = (bf16[2048,256]{1,0:T(8,128)(2,1)S(1)}, bf16[2048,256]{1,0:T(8,128)(2,1)S(1)}, u32[]{:S(2)}, u32[]{:S(2)}) collective-permute-start(bf16[2048,256]{1,0:T(8,128)(2,1)S(1)} %copy-done.1), channel_id=1, source_target_pairs={{0,16},{16,0},{1,17},{17,1},{2,18},{18,2},{3,19},{19,3},{4,20},{20... | collective-permute-start | bytes 3145736 | tf_op jit(solution)/shard_map/ppermute | solution.py:230
  48.0 0.1 stack.27.refs_0_
  48.1 0.0 all-to-all-done.refs_0_.refs_1_
  48.2 0.7 collective-permute-start
  48.8 0.8 collective-permute-done.1.refs_3_
  49.6 6.1 %shard_map.79.refs_1_ = bf16[16,136,256]{2,1,0:T(8,128)(2,1)S(1)} custom-call(s32[5]{0:T(128)S(1)} %stack.27.refs_0_, bf16[16,40,256]{2,1,0:T(8,128)(2,1)S(1)} %all-to-all-done.refs_0_.refs_1_, bf16[2048,256]{1,0:T(8,128)(2,1)S(1)} %copy-done.1, bf16[2048,256]{1,0:T(8,128)(2,1)S(1)} %collective-permute-done.1.refs_3_, bf16[64,256]{1,0:T(8,128)(2,1)S(1)} %shard_map.77.refs_4_), custom_call_target="tpu_custom_call" | custom-call | flops 3221225472 | bytes 2097152 | tf_op jit(solution)/shard_map/pallas_call | solution.py:254
  55.7 0.0 collective-permute-done.refs_0_
  55.8 0.0 copy-start
  55.8 32.3 %all_to_all.10.refs_0_.refs_1_ = bf16[16,136,256]{2,1,0:T(8,128)(2,1)S(1)} all-to-all(bf16[16,136,256]{2,1,0:T(8,128)(2,1)S(1)} %shard_map.80), channel_id=1, replica_groups=mesh['x'=4,'y'=4,'c'=2,'z'=16] {'x','y'}, dimensions={0} | all-to-all | bytes 2228224 | tf_op jit(solution)/shard_map/all_to_all | solution.py:271
  88.2 5.0 %collective-permute-start.2 = (bf16[16,64,256]{2,1,0:T(8,128)(2,1)S(1)}, bf16[16,64,256]{2,1,0:T(8,128)(2,1)S(1)}, u32[]{:S(2)}, u32[]{:S(2)}) collective-permute-start(bf16[16,64,256]{2,1,0:T(8,128)(2,1)S(1)} %slice.4), channel_id=1, source_target_pairs={{0,16},{16,0},{1,17},{17,1},{2,18},{18,2},{3,19},{19,3},{4,20},{20... | collective-permute-start | bytes 1572872 | tf_op jit(solution)/shard_map/ppermute | solution.py:272
  93.2 0.0 copy-done
  93.2 0.9 shard_map.81
  94.1 0.6 collective-permute-done.2.refs_2_
  94.7 0.6 shard_map.82
  (3 shorter events, 0.1 us)
Async XLA Ops:
  2.1 46.0 %all-to-all-start = ((bf16[16,40,256]{2,1,0:T(8,128)(2,1)}), bf16[16,40,256]{2,1,0:T(8,128)(2,1)S(1)}, u32[]{:S(2)}, u32[]{:S(2)}) async-start(bf16[16,40,256]{2,1,0:T(8,128)(2,1)} %shard_map.76.after_ref), calls=%async_computation | async-start | bytes 655360 | tf_op jit(solution)/shard_map/all_to_all | solution.py:219
  9.7 32.9 %copy-start.1 = (bf16[2048,256]{1,0:T(8,128)(2,1)S(1)}, bf16[2048,256]{1,0:T(8,128)(2,1)}, u32[]{:S(2)}) copy-start(bf16[2048,256]{1,0:T(8,128)(2,1)} %refs_2_.3) | copy-start | bytes 3145732
  42.6 7.0 %collective-permute-start.1 = (bf16[2048,256]{1,0:T(8,128)(2,1)S(1)}, bf16[2048,256]{1,0:T(8,128)(2,1)S(1)}, u32[]{:S(2)}, u32[]{:S(2)}) collective-permute-start(bf16[2048,256]{1,0:T(8,128)(2,1)S(1)} %copy-done.1), channel_id=1, source_target_pairs={{0,16},{16,0},{1,17},{17,1},{2,18},{18,2},{3,19},{19,3},{4,20},{20... | collective-permute-start | bytes 3145736 | tf_op jit(solution)/shard_map/ppermute | solution.py:230
  48.2 7.6 %collective-permute-start = (bf16[64,256]{1,0:T(8,128)(2,1)S(1)}, bf16[64,256]{1,0:T(8,128)(2,1)S(1)}, u32[]{:S(2)}, u32[]{:S(2)}) collective-permute-start(bf16[64,256]{1,0:T(8,128)(2,1)S(1)} %shard_map.77.refs_4_), channel_id=1, source_target_pairs={{0,0},{1,1},{2,2},{3,3},{4,4},{5,5},{6,6},{7,7},{8,8},{9,9},{10,10... | collective-permute-start | bytes 98312 | tf_op jit(solution)/shard_map/ppermute | solution.py:246
  55.8 37.4 %copy-start = (bf16[32,256]{1,0:T(8,128)(2,1)S(1)}, bf16[32,256]{1,0:T(8,128)(2,1)}, u32[]{:S(2)}) copy-start(bf16[32,256]{1,0:T(8,128)(2,1)} %refs_1_.1) | copy-start | bytes 49156
  88.2 6.5 %collective-permute-start.2 = (bf16[16,64,256]{2,1,0:T(8,128)(2,1)S(1)}, bf16[16,64,256]{2,1,0:T(8,128)(2,1)S(1)}, u32[]{:S(2)}, u32[]{:S(2)}) collective-permute-start(bf16[16,64,256]{2,1,0:T(8,128)(2,1)S(1)} %slice.4), channel_id=1, source_target_pairs={{0,16},{16,0},{1,17},{17,1},{2,18},{18,2},{3,19},{19,3},{4,20},{20... | collective-permute-start | bytes 1572872 | tf_op jit(solution)/shard_map/ppermute | solution.py:272

commit v6 on v5

--- a/solution.py
+++ b/solution.py
@@ -220,7 +220,7 @@
     kept = pl.pallas_call(
         slab_kernel,
         out_shape=jax.ShapeDtypeStruct(queue.shape, BF),
-        in_specs=[ANY, ANY],
+        in_specs=[ANY, VMEM],
         out_specs=ANY,
         scratch_shapes=[pltpu.SemaphoreType.DMA],
         compiler_params=pltpu.CompilerParams(vmem_limit_bytes=56 * MIB),

time: 95.6 us -> 65.1 us (0.68)
  Pallas kernels: 42 us -> 11.4 us
    pallas_call x1, Pallas kernels: 32.9 us -> 2.29 us  [local(): pl.pallas_call(slab_kernel, out_shape=jax.ShapeDtypeStruct(queue.shape, B...]
  transfers between devices with their start and end apart: 4 -> 4, of which waited for: 2 -> 2; matrix products, arithmetic and copies ran while one was open for 0% -> 0% of each run, Pallas kernels for 42% -> 14%
where the time goes in v6:
time: 65.1 us; the launch traced here: 64.7 us
  blocking collectives  31.8 us (49%)
  starting transfers between devices  18.5 us (28%)
  Pallas kernels  11.4 us (18%)
  waiting for transfers between devices  1.43 us (2%)
  between operations  1.41 us (2%)
    all_to_all x1, blocking collectives, local(): back = lax.all_to_all(out, ('x', 'y'), 0, 0)  31.8 us
    all_to_all x1, starting transfers between devices, local(): got = lax.all_to_all(message, ('x', 'y'), 0, 0)  7.58 us
    pallas_call x1, Pallas kernels, local(): pl.pallas_call(lambda *refs: partial_kernel(scale, srcs, nq, *refs), out_...  6.11 us
    ppermute x1, starting transfers between devices, local(): twin = lax.ppermute(back[:, at:at + srcs * nk, :], 'c', swap)  5.52 us
    ppermute x1, starting transfers between devices, local(): other = lax.ppermute(slab_keys, 'c', swap)  4.74 us
    pallas_call x1, Pallas kernels, local(): pl.pallas_call(slab_kernel, out_shape=jax.ShapeDtypeStruct(queue.shape, B...  2.29 us
    pallas_call x1, Pallas kernels, local(): pl.pallas_call(lambda *refs: message_kernel(srcs, *refs), out_shape=jax.S...  1.49 us
  transfers between devices with their start and end apart: 4, of which 2 were waited for; matrix products, arithmetic and copies ran while one was open for 0% of the time, Pallas kernels for 14%

profile of v6, /device:TPU:1, one launch (start us, length us, event | category | flops | bytes accessed | tf_op | source)
XLA Modules:
  0.0 64.7 jit_solution(526681993605505452)
XLA Ops:
  0.6 1.5 %shard_map.76.after_ref = bf16[16,40,256]{2,1,0:T(8,128)(2,1)} custom-call(bf16[32,256]{1,0:T(8,128)(2,1)} %refs_1_.1, s32[1,32]{1,0:T(1,128)} %bitcast.11, bf16[4,256]{1,0:T(4,128)(2,1)} %refs_2_.2), custom_call_target="tpu_custom_call" | custom-call | tf_op jit(solution)/shard_map/pallas_call | solution.py:211
  2.1 7.6 %all-to-all-start = ((bf16[16,40,256]{2,1,0:T(8,128)(2,1)}), bf16[16,40,256]{2,1,0:T(8,128)(2,1)S(1)}, u32[]{:S(2)}, u32[]{:S(2)}) async-start(bf16[16,40,256]{2,1,0:T(8,128)(2,1)} %shard_map.76.after_ref), calls=%async_computation | async-start | bytes 655360 | tf_op jit(solution)/shard_map/all_to_all | solution.py:219
  9.7 0.0 copy-start.1
  9.7 2.3 %shard_map.78.refs_3_ = bf16[2048,256]{1,0:T(8,128)(2,1)} custom-call(bf16[16,40,256]{2,1,0:T(8,128)(2,1)} %shard_map.76.after_ref, bf16[2048,256]{1,0:T(8,128)(2,1)} %refs_2_.3), custom_call_target="tpu_custom_call" | custom-call | flops 6000000000 | tf_op jit(solution)/shard_map/pallas_call | solution.py:220
  12.0 0.0 copy-done.1
  12.0 4.7 %collective-permute-start.1 = (bf16[2048,256]{1,0:T(8,128)(2,1)S(1)}, bf16[2048,256]{1,0:T(8,128)(2,1)S(1)}, u32[]{:S(2)}, u32[]{:S(2)}) collective-permute-start(bf16[2048,256]{1,0:T(8,128)(2,1)S(1)} %copy-done.1), channel_id=1, source_target_pairs={{0,16},{16,0},{1,17},{17,1},{2,18},{18,2},{3,19},{19,3},{4,20},{20... | collective-permute-start | bytes 3145736 | tf_op jit(solution)/shard_map/ppermute | solution.py:230
  17.5 0.1 stack.27.refs_0_
  17.5 0.0 all-to-all-done.refs_0_.refs_1_
  17.6 0.7 %collective-permute-start = (bf16[64,256]{1,0:T(8,128)(2,1)S(1)}, bf16[64,256]{1,0:T(8,128)(2,1)S(1)}, u32[]{:S(2)}, u32[]{:S(2)}) collective-permute-start(bf16[64,256]{1,0:T(8,128)(2,1)S(1)} %shard_map.77.refs_4_), channel_id=1, source_target_pairs={{0,0},{1,1},{2,2},{3,3},{4,4},{5,5},{6,6},{7,7},{8,8},{9,9},{10,10... | collective-permute-start | bytes 98312 | tf_op jit(solution)/shard_map/ppermute | solution.py:246
  18.2 0.8 %collective-permute-done.1.refs_3_ = bf16[2048,256]{1,0:T(8,128)(2,1)S(1)} collective-permute-done((bf16[2048,256]{1,0:T(8,128)(2,1)S(1)}, bf16[2048,256]{1,0:T(8,128)(2,1)S(1)}, u32[]{:S(2)}, u32[]{:S(2)}) %collective-permute-start.1) | collective-permute-done | bytes 1048608 | tf_op jit(solution)/shard_map/ppermute | solution.py:230
  19.1 6.1 %shard_map.79.refs_1_ = bf16[16,136,256]{2,1,0:T(8,128)(2,1)S(1)} custom-call(s32[5]{0:T(128)S(1)} %stack.27.refs_0_, bf16[16,40,256]{2,1,0:T(8,128)(2,1)S(1)} %all-to-all-done.refs_0_.refs_1_, bf16[2048,256]{1,0:T(8,128)(2,1)S(1)} %copy-done.1, bf16[2048,256]{1,0:T(8,128)(2,1)S(1)} %collective-permute-done.1.refs_3_, bf16[64,256]{1,0:T(8,128)(2,1)S(1)} %shard_map.77.refs_4_), custom_call_target="tpu_custom_call" | custom-call | flops 3221225472 | bytes 2097152 | tf_op jit(solution)/shard_map/pallas_call | solution.py:254
  25.2 0.0 collective-permute-done.refs_0_
  25.2 0.0 copy-start
  25.2 31.8 %all_to_all.10.refs_0_.refs_1_ = bf16[16,136,256]{2,1,0:T(8,128)(2,1)S(1)} all-to-all(bf16[16,136,256]{2,1,0:T(8,128)(2,1)S(1)} %shard_map.80), channel_id=1, replica_groups=mesh['x'=4,'y'=4,'c'=2,'z'=16] {'x','y'}, dimensions={0} | all-to-all | bytes 2228224 | tf_op jit(solution)/shard_map/all_to_all | solution.py:271
  57.1 5.5 %collective-permute-start.2 = (bf16[16,64,256]{2,1,0:T(8,128)(2,1)S(1)}, bf16[16,64,256]{2,1,0:T(8,128)(2,1)S(1)}, u32[]{:S(2)}, u32[]{:S(2)}) collective-permute-start(bf16[16,64,256]{2,1,0:T(8,128)(2,1)S(1)} %slice.4), channel_id=1, source_target_pairs={{0,16},{16,0},{1,17},{17,1},{2,18},{18,2},{3,19},{19,3},{4,20},{20... | collective-permute-start | bytes 1572872 | tf_op jit(solution)/shard_map/ppermute | solution.py:272
  62.6 0.0 copy-done
  62.6 0.9 %shard_map.81 = (f32[1,32]{1,0:T(1,128)}, bf16[32,256]{1,0:T(8,128)(2,1)}) custom-call(bf16[16,136,256]{2,1,0:T(8,128)(2,1)S(1)} %all_to_all.10.refs_0_.refs_1_, bf16[32,256]{1,0:T(8,128)(2,1)S(1)} %copy-done), custom_call_target="tpu_custom_call" | custom-call | tf_op jit(solution)/shard_map/pallas_call | solution.py:274
  63.5 0.6 collective-permute-done.2.refs_2_
  64.1 0.6 shard_map.82
  (3 shorter events, 0.1 us)
Async XLA Ops:
  2.1 15.4 %all-to-all-start = ((bf16[16,40,256]{2,1,0:T(8,128)(2,1)}), bf16[16,40,256]{2,1,0:T(8,128)(2,1)S(1)}, u32[]{:S(2)}, u32[]{:S(2)}) async-start(bf16[16,40,256]{2,1,0:T(8,128)(2,1)} %shard_map.76.after_ref), calls=%async_computation | async-start | bytes 655360 | tf_op jit(solution)/shard_map/all_to_all | solution.py:219
  9.7 2.3 %copy-start.1 = (bf16[2048,256]{1,0:T(8,128)(2,1)S(1)}, bf16[2048,256]{1,0:T(8,128)(2,1)}, u32[]{:S(2)}) copy-start(bf16[2048,256]{1,0:T(8,128)(2,1)} %refs_2_.3) | copy-start | bytes 3145732
  12.0 7.0 %collective-permute-start.1 = (bf16[2048,256]{1,0:T(8,128)(2,1)S(1)}, bf16[2048,256]{1,0:T(8,128)(2,1)S(1)}, u32[]{:S(2)}, u32[]{:S(2)}) collective-permute-start(bf16[2048,256]{1,0:T(8,128)(2,1)S(1)} %copy-done.1), channel_id=1, source_target_pairs={{0,16},{16,0},{1,17},{17,1},{2,18},{18,2},{3,19},{19,3},{4,20},{20... | collective-permute-start | bytes 3145736 | tf_op jit(solution)/shard_map/ppermute | solution.py:230
  17.6 7.6 %collective-permute-start = (bf16[64,256]{1,0:T(8,128)(2,1)S(1)}, bf16[64,256]{1,0:T(8,128)(2,1)S(1)}, u32[]{:S(2)}, u32[]{:S(2)}) collective-permute-start(bf16[64,256]{1,0:T(8,128)(2,1)S(1)} %shard_map.77.refs_4_), channel_id=1, source_target_pairs={{0,0},{1,1},{2,2},{3,3},{4,4},{5,5},{6,6},{7,7},{8,8},{9,9},{10,10... | collective-permute-start | bytes 98312 | tf_op jit(solution)/shard_map/ppermute | solution.py:246
  25.2 37.4 %copy-start = (bf16[32,256]{1,0:T(8,128)(2,1)S(1)}, bf16[32,256]{1,0:T(8,128)(2,1)}, u32[]{:S(2)}) copy-start(bf16[32,256]{1,0:T(8,128)(2,1)} %refs_1_.1) | copy-start | bytes 49156
  57.1 7.0 %collective-permute-start.2 = (bf16[16,64,256]{2,1,0:T(8,128)(2,1)S(1)}, bf16[16,64,256]{2,1,0:T(8,128)(2,1)S(1)}, u32[]{:S(2)}, u32[]{:S(2)}) collective-permute-start(bf16[16,64,256]{2,1,0:T(8,128)(2,1)S(1)} %slice.4), channel_id=1, source_target_pairs={{0,16},{16,0},{1,17},{17,1},{2,18},{18,2},{3,19},{19,3},{4,20},{20... | collective-permute-start | bytes 1572872 | tf_op jit(solution)/shard_map/ppermute | solution.py:272

commit v7 on v6

--- a/solution.py
+++ b/solution.py
@@ -56,16 +56,17 @@
     total = jnp.zeros((n, 128), F32)
     grad = jnp.zeros((n, width), F32)
     positive = jnp.zeros((n, width), F32)
-    column = lax.broadcasted_iota(jnp.int32, (n, block), 1)
+    column = lax.broadcasted_iota(jnp.int32, (n, block), 1).astype(F32).astype(BF)
+    zero, one = jnp.zeros((n, block), BF), jnp.ones((n, block), BF)
     for i, (start, ref, b) in enumerate(blocks):
         s = s_ref[:, i * block:(i + 1) * block]
-        hit = column == (target - start)
-        e = jnp.where(hit, 0.0, jnp.exp2((s - point) * (scale * LOG2E)))
+        e = jnp.exp2((s - point) * (scale * LOG2E))
         for c in range(block // 128):
             total += e[:, c * 128:(c + 1) * 128]
+        hit = column == jnp.broadcast_to((target - start).astype(F32), (n, block)).astype(BF)
         keys = ref[b * block:(b + 1) * block, :]
-        grad += jnp.dot(e.astype(BF), keys, preferred_element_type=F32)
-        positive += jnp.dot(hit.astype(F32).astype(BF), keys, preferred_element_type=F32)
+        grad += jnp.dot(jnp.where(hit, zero, e.astype(BF)), keys, preferred_element_type=F32)
+        positive += jnp.dot(jnp.where(hit, one, zero), keys, preferred_element_type=F32)
     total = jnp.sum(total, axis=1, keepdims=True)
     t0 = total.astype(BF).astype(F32)
     t1 = (total - t0).astype(BF).astype(F32)
@@ -100,11 +101,13 @@
         points.append(jnp.sum(jnp.where(lane == row, st, 0.0), axis=1, keepdims=True))
         three = (lane >= nq) & (lane % nq == row)
         totals.append(jnp.sum(jnp.where(three, st, 0.0), axis=1, keepdims=True))
-    s_pos = jnp.sum(q_ref[...].astype(F32) * positive, axis=1, keepdims=True)
+    s_pos = rows_dot(q_ref[...], positive.astype(BF))
+    square = lax.broadcasted_iota(jnp.int32, (nq, nq), 0) == lax.broadcasted_iota(jnp.int32, (nq, nq), 1)
+    s_pos = jnp.sum(jnp.where(square, s_pos, 0.0), axis=1, keepdims=True)
     top = s_pos
     for p in points:
         top = jnp.maximum(top, p)
-    total = jnp.exp2((s_pos - top) * (scale * LOG2E))
+    total = jnp.zeros((nq, 1), F32)
     grad = jnp.zeros((nq, width), F32)
     for j in range(srcs):
         a = jnp.exp2((points[j] - top) * (scale * LOG2E))

time: 65.1 us -> 64.3 us (0.988)
  Pallas kernels: 11.4 us -> 10.7 us
    pallas_call x1, Pallas kernels: 6.11 us -> 5.37 us  [local(): pl.pallas_call(lambda *refs: partial_kernel(scale, srcs, nq, *refs), out_...]
where the time goes in v7:
time: 64.3 us; the launch traced here: 63.9 us
  blocking collectives  31.8 us (49%)
  starting transfers between devices  18.5 us (29%)
  Pallas kernels  10.7 us (17%)
  between operations  1.41 us (2%)
  waiting for transfers between devices  1.35 us (2%)
    all_to_all x1, blocking collectives, local(): back = lax.all_to_all(out, ('x', 'y'), 0, 0)  31.8 us
    all_to_all x1, starting transfers between devices, local(): got = lax.all_to_all(message, ('x', 'y'), 0, 0)  7.58 us
    ppermute x1, starting transfers between devices, local(): twin = lax.ppermute(back[:, at:at + srcs * nk, :], 'c', swap)  5.52 us
    pallas_call x1, Pallas kernels, local(): pl.pallas_call(lambda *refs: partial_kernel(scale, srcs, nq, *refs), out_...  5.37 us
    ppermute x1, starting transfers between devices, local(): other = lax.ppermute(slab_keys, 'c', swap)  4.74 us
    pallas_call x1, Pallas kernels, local(): pl.pallas_call(slab_kernel, out_shape=jax.ShapeDtypeStruct(queue.shape, B...  2.29 us
    pallas_call x1, Pallas kernels, local(): pl.pallas_call(lambda *refs: message_kernel(srcs, *refs), out_shape=jax.S...  1.49 us
  transfers between devices with their start and end apart: 4, of which 2 were waited for; matrix products, arithmetic and copies ran while one was open for 0% of the time, Pallas kernels for 14%

profile of v7, /device:TPU:1, one launch (start us, length us, event | category | flops | bytes accessed | tf_op | source)
XLA Modules:
  0.0 63.9 jit_solution(3021732310902191770)
XLA Ops:
  0.6 1.5 %shard_map.76.after_ref = bf16[16,40,256]{2,1,0:T(8,128)(2,1)} custom-call(bf16[32,256]{1,0:T(8,128)(2,1)} %refs_1_.1, s32[1,32]{1,0:T(1,128)} %bitcast.11, bf16[4,256]{1,0:T(4,128)(2,1)} %refs_2_.2), custom_call_target="tpu_custom_call" | custom-call | tf_op jit(solution)/shard_map/pallas_call | solution.py:214
  2.1 7.6 %all-to-all-start = ((bf16[16,40,256]{2,1,0:T(8,128)(2,1)}), bf16[16,40,256]{2,1,0:T(8,128)(2,1)S(1)}, u32[]{:S(2)}, u32[]{:S(2)}) async-start(bf16[16,40,256]{2,1,0:T(8,128)(2,1)} %shard_map.76.after_ref), calls=%async_computation | async-start | bytes 655360 | tf_op jit(solution)/shard_map/all_to_all | solution.py:222
  9.7 0.0 copy-start.1
  9.7 2.3 %shard_map.78.refs_3_ = bf16[2048,256]{1,0:T(8,128)(2,1)} custom-call(bf16[16,40,256]{2,1,0:T(8,128)(2,1)} %shard_map.76.after_ref, bf16[2048,256]{1,0:T(8,128)(2,1)} %refs_2_.3), custom_call_target="tpu_custom_call" | custom-call | flops 6000000000 | tf_op jit(solution)/shard_map/pallas_call | solution.py:223
  12.0 0.0 copy-done.1
  12.0 4.7 %collective-permute-start.1 = (bf16[2048,256]{1,0:T(8,128)(2,1)S(1)}, bf16[2048,256]{1,0:T(8,128)(2,1)S(1)}, u32[]{:S(2)}, u32[]{:S(2)}) collective-permute-start(bf16[2048,256]{1,0:T(8,128)(2,1)S(1)} %copy-done.1), channel_id=1, source_target_pairs={{0,16},{16,0},{1,17},{17,1},{2,18},{18,2},{3,19},{19,3},{4,20},{20... | collective-permute-start | bytes 3145736 | tf_op jit(solution)/shard_map/ppermute | solution.py:233
  17.5 0.1 stack.27.refs_0_
  17.5 0.0 all-to-all-done.refs_0_.refs_1_
  17.6 0.7 %collective-permute-start = (bf16[64,256]{1,0:T(8,128)(2,1)S(1)}, bf16[64,256]{1,0:T(8,128)(2,1)S(1)}, u32[]{:S(2)}, u32[]{:S(2)}) collective-permute-start(bf16[64,256]{1,0:T(8,128)(2,1)S(1)} %shard_map.77.refs_4_), channel_id=1, source_target_pairs={{0,0},{1,1},{2,2},{3,3},{4,4},{5,5},{6,6},{7,7},{8,8},{9,9},{10,10... | collective-permute-start | bytes 98312 | tf_op jit(solution)/shard_map/ppermute | solution.py:249
  18.2 0.8 %collective-permute-done.1.refs_3_ = bf16[2048,256]{1,0:T(8,128)(2,1)S(1)} collective-permute-done((bf16[2048,256]{1,0:T(8,128)(2,1)S(1)}, bf16[2048,256]{1,0:T(8,128)(2,1)S(1)}, u32[]{:S(2)}, u32[]{:S(2)}) %collective-permute-start.1) | collective-permute-done | bytes 1048608 | tf_op jit(solution)/shard_map/ppermute | solution.py:233
  19.1 5.4 %shard_map.79.refs_1_ = bf16[16,136,256]{2,1,0:T(8,128)(2,1)S(1)} custom-call(s32[5]{0:T(128)S(1)} %stack.27.refs_0_, bf16[16,40,256]{2,1,0:T(8,128)(2,1)S(1)} %all-to-all-done.refs_0_.refs_1_, bf16[2048,256]{1,0:T(8,128)(2,1)S(1)} %copy-done.1, bf16[2048,256]{1,0:T(8,128)(2,1)S(1)} %collective-permute-done.1.refs_3_, bf16[64,256]{1,0:T(8,128)(2,1)S(1)} %shard_map.77.refs_4_), custom_call_target="tpu_custom_call" | custom-call | flops 3221225472 | bytes 2097152 | tf_op jit(solution)/shard_map/pallas_call | solution.py:257
  24.4 0.0 collective-permute-done.refs_0_
  24.5 0.0 copy-start
  24.5 31.8 %all_to_all.10.refs_0_.refs_1_ = bf16[16,136,256]{2,1,0:T(8,128)(2,1)S(1)} all-to-all(bf16[16,136,256]{2,1,0:T(8,128)(2,1)S(1)} %shard_map.80), channel_id=1, replica_groups=mesh['x'=4,'y'=4,'c'=2,'z'=16] {'x','y'}, dimensions={0} | all-to-all | bytes 2228224 | tf_op jit(solution)/shard_map/all_to_all | solution.py:274
  56.3 5.5 %collective-permute-start.2 = (bf16[16,64,256]{2,1,0:T(8,128)(2,1)S(1)}, bf16[16,64,256]{2,1,0:T(8,128)(2,1)S(1)}, u32[]{:S(2)}, u32[]{:S(2)}) collective-permute-start(bf16[16,64,256]{2,1,0:T(8,128)(2,1)S(1)} %slice.4), channel_id=1, source_target_pairs={{0,16},{16,0},{1,17},{17,1},{2,18},{18,2},{3,19},{19,3},{4,20},{20... | collective-permute-start | bytes 1572872 | tf_op jit(solution)/shard_map/ppermute | solution.py:275
  61.8 0.0 copy-done
  61.9 1.0 %shard_map.81 = (f32[1,32]{1,0:T(1,128)}, bf16[32,256]{1,0:T(8,128)(2,1)}) custom-call(bf16[16,136,256]{2,1,0:T(8,128)(2,1)S(1)} %all_to_all.10.refs_0_.refs_1_, bf16[32,256]{1,0:T(8,128)(2,1)S(1)} %copy-done), custom_call_target="tpu_custom_call" | custom-call | tf_op jit(solution)/shard_map/pallas_call | solution.py:277
  62.8 0.5 collective-permute-done.2.refs_2_
  63.4 0.6 shard_map.82
  (3 shorter events, 0.1 us)
Async XLA Ops:
  2.1 15.4 %all-to-all-start = ((bf16[16,40,256]{2,1,0:T(8,128)(2,1)}), bf16[16,40,256]{2,1,0:T(8,128)(2,1)S(1)}, u32[]{:S(2)}, u32[]{:S(2)}) async-start(bf16[16,40,256]{2,1,0:T(8,128)(2,1)} %shard_map.76.after_ref), calls=%async_computation | async-start | bytes 655360 | tf_op jit(solution)/shard_map/all_to_all | solution.py:222
  9.7 2.3 %copy-start.1 = (bf16[2048,256]{1,0:T(8,128)(2,1)S(1)}, bf16[2048,256]{1,0:T(8,128)(2,1)}, u32[]{:S(2)}) copy-start(bf16[2048,256]{1,0:T(8,128)(2,1)} %refs_2_.3) | copy-start | bytes 3145732
  12.0 7.0 %collective-permute-start.1 = (bf16[2048,256]{1,0:T(8,128)(2,1)S(1)}, bf16[2048,256]{1,0:T(8,128)(2,1)S(1)}, u32[]{:S(2)}, u32[]{:S(2)}) collective-permute-start(bf16[2048,256]{1,0:T(8,128)(2,1)S(1)} %copy-done.1), channel_id=1, source_target_pairs={{0,16},{16,0},{1,17},{17,1},{2,18},{18,2},{3,19},{19,3},{4,20},{20... | collective-permute-start | bytes 3145736 | tf_op jit(solution)/shard_map/ppermute | solution.py:233
  17.6 6.9 %collective-permute-start = (bf16[64,256]{1,0:T(8,128)(2,1)S(1)}, bf16[64,256]{1,0:T(8,128)(2,1)S(1)}, u32[]{:S(2)}, u32[]{:S(2)}) collective-permute-start(bf16[64,256]{1,0:T(8,128)(2,1)S(1)} %shard_map.77.refs_4_), channel_id=1, source_target_pairs={{0,0},{1,1},{2,2},{3,3},{4,4},{5,5},{6,6},{7,7},{8,8},{9,9},{10,10... | collective-permute-start | bytes 98312 | tf_op jit(solution)/shard_map/ppermute | solution.py:249
  24.5 37.4 %copy-start = (bf16[32,256]{1,0:T(8,128)(2,1)S(1)}, bf16[32,256]{1,0:T(8,128)(2,1)}, u32[]{:S(2)}) copy-start(bf16[32,256]{1,0:T(8,128)(2,1)} %refs_1_.1) | copy-start | bytes 49156
  56.3 7.0 %collective-permute-start.2 = (bf16[16,64,256]{2,1,0:T(8,128)(2,1)S(1)}, bf16[16,64,256]{2,1,0:T(8,128)(2,1)S(1)}, u32[]{:S(2)}, u32[]{:S(2)}) collective-permute-start(bf16[16,64,256]{2,1,0:T(8,128)(2,1)S(1)} %slice.4), channel_id=1, source_target_pairs={{0,16},{16,0},{1,17},{17,1},{2,18},{18,2},{3,19},{19,3},{4,20},{20... | collective-permute-start | bytes 1572872 | tf_op jit(solution)/shard_map/ppermute | solution.py:275

commit v8 on v7

--- a/solution.py
+++ b/solution.py
@@ -170,7 +170,7 @@
                 tiles = []
                 for k in range(4):
                     plane = 4 * b + k
-                    slot = ((z - plane) if c == 0 else (plane - z)) & (cols - 1)
+                    slot = (z - plane - c * (cols // 2)) & (cols - 1)
                     block = ref[slot, base + 16 * a:base + 16 * a + 16, :].astype(F32)
                     tiles.append((block[:8], block[8:]))
                 for v in range(4):
@@ -244,7 +244,7 @@
     for s in range(srcs):
         for c in range(2):
             for k in range(nz):
-                to = (k + s) % nz if c == 0 else (k - s) % nz
+                to = (k + s + c * nz // 2) % nz
                 pairs.append(((s * 2 + c) * nz + k, (s * 2 + c) * nz + to))
     moved = lax.ppermute(plane_keys, ("x", "y", "c", "z"), pairs)
 

time: 64.3 us -> 64.3 us (level)
  starting transfers between devices: 18.5 us -> 33.4 us
  blocking collectives: 31.8 us -> 17.7 us
  waiting for transfers between devices: 1.35 us -> 0.54 us
    ppermute x1, starting transfers between devices: 0.66 us -> 15.4 us  [local(): moved = lax.ppermute(plane_keys, ('x', 'y', 'c', 'z'), pairs)]
    all_to_all x1, blocking collectives: 31.8 us -> 17.7 us  [local(): back = lax.all_to_all(out, ('x', 'y'), 0, 0)]
    ppermute x1, waiting for transfers between devices: 0.81 us -> 0.01 us  [local(): other = lax.ppermute(slab_keys, 'c', swap)]
  transfers between devices with their start and end apart: 4 -> 4, of which waited for: 2 -> 1; matrix products, arithmetic and copies ran while one was open for 0% -> 0% of each run, Pallas kernels for 14% -> 14%
where the time goes in v8:
time: 64.3 us; the launch traced here: 63.9 us
  starting transfers between devices  33.4 us (52%)
  blocking collectives  17.7 us (28%)
  Pallas kernels  10.7 us (17%)
  between operations  1.42 us (2%)
    all_to_all x1, blocking collectives, local(): back = lax.all_to_all(out, ('x', 'y'), 0, 0)  17.7 us
    ppermute x1, starting transfers between devices, local(): moved = lax.ppermute(plane_keys, ('x', 'y', 'c', 'z'), pairs)  15.4 us
    all_to_all x1, starting transfers between devices, local(): got = lax.all_to_all(message, ('x', 'y'), 0, 0)  7.58 us
    ppermute x1, starting transfers between devices, local(): twin = lax.ppermute(back[:, at:at + srcs * nk, :], 'c', swap)  5.61 us
    pallas_call x1, Pallas kernels, local(): pl.pallas_call(lambda *refs: partial_kernel(scale, srcs, nq, *refs), out_...  5.37 us
    ppermute x1, starting transfers between devices, local(): other = lax.ppermute(slab_keys, 'c', swap)  4.74 us
    pallas_call x1, Pallas kernels, local(): pl.pallas_call(slab_kernel, out_shape=jax.ShapeDtypeStruct(queue.shape, B...  2.29 us
    pallas_call x1, Pallas kernels, local(): pl.pallas_call(lambda *refs: message_kernel(srcs, *refs), out_shape=jax.S...  1.49 us
  transfers between devices with their start and end apart: 4, of which 1 were waited for; matrix products, arithmetic and copies ran while one was open for 0% of the time, Pallas kernels for 14%

profile of v8, /device:TPU:1, one launch (start us, length us, event | category | flops | bytes accessed | tf_op | source)
XLA Modules:
  0.0 63.9 jit_solution(14352337590315584184)
XLA Ops:
  0.6 1.5 %shard_map.76.after_ref = bf16[16,40,256]{2,1,0:T(8,128)(2,1)} custom-call(bf16[32,256]{1,0:T(8,128)(2,1)} %refs_1_.1, s32[1,32]{1,0:T(1,128)} %bitcast.11, bf16[4,256]{1,0:T(4,128)(2,1)} %refs_2_.2), custom_call_target="tpu_custom_call" | custom-call | tf_op jit(solution)/shard_map/pallas_call | solution.py:214
  2.1 7.6 %all-to-all-start = ((bf16[16,40,256]{2,1,0:T(8,128)(2,1)}), bf16[16,40,256]{2,1,0:T(8,128)(2,1)S(1)}, u32[]{:S(2)}, u32[]{:S(2)}) async-start(bf16[16,40,256]{2,1,0:T(8,128)(2,1)} %shard_map.76.after_ref), calls=%async_computation | async-start | bytes 655360 | tf_op jit(solution)/shard_map/all_to_all | solution.py:222
  9.7 0.0 copy-start.1
  9.7 2.3 %shard_map.78.refs_3_ = bf16[2048,256]{1,0:T(8,128)(2,1)} custom-call(bf16[16,40,256]{2,1,0:T(8,128)(2,1)} %shard_map.76.after_ref, bf16[2048,256]{1,0:T(8,128)(2,1)} %refs_2_.3), custom_call_target="tpu_custom_call" | custom-call | flops 6000000000 | tf_op jit(solution)/shard_map/pallas_call | solution.py:223
  12.0 0.0 copy-done.1
  12.0 4.7 %collective-permute-start.1 = (bf16[2048,256]{1,0:T(8,128)(2,1)S(1)}, bf16[2048,256]{1,0:T(8,128)(2,1)S(1)}, u32[]{:S(2)}, u32[]{:S(2)}) collective-permute-start(bf16[2048,256]{1,0:T(8,128)(2,1)S(1)} %copy-done.1), channel_id=1, source_target_pairs={{0,16},{16,0},{1,17},{17,1},{2,18},{18,2},{3,19},{19,3},{4,20},{20... | collective-permute-start | bytes 3145736 | tf_op jit(solution)/shard_map/ppermute | solution.py:233
  17.5 0.1 stack.27.refs_0_
  17.5 0.0 all-to-all-done.refs_0_.refs_1_
  17.6 15.4 %collective-permute-start = (bf16[64,256]{1,0:T(8,128)(2,1)S(1)}, bf16[64,256]{1,0:T(8,128)(2,1)S(1)}, u32[]{:S(2)}, u32[]{:S(2)}) collective-permute-start(bf16[64,256]{1,0:T(8,128)(2,1)S(1)} %shard_map.77.refs_4_), channel_id=1, source_target_pairs={{0,0},{1,1},{2,2},{3,3},{4,4},{5,5},{6,6},{7,7},{8,8},{9,9},{10,10... | collective-permute-start | bytes 98312 | tf_op jit(solution)/shard_map/ppermute | solution.py:249
  33.0 0.0 collective-permute-done.1.refs_3_
  33.0 5.4 %shard_map.79.refs_1_ = bf16[16,136,256]{2,1,0:T(8,128)(2,1)S(1)} custom-call(s32[5]{0:T(128)S(1)} %stack.27.refs_0_, bf16[16,40,256]{2,1,0:T(8,128)(2,1)S(1)} %all-to-all-done.refs_0_.refs_1_, bf16[2048,256]{1,0:T(8,128)(2,1)S(1)} %copy-done.1, bf16[2048,256]{1,0:T(8,128)(2,1)S(1)} %collective-permute-done.1.refs_3_, bf16[64,256]{1,0:T(8,128)(2,1)S(1)} %shard_map.77.refs_4_), custom_call_target="tpu_custom_call" | custom-call | flops 3221225472 | bytes 2097152 | tf_op jit(solution)/shard_map/pallas_call | solution.py:257
  38.4 0.0 collective-permute-done.refs_0_
  38.5 0.0 copy-start
  38.5 17.7 %all_to_all.10.refs_0_.refs_1_ = bf16[16,136,256]{2,1,0:T(8,128)(2,1)S(1)} all-to-all(bf16[16,136,256]{2,1,0:T(8,128)(2,1)S(1)} %shard_map.80), channel_id=1, replica_groups=mesh['x'=4,'y'=4,'c'=2,'z'=16] {'x','y'}, dimensions={0} | all-to-all | bytes 2228224 | tf_op jit(solution)/shard_map/all_to_all | solution.py:274
  56.2 5.6 %collective-permute-start.2 = (bf16[16,64,256]{2,1,0:T(8,128)(2,1)S(1)}, bf16[16,64,256]{2,1,0:T(8,128)(2,1)S(1)}, u32[]{:S(2)}, u32[]{:S(2)}) collective-permute-start(bf16[16,64,256]{2,1,0:T(8,128)(2,1)S(1)} %slice.4), channel_id=1, source_target_pairs={{0,16},{16,0},{1,17},{17,1},{2,18},{18,2},{3,19},{19,3},{4,20},{20... | collective-permute-start | bytes 1572872 | tf_op jit(solution)/shard_map/ppermute | solution.py:275
  61.8 0.0 copy-done
  61.8 1.0 %shard_map.81 = (f32[1,32]{1,0:T(1,128)}, bf16[32,256]{1,0:T(8,128)(2,1)}) custom-call(bf16[16,136,256]{2,1,0:T(8,128)(2,1)S(1)} %all_to_all.10.refs_0_.refs_1_, bf16[32,256]{1,0:T(8,128)(2,1)S(1)} %copy-done), custom_call_target="tpu_custom_call" | custom-call | tf_op jit(solution)/shard_map/pallas_call | solution.py:277
  62.8 0.5 collective-permute-done.2.refs_2_
  63.3 0.6 shard_map.82
  (3 shorter events, 0.1 us)
Async XLA Ops:
  2.1 15.4 %all-to-all-start = ((bf16[16,40,256]{2,1,0:T(8,128)(2,1)}), bf16[16,40,256]{2,1,0:T(8,128)(2,1)S(1)}, u32[]{:S(2)}, u32[]{:S(2)}) async-start(bf16[16,40,256]{2,1,0:T(8,128)(2,1)} %shard_map.76.after_ref), calls=%async_computation | async-start | bytes 655360 | tf_op jit(solution)/shard_map/all_to_all | solution.py:222
  9.7 2.3 %copy-start.1 = (bf16[2048,256]{1,0:T(8,128)(2,1)S(1)}, bf16[2048,256]{1,0:T(8,128)(2,1)}, u32[]{:S(2)}) copy-start(bf16[2048,256]{1,0:T(8,128)(2,1)} %refs_2_.3) | copy-start | bytes 3145732
  12.0 21.0 %collective-permute-start.1 = (bf16[2048,256]{1,0:T(8,128)(2,1)S(1)}, bf16[2048,256]{1,0:T(8,128)(2,1)S(1)}, u32[]{:S(2)}, u32[]{:S(2)}) collective-permute-start(bf16[2048,256]{1,0:T(8,128)(2,1)S(1)} %copy-done.1), channel_id=1, source_target_pairs={{0,16},{16,0},{1,17},{17,1},{2,18},{18,2},{3,19},{19,3},{4,20},{20... | collective-permute-start | bytes 3145736 | tf_op jit(solution)/shard_map/ppermute | solution.py:233
  17.6 20.8 %collective-permute-start = (bf16[64,256]{1,0:T(8,128)(2,1)S(1)}, bf16[64,256]{1,0:T(8,128)(2,1)S(1)}, u32[]{:S(2)}, u32[]{:S(2)}) collective-permute-start(bf16[64,256]{1,0:T(8,128)(2,1)S(1)} %shard_map.77.refs_4_), channel_id=1, source_target_pairs={{0,0},{1,1},{2,2},{3,3},{4,4},{5,5},{6,6},{7,7},{8,8},{9,9},{10,10... | collective-permute-start | bytes 98312 | tf_op jit(solution)/shard_map/ppermute | solution.py:249
  38.5 23.3 %copy-start = (bf16[32,256]{1,0:T(8,128)(2,1)S(1)}, bf16[32,256]{1,0:T(8,128)(2,1)}, u32[]{:S(2)}) copy-start(bf16[32,256]{1,0:T(8,128)(2,1)} %refs_1_.1) | copy-start | bytes 49156
  56.2 7.1 %collective-permute-start.2 = (bf16[16,64,256]{2,1,0:T(8,128)(2,1)S(1)}, bf16[16,64,256]{2,1,0:T(8,128)(2,1)S(1)}, u32[]{:S(2)}, u32[]{:S(2)}) collective-permute-start(bf16[16,64,256]{2,1,0:T(8,128)(2,1)S(1)} %slice.4), channel_id=1, source_target_pairs={{0,16},{16,0},{1,17},{17,1},{2,18},{18,2},{3,19},{19,3},{4,20},{20... | collective-permute-start | bytes 1572872 | tf_op jit(solution)/shard_map/ppermute | solution.py:275

commit v9 on v8

--- a/solution.py
+++ b/solution.py
@@ -39,34 +39,47 @@
         line = tail[4:5, :] * 256.0 + tail[5:6, :]
         parts.append(jnp.sum(jnp.where(lane == row, line, 0.0), axis=1, keepdims=True))
     target = jnp.concatenate(parts, axis=0).astype(jnp.int32)
-    queries = q_ref[...]
-    top = None
     blocks = []
     for b in range(slab // block):
         blocks.append((info_ref[0] + b * block, own_ref, b))
     for b in range(slab // block):
         blocks.append((info_ref[1] + b * block, other_ref, b))
-    for i, (start, ref, b) in enumerate(blocks):
-        s = rows_dot(queries, ref[b * block:(b + 1) * block, :])
-        s_ref[:, i * block:(i + 1) * block] = s
+    half = n // 2
+    column = lax.broadcasted_iota(jnp.int32, (half, block), 1).astype(F32).astype(BF)
+    zero, one = jnp.zeros((half, block), BF), jnp.ones((half, block), BF)
+
+    def score(at, i, top):
+        _, ref, b = blocks[i]
+        s = rows_dot(q_ref[at, :], ref[b * block:(b + 1) * block, :])
+        s_ref[at, i * block:(i + 1) * block] = s
         for c in range(block // 128):
             piece = s[:, c * 128:(c + 1) * 128]
             top = piece if top is None else jnp.maximum(top, piece)
-    point = jnp.max(top, axis=1, keepdims=True).astype(BF).astype(F32)
-    total = jnp.zeros((n, 128), F32)
-    grad = jnp.zeros((n, width), F32)
-    positive = jnp.zeros((n, width), F32)
-    column = lax.broadcasted_iota(jnp.int32, (n, block), 1).astype(F32).astype(BF)
-    zero, one = jnp.zeros((n, block), BF), jnp.ones((n, block), BF)
-    for i, (start, ref, b) in enumerate(blocks):
-        s = s_ref[:, i * block:(i + 1) * block]
-        e = jnp.exp2((s - point) * (scale * LOG2E))
-        for c in range(block // 128):
-            total += e[:, c * 128:(c + 1) * 128]
-        hit = column == jnp.broadcast_to((target - start).astype(F32), (n, block)).astype(BF)
-        keys = ref[b * block:(b + 1) * block, :]
-        grad += jnp.dot(jnp.where(hit, zero, e.astype(BF)), keys, preferred_element_type=F32)
-        positive += jnp.dot(jnp.where(hit, one, zero), keys, preferred_element_type=F32)
+        return top
+
+    halves = (slice(0, half), slice(half, n))
+    tops = [None, None]
+    for i in range(len(blocks)):
+        tops[0] = score(halves[0], i, tops[0])
+    found = []
+    for h, at in enumerate(halves):
+        point = jnp.max(tops[h], axis=1, keepdims=True).astype(BF).astype(F32)
+        total = jnp.zeros((half, 128), F32)
+        grad = jnp.zeros((half, width), F32)
+        positive = jnp.zeros((half, width), F32)
+        for i, (start, ref, b) in enumerate(blocks):
+            if h == 0:
+                tops[1] = score(halves[1], i, tops[1])
+            s = s_ref[at, i * block:(i + 1) * block]
+            e = jnp.exp2((s - point) * (scale * LOG2E))
+            for c in range(block // 128):
+                total += e[:, c * 128:(c + 1) * 128]
+            hit = column == jnp.broadcast_to((target[at] - start).astype(F32), (half, block)).astype(BF)
+            keys = ref[b * block:(b + 1) * block, :]
+            grad += jnp.dot(jnp.where(hit, zero, e.astype(BF)), keys, preferred_element_type=F32)
+            positive += jnp.dot(jnp.where(hit, one, zero), keys, preferred_element_type=F32)
+        found.append((point, total, grad, positive))
+    point, total, grad, positive = (jnp.concatenate(pair, axis=0) for pair in zip(*found))
     total = jnp.sum(total, axis=1, keepdims=True)
     t0 = total.astype(BF).astype(F32)
     t1 = (total - t0).astype(BF).astype(F32)

time: 64.3 us -> 64 us (level)
  transfers between devices with their start and end apart: 4 -> 4, of which waited for: 1 -> 1; matrix products, arithmetic and copies ran while one was open for 0% -> 0% of each run, Pallas kernels for 14% -> 13%
where the time goes in v9:
time: 64 us; the launch traced here: 63.5 us
  starting transfers between devices  33.4 us (52%)
  blocking collectives  17.7 us (28%)
  Pallas kernels  10.4 us (16%)
  between operations  1.42 us (2%)
    all_to_all x1, blocking collectives, local(): back = lax.all_to_all(out, ('x', 'y'), 0, 0)  17.7 us
    ppermute x1, starting transfers between devices, local(): moved = lax.ppermute(plane_keys, ('x', 'y', 'c', 'z'), pairs)  15.4 us
    all_to_all x1, starting transfers between devices, local(): got = lax.all_to_all(message, ('x', 'y'), 0, 0)  7.58 us
    ppermute x1, starting transfers between devices, local(): twin = lax.ppermute(back[:, at:at + srcs * nk, :], 'c', swap)  5.6 us
    pallas_call x1, Pallas kernels, local(): pl.pallas_call(lambda *refs: partial_kernel(scale, srcs, nq, *refs), out_...  5.04 us
    ppermute x1, starting transfers between devices, local(): other = lax.ppermute(slab_keys, 'c', swap)  4.74 us
    pallas_call x1, Pallas kernels, local(): pl.pallas_call(slab_kernel, out_shape=jax.ShapeDtypeStruct(queue.shape, B...  2.29 us
    pallas_call x1, Pallas kernels, local(): pl.pallas_call(lambda *refs: message_kernel(srcs, *refs), out_shape=jax.S...  1.49 us
  transfers between devices with their start and end apart: 4, of which 1 were waited for; matrix products, arithmetic and copies ran while one was open for 0% of the time, Pallas kernels for 13%

profile of v9, /device:TPU:1, one launch (start us, length us, event | category | flops | bytes accessed | tf_op | source)
XLA Modules:
  0.0 63.5 jit_solution(1978098090503831302)
XLA Ops:
  0.6 1.5 %shard_map.76.after_ref = bf16[16,40,256]{2,1,0:T(8,128)(2,1)} custom-call(bf16[32,256]{1,0:T(8,128)(2,1)} %refs_1_.1, s32[1,32]{1,0:T(1,128)} %bitcast.11, bf16[4,256]{1,0:T(4,128)(2,1)} %refs_2_.2), custom_call_target="tpu_custom_call" | custom-call | tf_op jit(solution)/shard_map/pallas_call | solution.py:227
  2.1 7.6 %all-to-all-start = ((bf16[16,40,256]{2,1,0:T(8,128)(2,1)}), bf16[16,40,256]{2,1,0:T(8,128)(2,1)S(1)}, u32[]{:S(2)}, u32[]{:S(2)}) async-start(bf16[16,40,256]{2,1,0:T(8,128)(2,1)} %shard_map.76.after_ref), calls=%async_computation | async-start | bytes 655360 | tf_op jit(solution)/shard_map/all_to_all | solution.py:235
  9.7 0.0 copy-start.1
  9.7 2.3 %shard_map.78.refs_3_ = bf16[2048,256]{1,0:T(8,128)(2,1)} custom-call(bf16[16,40,256]{2,1,0:T(8,128)(2,1)} %shard_map.76.after_ref, bf16[2048,256]{1,0:T(8,128)(2,1)} %refs_2_.3), custom_call_target="tpu_custom_call" | custom-call | flops 6000000000 | tf_op jit(solution)/shard_map/pallas_call | solution.py:236
  12.0 0.0 copy-done.1
  12.0 4.7 %collective-permute-start.1 = (bf16[2048,256]{1,0:T(8,128)(2,1)S(1)}, bf16[2048,256]{1,0:T(8,128)(2,1)S(1)}, u32[]{:S(2)}, u32[]{:S(2)}) collective-permute-start(bf16[2048,256]{1,0:T(8,128)(2,1)S(1)} %copy-done.1), channel_id=1, source_target_pairs={{0,16},{16,0},{1,17},{17,1},{2,18},{18,2},{3,19},{19,3},{4,20},{20... | collective-permute-start | bytes 3145736 | tf_op jit(solution)/shard_map/ppermute | solution.py:246
  17.5 0.1 stack.27.refs_0_
  17.5 0.0 all-to-all-done.refs_0_.refs_1_
  17.6 15.4 %collective-permute-start = (bf16[64,256]{1,0:T(8,128)(2,1)S(1)}, bf16[64,256]{1,0:T(8,128)(2,1)S(1)}, u32[]{:S(2)}, u32[]{:S(2)}) collective-permute-start(bf16[64,256]{1,0:T(8,128)(2,1)S(1)} %shard_map.77.refs_4_), channel_id=1, source_target_pairs={{0,0},{1,1},{2,2},{3,3},{4,4},{5,5},{6,6},{7,7},{8,8},{9,9},{10,10... | collective-permute-start | bytes 98312 | tf_op jit(solution)/shard_map/ppermute | solution.py:262
  33.0 0.0 collective-permute-done.1.refs_3_
  33.0 5.0 %shard_map.79.refs_1_ = bf16[16,136,256]{2,1,0:T(8,128)(2,1)S(1)} custom-call(s32[5]{0:T(128)S(1)} %stack.27.refs_0_, bf16[16,40,256]{2,1,0:T(8,128)(2,1)S(1)} %all-to-all-done.refs_0_.refs_1_, bf16[2048,256]{1,0:T(8,128)(2,1)S(1)} %copy-done.1, bf16[2048,256]{1,0:T(8,128)(2,1)S(1)} %collective-permute-done.1.refs_3_, bf16[64,256]{1,0:T(8,128)(2,1)S(1)} %shard_map.77.refs_4_), custom_call_target="tpu_custom_call" | custom-call | flops 3221225472 | bytes 2097152 | tf_op jit(solution)/shard_map/pallas_call | solution.py:270
  38.1 0.0 collective-permute-done.refs_0_
  38.1 0.0 copy-start
  38.1 17.7 %all_to_all.10.refs_0_.refs_1_ = bf16[16,136,256]{2,1,0:T(8,128)(2,1)S(1)} all-to-all(bf16[16,136,256]{2,1,0:T(8,128)(2,1)S(1)} %shard_map.80), channel_id=1, replica_groups=mesh['x'=4,'y'=4,'c'=2,'z'=16] {'x','y'}, dimensions={0} | all-to-all | bytes 2228224 | tf_op jit(solution)/shard_map/all_to_all | solution.py:287
  55.8 5.6 %collective-permute-start.2 = (bf16[16,64,256]{2,1,0:T(8,128)(2,1)S(1)}, bf16[16,64,256]{2,1,0:T(8,128)(2,1)S(1)}, u32[]{:S(2)}, u32[]{:S(2)}) collective-permute-start(bf16[16,64,256]{2,1,0:T(8,128)(2,1)S(1)} %slice.4), channel_id=1, source_target_pairs={{0,16},{16,0},{1,17},{17,1},{2,18},{18,2},{3,19},{19,3},{4,20},{20... | collective-permute-start | bytes 1572872 | tf_op jit(solution)/shard_map/ppermute | solution.py:288
  61.5 0.0 copy-done
  61.5 1.0 %shard_map.81 = (f32[1,32]{1,0:T(1,128)}, bf16[32,256]{1,0:T(8,128)(2,1)}) custom-call(bf16[16,136,256]{2,1,0:T(8,128)(2,1)S(1)} %all_to_all.10.refs_0_.refs_1_, bf16[32,256]{1,0:T(8,128)(2,1)S(1)} %copy-done), custom_call_target="tpu_custom_call" | custom-call | tf_op jit(solution)/shard_map/pallas_call | solution.py:290
  62.4 0.5 collective-permute-done.2.refs_2_
  63.0 0.6 shard_map.82
  (3 shorter events, 0.1 us)
Async XLA Ops:
  2.1 15.4 %all-to-all-start = ((bf16[16,40,256]{2,1,0:T(8,128)(2,1)}), bf16[16,40,256]{2,1,0:T(8,128)(2,1)S(1)}, u32[]{:S(2)}, u32[]{:S(2)}) async-start(bf16[16,40,256]{2,1,0:T(8,128)(2,1)} %shard_map.76.after_ref), calls=%async_computation | async-start | bytes 655360 | tf_op jit(solution)/shard_map/all_to_all | solution.py:235
  9.7 2.3 %copy-start.1 = (bf16[2048,256]{1,0:T(8,128)(2,1)S(1)}, bf16[2048,256]{1,0:T(8,128)(2,1)}, u32[]{:S(2)}) copy-start(bf16[2048,256]{1,0:T(8,128)(2,1)} %refs_2_.3) | copy-start | bytes 3145732
  12.0 21.0 %collective-permute-start.1 = (bf16[2048,256]{1,0:T(8,128)(2,1)S(1)}, bf16[2048,256]{1,0:T(8,128)(2,1)S(1)}, u32[]{:S(2)}, u32[]{:S(2)}) collective-permute-start(bf16[2048,256]{1,0:T(8,128)(2,1)S(1)} %copy-done.1), channel_id=1, source_target_pairs={{0,16},{16,0},{1,17},{17,1},{2,18},{18,2},{3,19},{19,3},{4,20},{20... | collective-permute-start | bytes 3145736 | tf_op jit(solution)/shard_map/ppermute | solution.py:246
  17.6 20.5 %collective-permute-start = (bf16[64,256]{1,0:T(8,128)(2,1)S(1)}, bf16[64,256]{1,0:T(8,128)(2,1)S(1)}, u32[]{:S(2)}, u32[]{:S(2)}) collective-permute-start(bf16[64,256]{1,0:T(8,128)(2,1)S(1)} %shard_map.77.refs_4_), channel_id=1, source_target_pairs={{0,0},{1,1},{2,2},{3,3},{4,4},{5,5},{6,6},{7,7},{8,8},{9,9},{10,10... | collective-permute-start | bytes 98312 | tf_op jit(solution)/shard_map/ppermute | solution.py:262
  38.1 23.3 %copy-start = (bf16[32,256]{1,0:T(8,128)(2,1)S(1)}, bf16[32,256]{1,0:T(8,128)(2,1)}, u32[]{:S(2)}) copy-start(bf16[32,256]{1,0:T(8,128)(2,1)} %refs_1_.1) | copy-start | bytes 49156
  55.8 7.1 %collective-permute-start.2 = (bf16[16,64,256]{2,1,0:T(8,128)(2,1)S(1)}, bf16[16,64,256]{2,1,0:T(8,128)(2,1)S(1)}, u32[]{:S(2)}, u32[]{:S(2)}) collective-permute-start(bf16[16,64,256]{2,1,0:T(8,128)(2,1)S(1)} %slice.4), channel_id=1, source_target_pairs={{0,16},{16,0},{1,17},{17,1},{2,18},{18,2},{3,19},{19,3},{4,20},{20... | collective-permute-start | bytes 1572872 | tf_op jit(solution)/shard_map/ppermute | solution.py:288

commit v10 on v9

--- a/solution.py
+++ b/solution.py
@@ -25,7 +25,7 @@
 
 
 def partial_kernel(scale, srcs, nq, info_ref, msg_ref, own_ref, *refs):
-    other_ref, _, out_ref, q_ref, s_ref = refs
+    other_ref, _, _, out_ref, q_ref, s_ref = refs
     width = own_ref.shape[1]
     slab = own_ref.shape[0]
     n = srcs * nq
@@ -153,6 +153,11 @@
         out_ref[j, at:at + keys.shape[0], :] = keys
 
 
+def gate_kernel(after_ref, out_ref):
+    del after_ref
+    out_ref[...] = jnp.zeros_like(out_ref)
+
+
 def slab_kernel(after_ref, queue_ref, out_ref, sem):
     del after_ref
     copy = pltpu.make_async_copy(queue_ref, out_ref, sem)
@@ -233,6 +238,16 @@
         compiler_params=pltpu.CompilerParams(vmem_limit_bytes=56 * MIB),
     )(queries, positions[None], new_keys)
     got = lax.all_to_all(message, ("x", "y"), 0, 0)
+    gate = pl.pallas_call(
+        gate_kernel,
+        out_shape=jax.ShapeDtypeStruct((8, 128), F32),
+        in_specs=[ANY],
+        out_specs=VMEM,
+        compiler_params=pltpu.CompilerParams(vmem_limit_bytes=56 * MIB),
+        cost_estimate=LATE,
+    )(message)
+    slab_keys, gate = lax.optimization_barrier((queue, gate))
+    other = lax.ppermute(slab_keys, "c", swap)
     kept = pl.pallas_call(
         slab_kernel,
         out_shape=jax.ShapeDtypeStruct(queue.shape, BF),
@@ -241,9 +256,7 @@
         scratch_shapes=[pltpu.SemaphoreType.DMA],
         compiler_params=pltpu.CompilerParams(vmem_limit_bytes=56 * MIB),
         cost_estimate=LATE,
-    )(message, queue)
-    slab_keys, kept = lax.optimization_barrier((queue, kept))
-    other = lax.ppermute(slab_keys, "c", swap)
+    )(gate, queue)
 
     plane_keys = pl.pallas_call(
         lambda *refs: plane_keys_kernel(nq, *refs),
@@ -270,12 +283,12 @@
     out = pl.pallas_call(
         lambda *refs: partial_kernel(scale, srcs, nq, *refs),
         out_shape=out_shape,
-        in_specs=[SMEM, VMEM, VMEM, VMEM, ANY],
+        in_specs=[SMEM, VMEM, VMEM, VMEM, ANY, ANY],
         out_specs=VMEM,
         scratch_shapes=[pltpu.VMEM((n, width), BF), pltpu.VMEM((n, 2 * slab), F32)],
         compiler_params=pltpu.CompilerParams(vmem_limit_bytes=24 * MIB),
         cost_estimate=pl.CostEstimate(flops=3 * flops, bytes_accessed=4 * slab * width, transcendentals=2 * n * slab),
-    )(info, got, queue, other, plane_keys)
+    )(info, got, queue, other, plane_keys, kept)
     out = pl.pallas_call(
         lambda *refs: fill_kernel(srcs, at, *refs),
         out_shape=out_shape,

time: 64 us -> 65.1 us (1.017)
  Pallas kernels: 10.4 us -> 11.6 us
    pallas_call x1, Pallas kernels: 5.04 us -> 5.74 us  [local(): pl.pallas_call(lambda *refs: partial_kernel(scale, srcs, nq, *refs), out_...]
  transfers between devices with their start and end apart: 4 -> 4, of which waited for: 1 -> 1; matrix products, arithmetic and copies ran while one was open for 0% -> 0% of each run, Pallas kernels for 13% -> 15%
where the time goes in v10:
time: 65.1 us; the launch traced here: 64.2 us
  starting transfers between devices  33 us (51%)
  blocking collectives  17.5 us (27%)
  Pallas kernels  11.6 us (18%)
  between operations  1.41 us (2%)
    all_to_all x1, blocking collectives, local(): back = lax.all_to_all(out, ('x', 'y'), 0, 0)  17.5 us
    ppermute x1, starting transfers between devices, local(): moved = lax.ppermute(plane_keys, ('x', 'y', 'c', 'z'), pairs)  15 us
    all_to_all x1, starting transfers between devices, local(): got = lax.all_to_all(message, ('x', 'y'), 0, 0)  7.58 us
    ppermute x1, starting transfers between devices, local(): twin = lax.ppermute(back[:, at:at + srcs * nk, :], 'c', swap)  5.74 us
    pallas_call x1, Pallas kernels, local(): pl.pallas_call(lambda *refs: partial_kernel(scale, srcs, nq, *refs), out_...  5.74 us
    ppermute x1, starting transfers between devices, local(): other = lax.ppermute(slab_keys, 'c', swap)  4.73 us
    pallas_call x1, Pallas kernels, local(): pl.pallas_call(slab_kernel, out_shape=jax.ShapeDtypeStruct(queue.shape, B...  2.2 us
    pallas_call x1, Pallas kernels, local(): pl.pallas_call(lambda *refs: message_kernel(srcs, *refs), out_shape=jax.S...  1.49 us
  transfers between devices with their start and end apart: 4, of which 1 were waited for; matrix products, arithmetic and copies ran while one was open for 0% of the time, Pallas kernels for 15%

profile of v10, /device:TPU:1, one launch (start us, length us, event | category | flops | bytes accessed | tf_op | source)
XLA Modules:
  0.0 64.2 jit_solution(2383060603729050640)
XLA Ops:
  0.6 1.5 %shard_map.76.after_ref = bf16[16,40,256]{2,1,0:T(8,128)(2,1)} custom-call(bf16[32,256]{1,0:T(8,128)(2,1)} %refs_1_.1, s32[1,32]{1,0:T(1,128)} %bitcast.11, bf16[4,256]{1,0:T(4,128)(2,1)} %refs_2_.2), custom_call_target="tpu_custom_call" | custom-call | tf_op jit(solution)/shard_map/pallas_call | solution.py:232
  2.1 7.6 %all-to-all-start = ((bf16[16,40,256]{2,1,0:T(8,128)(2,1)}), bf16[16,40,256]{2,1,0:T(8,128)(2,1)S(1)}, u32[]{:S(2)}, u32[]{:S(2)}) async-start(bf16[16,40,256]{2,1,0:T(8,128)(2,1)} %shard_map.76.after_ref), calls=%async_computation | async-start | bytes 655360 | tf_op jit(solution)/shard_map/all_to_all | solution.py:240
  9.7 0.6 shard_map.78.after_ref
  10.3 4.7 %collective-permute-start.1 = (bf16[2048,256]{1,0:T(8,128)(2,1)}, bf16[2048,256]{1,0:T(8,128)(2,1)S(1)}, u32[]{:S(2)}, u32[]{:S(2)}) collective-permute-start(bf16[2048,256]{1,0:T(8,128)(2,1)} %refs_2_.3), channel_id=1, source_target_pairs={{0,16},{16,0},{1,17},{17,1},{2,18},{18,2},{3,19},{19,3},{4,20},{20... | collective-permute-start | bytes 3145736 | tf_op jit(solution)/shard_map/ppermute | solution.py:250
  15.1 2.2 %shard_map.79.refs_5_.refs_3_ = bf16[2048,256]{1,0:T(8,128)(2,1)} custom-call(f32[8,128]{1,0:T(8,128)} %shard_map.78.after_ref, bf16[2048,256]{1,0:T(8,128)(2,1)} %refs_2_.3), custom_call_target="tpu_custom_call" | custom-call | flops 6000000000 | tf_op jit(solution)/shard_map/pallas_call | solution.py:251
  17.9 0.1 stack.27.refs_0_
  18.0 0.0 copy-start
  18.0 0.0 all-to-all-done.refs_0_.refs_1_
  18.0 15.0 %collective-permute-start = (bf16[64,256]{1,0:T(8,128)(2,1)S(1)}, bf16[64,256]{1,0:T(8,128)(2,1)S(1)}, u32[]{:S(2)}, u32[]{:S(2)}) collective-permute-start(bf16[64,256]{1,0:T(8,128)(2,1)S(1)} %shard_map.77.refs_4_), channel_id=1, source_target_pairs={{0,0},{1,1},{2,2},{3,3},{4,4},{5,5},{6,6},{7,7},{8,8},{9,9},{10,10... | collective-permute-start | bytes 98312 | tf_op jit(solution)/shard_map/ppermute | solution.py:275
  33.0 0.0 collective-permute-done.1.refs_3_
  33.0 0.0 copy-done
  33.0 5.7 %shard_map.80.refs_1_ = bf16[16,136,256]{2,1,0:T(8,128)(2,1)S(1)} custom-call(s32[5]{0:T(128)S(1)} %stack.27.refs_0_, bf16[16,40,256]{2,1,0:T(8,128)(2,1)S(1)} %all-to-all-done.refs_0_.refs_1_, bf16[2048,256]{1,0:T(8,128)(2,1)} %refs_2_.3, bf16[2048,256]{1,0:T(8,128)(2,1)S(1)} %collective-permute-done.1.refs_3_, bf16[64,256]{1,0:T(8,128)(2,1)S(1)} %shard_map.77.refs_4_, ...), custom_call_target="tpu_custom_call" | custom-call | flops 3221225472 | bytes 2097152 | tf_op jit(solution)/shard_map/pallas_call | solution.py:283
  38.8 0.0 collective-permute-done.refs_0_
  38.8 0.0 copy-start.1
  38.8 17.5 %all_to_all.10.refs_0_.refs_1_ = bf16[16,136,256]{2,1,0:T(8,128)(2,1)S(1)} all-to-all(bf16[16,136,256]{2,1,0:T(8,128)(2,1)S(1)} %shard_map.81), channel_id=1, replica_groups=mesh['x'=4,'y'=4,'c'=2,'z'=16] {'x','y'}, dimensions={0} | all-to-all | bytes 2228224 | tf_op jit(solution)/shard_map/all_to_all | solution.py:300
  56.4 5.7 %collective-permute-start.2 = (bf16[16,64,256]{2,1,0:T(8,128)(2,1)S(1)}, bf16[16,64,256]{2,1,0:T(8,128)(2,1)S(1)}, u32[]{:S(2)}, u32[]{:S(2)}) collective-permute-start(bf16[16,64,256]{2,1,0:T(8,128)(2,1)S(1)} %slice.4), channel_id=1, source_target_pairs={{0,16},{16,0},{1,17},{17,1},{2,18},{18,2},{3,19},{19,3},{4,20},{20... | collective-permute-start | bytes 1572872 | tf_op jit(solution)/shard_map/ppermute | solution.py:301
  62.2 0.0 copy-done.1
  62.2 1.0 %shard_map.82 = (f32[1,32]{1,0:T(1,128)}, bf16[32,256]{1,0:T(8,128)(2,1)}) custom-call(bf16[16,136,256]{2,1,0:T(8,128)(2,1)S(1)} %all_to_all.10.refs_0_.refs_1_, bf16[32,256]{1,0:T(8,128)(2,1)S(1)} %copy-done.1), custom_call_target="tpu_custom_call" | custom-call | tf_op jit(solution)/shard_map/pallas_call | solution.py:303
  63.1 0.5 collective-permute-done.2.refs_2_
  63.7 0.6 shard_map.83
  (3 shorter events, 0.1 us)
Async XLA Ops:
  2.1 15.9 %all-to-all-start = ((bf16[16,40,256]{2,1,0:T(8,128)(2,1)}), bf16[16,40,256]{2,1,0:T(8,128)(2,1)S(1)}, u32[]{:S(2)}, u32[]{:S(2)}) async-start(bf16[16,40,256]{2,1,0:T(8,128)(2,1)} %shard_map.76.after_ref), calls=%async_computation | async-start | bytes 655360 | tf_op jit(solution)/shard_map/all_to_all | solution.py:240
  10.3 22.7 %collective-permute-start.1 = (bf16[2048,256]{1,0:T(8,128)(2,1)}, bf16[2048,256]{1,0:T(8,128)(2,1)S(1)}, u32[]{:S(2)}, u32[]{:S(2)}) collective-permute-start(bf16[2048,256]{1,0:T(8,128)(2,1)} %refs_2_.3), channel_id=1, source_target_pairs={{0,16},{16,0},{1,17},{17,1},{2,18},{18,2},{3,19},{19,3},{4,20},{20... | collective-permute-start | bytes 3145736 | tf_op jit(solution)/shard_map/ppermute | solution.py:250
  18.0 15.0 %copy-start = (bf16[2048,256]{1,0:T(8,128)(2,1)S(1)}, bf16[2048,256]{1,0:T(8,128)(2,1)}, u32[]{:S(2)}) copy-start(bf16[2048,256]{1,0:T(8,128)(2,1)} %shard_map.79.refs_5_.refs_3_) | copy-start | bytes 3145732
  18.0 20.7 %collective-permute-start = (bf16[64,256]{1,0:T(8,128)(2,1)S(1)}, bf16[64,256]{1,0:T(8,128)(2,1)S(1)}, u32[]{:S(2)}, u32[]{:S(2)}) collective-permute-start(bf16[64,256]{1,0:T(8,128)(2,1)S(1)} %shard_map.77.refs_4_), channel_id=1, source_target_pairs={{0,0},{1,1},{2,2},{3,3},{4,4},{5,5},{6,6},{7,7},{8,8},{9,9},{10,10... | collective-permute-start | bytes 98312 | tf_op jit(solution)/shard_map/ppermute | solution.py:275
  38.8 23.3 %copy-start.1 = (bf16[32,256]{1,0:T(8,128)(2,1)S(1)}, bf16[32,256]{1,0:T(8,128)(2,1)}, u32[]{:S(2)}) copy-start(bf16[32,256]{1,0:T(8,128)(2,1)} %refs_1_.1) | copy-start | bytes 49156
  56.4 7.3 %collective-permute-start.2 = (bf16[16,64,256]{2,1,0:T(8,128)(2,1)S(1)}, bf16[16,64,256]{2,1,0:T(8,128)(2,1)S(1)}, u32[]{:S(2)}, u32[]{:S(2)}) collective-permute-start(bf16[16,64,256]{2,1,0:T(8,128)(2,1)S(1)} %slice.4), channel_id=1, source_target_pairs={{0,16},{16,0},{1,17},{17,1},{2,18},{18,2},{3,19},{19,3},{4,20},{20... | collective-permute-start | bytes 1572872 | tf_op jit(solution)/shard_map/ppermute | solution.py:301
